TPU v7x, 512 devices: a whole 4x8x8 slice. The times are simulated.
512 devices in a mesh: freq: 64 (over x, y, core), rcv: 8 (over z).
Axes of the slice: x: 4, y: 8, z: 8, core: 2. Of those that a mesh axis runs over, the one named last changes fastest.
Arguments:
- focus_start: bfloat16 [16, 2048, 1024], P(None, ('rcv', 'freq')), may hold values from -6 to 6
- onset: int32 [16, 2048], P(None, ('rcv', 'freq')), may hold values from 128 to 383
- bins: int32 [64], replicated, may hold values from 0 to 63, each once
- refl_real: bfloat16 [64, 2048, 2048], P('freq', 'rcv'), may hold values from -0.09375 to 0.09375
- refl_imag: bfloat16 [64, 2048, 2048], P('freq', 'rcv'), may hold values from -0.09375 to 0.09375
Outputs:
- focus_plus: bfloat16 [16, 2048, 1024], P(None, ('rcv', 'freq'))
- focus_minus: bfloat16 [16, 2048, 1024], P(None, ('rcv', 'freq'))
Inputs may be any that keep to these rules, and one draw needn't show every extreme that they name: `bins`: each value 0 to 63 appears once.
All inputs are finite; a program needn't handle non-finite values.
Results may differ from a plain program's by a relative error of at most 0.022.
Values may be sent and summed in bfloat16 or wider, within the bound.
No kernel may reach another device: no remote copies, remote signals or barrier semaphores. Data moves between devices by JAX's collectives and lax.ppermute only.
A program may use at most 64 MiB of HBM per device.

v0:
```python
import math

import jax
import jax.numpy as jnp
from jax import lax
from jax.sharding import PartitionSpec as P

FLO = 8
ITERS = 2


def make_tables(bins, nsamp, nfreq):
    times = jnp.arange(nsamp, dtype=jnp.int32)
    waves = FLO + bins
    phase = times[:, None] * waves[None, :] % nsamp
    angle = phase.astype(jnp.float32) * jnp.float32(2.0 * math.pi / nsamp)
    forward = jnp.concatenate([jnp.cos(angle), -jnp.sin(angle)], axis=1) * jnp.float32(
        1.0 / math.sqrt(nsamp)
    )
    inverse = jnp.concatenate([jnp.cos(angle).T, -jnp.sin(angle).T], axis=0) * jnp.float32(
        math.sqrt(2.0 / nfreq)
    )
    return (forward.astype(jnp.bfloat16), inverse.astype(jnp.bfloat16))


def window_apply(values, onset):
    nsamp = values.shape[2]
    times = lax.broadcasted_iota(jnp.int32, (1, 1, nsamp), 2)
    keep = (times < onset[:, :, None]) | (times >= nsamp - onset[:, :, None])
    return jnp.where(keep, values, jnp.zeros_like(values))


def shards(focus_start, onset, bins, refl_real, refl_imag):
    points, local_rcv, nsamp = focus_start.shape
    nfreq = bins.shape[0]
    forward, inverse = make_tables(bins, nsamp, nfreq)
    block_rows = refl_real.shape[1]

    def spectrum(traces):
        flat = jnp.einsum("prt,tk->kpr", traces, forward, preferred_element_type=jnp.float32)
        return flat.astype(jnp.bfloat16).reshape(2, nfreq, points, local_rcv)

    def to_owners(spec):
        return lax.all_to_all(spec, "freq", split_axis=1, concat_axis=3, tiled=True)

    def to_trace(owned):
        spec = lax.all_to_all(owned, "freq", split_axis=3, concat_axis=1, tiled=True)
        spec = spec.reshape(2 * nfreq, points, local_rcv)
        return jnp.einsum("kpr,kt->prt", spec, inverse, preferred_element_type=jnp.float32)

    focus_plus = focus_start
    focus_minus = focus_start
    for step in range(ITERS):
        convolve_spec = spectrum(focus_plus)
        convolve_owned = to_owners(convolve_spec)
        full = lax.all_gather(convolve_owned, "rcv", axis=3, tiled=True)
        src_re = full[0, 0]
        src_im = full[1, 0]
        mat_re = refl_real[0]
        mat_im = refl_imag[0]
        convolve_out_re = jnp.einsum(
            "rs,ps->pr", mat_re, src_re, preferred_element_type=jnp.float32
        ) - jnp.einsum("rs,ps->pr", mat_im, src_im, preferred_element_type=jnp.float32)
        convolve_out_im = jnp.einsum(
            "rs,ps->pr", mat_re, src_im, preferred_element_type=jnp.float32
        ) + jnp.einsum("rs,ps->pr", mat_im, src_re, preferred_element_type=jnp.float32)
        convolve_owned_out = jnp.stack([convolve_out_re, convolve_out_im], axis=0).astype(
            jnp.bfloat16
        )[:, None]
        focus_minus = window_apply(to_trace(convolve_owned_out), onset).astype(jnp.bfloat16)
        correlate_owned = to_owners(spectrum(focus_minus))
        rows_re = correlate_owned[0, 0]
        rows_im = correlate_owned[1, 0]
        cols_re = refl_real[0]
        cols_im = refl_imag[0]
        out_re = jnp.einsum(
            "rs,pr->sp", cols_re, rows_re, preferred_element_type=jnp.float32
        ) + jnp.einsum("rs,pr->sp", cols_im, rows_im, preferred_element_type=jnp.float32)
        out_im = jnp.einsum(
            "rs,pr->sp", cols_re, rows_im, preferred_element_type=jnp.float32
        ) - jnp.einsum("rs,pr->sp", cols_im, rows_re, preferred_element_type=jnp.float32)
        summed = lax.psum_scatter(
            jnp.concatenate([out_re, out_im], axis=1).astype(jnp.bfloat16),
            "rcv",
            scatter_dimension=0,
            tiled=True,
        ).astype(jnp.float32)
        summed = summed.reshape(block_rows, 2, points)
        owned_out = jnp.transpose(summed, (1, 2, 0)).astype(jnp.bfloat16)[:, None]
        update = window_apply(to_trace(owned_out), onset)
        focus_plus = (focus_start.astype(jnp.float32) + update).astype(jnp.bfloat16)
    return (focus_plus, focus_minus)


def solution(mesh):
    return jax.shard_map(
        shards,
        mesh=mesh,
        in_specs=(
            P(None, ("rcv", "freq"), None),
            P(None, ("rcv", "freq")),
            P(),
            P("freq", "rcv", None),
            P("freq", "rcv", None),
        ),
        out_specs=(P(None, ("rcv", "freq"), None), P(None, ("rcv", "freq"), None)),
        check_vma=False,
    )
```

profile of v0, /device:TPU:1, one launch (start us, length us, event | category | flops | bytes accessed | tf_op | source)
XLA Modules:
  0.0 296.9 jit_solution(15804786274058866203)
XLA Ops:
  7.2 0.0 copy-start
  7.2 0.7 broadcast_add_fusion
  7.9 2.1 fusion.66
  10.0 0.2 fusion.63
  10.2 0.7 copy-done.3
  10.9 0.2 convolution_convert_fusion.1
  11.1 0.1 reshape.114
  11.2 0.8 copy.53
  12.0 11.6 %all-to-all-start = ((bf16[2,64,16,4]{2,3,0,1:T(4,128)(2,1)}), bf16[2,64,16,4]{2,3,0,1:T(4,128)(2,1)S(1)}, u32[]{:S(2)}, u32[]{:S(2)}) async-start(bf16[2,64,16,4]{2,3,0,1:T(4,128)(2,1)} %copy.53), calls=%async_computation | async-start | bytes 262144 | tf_op jit(solution)/shard_map/all_to_all | solution.py:44
  23.6 1.1 fusion.77
  24.7 9.2 %all-to-all-done = bf16[2,64,16,4]{2,3,0,1:T(4,128)(2,1)S(1)} async-done(((bf16[2,64,16,4]{2,3,0,1:T(4,128)(2,1)}), bf16[2,64,16,4]{2,3,0,1:T(4,128)(2,1)S(1)}, u32[]{:S(2)}, u32[]{:S(2)}) %all-to-all-start) | async-done | bytes 16416 | tf_op jit(solution)/shard_map/all_to_all | solution.py:44
  34.0 28.3 %all_gather.6 = bf16[2,1,16,2048]{2,3,0,1:T(8,128)(2,1)S(1)} all-gather(bf16[2,1,16,256]{2,3,0,1:T(8,128)(2,1)S(1)} %bitcast.149), channel_id=1, replica_groups=mesh['freq'=64,'rcv'=8] {'rcv'}, dimensions={3}, use_global_device_ids=true | all-gather | bytes 147456 | tf_op jit(solution)/shard_map/all_gather | solution.py:56
  62.3 0.4 fusion.46
  62.6 0.4 fusion.48
  63.0 0.9 copy-done.1
  63.9 0.4 fusion.24
  64.3 0.4 fusion.25
  64.7 0.8 copy.55
  65.5 9.9 %all-to-all-start.1 = ((bf16[2,1,16,256]{2,0,1,3:T(2,128)(2,1)}), bf16[2,1,16,256]{2,0,1,3:T(2,128)(2,1)S(1)}, u32[]{:S(2)}, u32[]{:S(2)}) async-start(bf16[2,1,16,256]{2,0,1,3:T(2,128)(2,1)} %copy.55), calls=%async_computation.1 | async-start | bytes 262144 | tf_op jit(solution)/shard_map/all_to_all | solution.py:47
  75.4 0.0 reduce-scatter.3.cloned.1.call-start
  75.5 10.3 %all-to-all-done.1 = bf16[2,1,16,256]{2,0,1,3:T(2,128)(2,1)S(1)} async-done(((bf16[2,1,16,256]{2,0,1,3:T(2,128)(2,1)}), bf16[2,1,16,256]{2,0,1,3:T(2,128)(2,1)S(1)}, u32[]{:S(2)}, u32[]{:S(2)}) %all-to-all-start.1) | async-done | bytes 16416 | tf_op jit(solution)/shard_map/all_to_all | solution.py:47
  85.7 0.3 fusion.16
  86.1 0.1 reshape.116
  86.2 0.1 copy.58
  86.3 15.0 %all_to_all.126 = bf16[2,64,16,4]{2,3,0,1:T(4,128)(2,1)S(1)} all-to-all(bf16[2,64,16,4]{2,3,0,1:T(4,128)(2,1)S(1)} %copy.58), channel_id=1, replica_groups=mesh['freq'=64,'rcv'=8] {'freq'}, dimensions={1} | all-to-all | bytes 32768 | tf_op jit(solution)/shard_map/all_to_all | solution.py:44
  101.4 0.3 fusion.42
  101.7 0.3 fusion.44
  102.0 0.3 fusion.6
  102.2 0.3 fusion.7
  102.5 0.7 pad_maximum_fusion
  103.2 0.0 reduce-scatter.3.cloned.1.call-update
  103.2 0.0 reduce-scatter.5.cloned.1.call-start
  103.3 27.1 %reduce-scatter.3.cloned.1.call-done = bf16[256,32]{0,1:T(8,128)(2,1)} async-done(((bf16[2048,32]{0,1:T(8,128)(2,1)}), bf16[256,32]{0,1:T(8,128)(2,1)}) %reduce-scatter.3.cloned.1.call-update) | async-done | bytes 16400 | tf_op jit(solution)/shard_map/reduce_scatter | solution.py:82
  130.4 0.8 copy.59
  131.2 25.9 %all_to_all.127 = bf16[2,1,16,256]{2,0,1,3:T(2,128)(2,1)S(1)} all-to-all(bf16[2,1,16,256]{2,0,1,3:T(2,128)(2,1)S(1)} %bitcast.154), channel_id=1, replica_groups=mesh['freq'=64,'rcv'=8] {'freq'}, dimensions={3} | all-to-all | bytes 32768 | tf_op jit(solution)/shard_map/all_to_all | solution.py:47
  157.1 0.4 fusion.17
  157.5 0.1 reshape.118
  157.6 0.1 copy.62
  157.7 15.0 %all_to_all.128 = bf16[2,64,16,4]{2,3,0,1:T(4,128)(2,1)S(1)} all-to-all(bf16[2,64,16,4]{2,3,0,1:T(4,128)(2,1)S(1)} %copy.62), channel_id=1, replica_groups=mesh['freq'=64,'rcv'=8] {'freq'}, dimensions={1} | all-to-all | bytes 32768 | tf_op jit(solution)/shard_map/all_to_all | solution.py:44
  172.8 21.6 %all_gather.7 = bf16[2,1,16,2048]{2,3,0,1:T(8,128)(2,1)S(1)} all-gather(bf16[2,1,16,256]{2,3,0,1:T(8,128)(2,1)S(1)} %bitcast.150), channel_id=1, replica_groups=mesh['freq'=64,'rcv'=8] {'rcv'}, dimensions={3}, use_global_device_ids=true | all-gather | bytes 147456 | tf_op jit(solution)/shard_map/all_gather | solution.py:56
  194.4 0.4 fusion.38
  194.8 0.4 fusion.40
  195.2 0.4 fusion.22
  195.6 0.4 fusion.23
  196.0 0.1 copy.64
  196.1 20.5 %all_to_all.129 = bf16[2,1,16,256]{2,0,1,3:T(2,128)(2,1)S(1)} all-to-all(bf16[2,1,16,256]{2,0,1,3:T(2,128)(2,1)S(1)} %copy.64), channel_id=1, replica_groups=mesh['freq'=64,'rcv'=8] {'freq'}, dimensions={3} | all-to-all | bytes 32768 | tf_op jit(solution)/shard_map/all_to_all | solution.py:47
  216.7 0.2 fusion.12
  216.9 0.2 convolution_convert_fusion
  217.1 0.1 reshape.120
  217.2 0.1 copy.67
  217.3 15.0 %all_to_all.130 = bf16[2,64,16,4]{2,3,0,1:T(4,128)(2,1)S(1)} all-to-all(bf16[2,64,16,4]{2,3,0,1:T(4,128)(2,1)S(1)} %copy.67), channel_id=1, replica_groups=mesh['freq'=64,'rcv'=8] {'freq'}, dimensions={1} | all-to-all | bytes 32768 | tf_op jit(solution)/shard_map/all_to_all | solution.py:44
  232.4 0.3 fusion.34
  232.7 0.3 fusion.36
  233.0 0.3 fusion.4
  233.2 0.3 fusion.5
  233.5 0.7 pad_maximum_fusion.1
  234.2 0.0 reduce-scatter.5.cloned.1.call-update
  234.2 27.2 %reduce-scatter.5.cloned.1.call-done = bf16[256,32]{0,1:T(8,128)(2,1)} async-done(((bf16[2048,32]{0,1:T(8,128)(2,1)}), bf16[256,32]{0,1:T(8,128)(2,1)}) %reduce-scatter.5.cloned.1.call-update) | async-done | bytes 16400 | tf_op jit(solution)/shard_map/reduce_scatter | solution.py:82
  261.4 1.5 copy.68
  262.9 15.7 %all-to-all-start.7 = ((bf16[2,1,16,256]{2,0,1,3:T(2,128)(2,1)}), bf16[2,1,16,256]{2,0,1,3:T(2,128)(2,1)S(1)}, u32[]{:S(2)}, u32[]{:S(2)}) async-start(bf16[2,1,16,256]{2,0,1,3:T(2,128)(2,1)} %bitcast.46), calls=%async_computation.9 | async-start | bytes 262144 | tf_op jit(solution)/shard_map/all_to_all | solution.py:47
  278.6 0.8 copy.72
  279.4 9.6 %all-to-all-done.7 = bf16[2,1,16,256]{2,0,1,3:T(2,128)(2,1)S(1)} async-done(((bf16[2,1,16,256]{2,0,1,3:T(2,128)(2,1)}), bf16[2,1,16,256]{2,0,1,3:T(2,128)(2,1)S(1)}, u32[]{:S(2)}, u32[]{:S(2)}) %all-to-all-start.7) | async-done | bytes 16416 | tf_op jit(solution)/shard_map/all_to_all | solution.py:47
  289.0 0.3 fusion.13
  289.3 0.8 copy.71
  (17 shorter events, 0.3 us)
Async XLA Ops:
  7.2 55.1 %copy-start = (bf16[1,256,2048]{2,1,0:T(8,128)(2,1)S(1)}, bf16[1,256,2048]{2,1,0:T(8,128)(2,1)}, u32[]{:S(2)}) copy-start(bf16[1,256,2048]{2,1,0:T(8,128)(2,1)} %param.8) | copy-start | bytes 3145732
  10.0 0.9 copy-start.3
  12.0 22.0 %all-to-all-start = ((bf16[2,64,16,4]{2,3,0,1:T(4,128)(2,1)}), bf16[2,64,16,4]{2,3,0,1:T(4,128)(2,1)S(1)}, u32[]{:S(2)}, u32[]{:S(2)}) async-start(bf16[2,64,16,4]{2,3,0,1:T(4,128)(2,1)} %copy.53), calls=%async_computation | async-start | bytes 262144 | tf_op jit(solution)/shard_map/all_to_all | solution.py:44
  23.6 1.1 copy-start.2
  62.6 1.2 copy-start.1
  65.5 20.3 %all-to-all-start.1 = ((bf16[2,1,16,256]{2,0,1,3:T(2,128)(2,1)}), bf16[2,1,16,256]{2,0,1,3:T(2,128)(2,1)S(1)}, u32[]{:S(2)}, u32[]{:S(2)}) async-start(bf16[2,1,16,256]{2,0,1,3:T(2,128)(2,1)} %copy.55), calls=%async_computation.1 | async-start | bytes 262144 | tf_op jit(solution)/shard_map/all_to_all | solution.py:47
  75.4 55.0 %reduce-scatter.3.cloned.1.call-start = ((), (), s32[]{:S(2)}) async-start(), calls=%async_computation.10 | async-start | bytes 147456 | tf_op jit(solution)/shard_map/reduce_scatter | solution.py:82
  103.2 158.2 %reduce-scatter.5.cloned.1.call-start = ((), (), s32[]{:S(2)}) async-start(), calls=%async_computation.11 | async-start | bytes 147456 | tf_op jit(solution)/shard_map/reduce_scatter | solution.py:82
  262.9 26.1 %all-to-all-start.7 = ((bf16[2,1,16,256]{2,0,1,3:T(2,128)(2,1)}), bf16[2,1,16,256]{2,0,1,3:T(2,128)(2,1)S(1)}, u32[]{:S(2)}, u32[]{:S(2)}) async-start(bf16[2,1,16,256]{2,0,1,3:T(2,128)(2,1)} %bitcast.46), calls=%async_computation.9 | async-start | bytes 262144 | tf_op jit(solution)/shard_map/all_to_all | solution.py:47
Sparse Core Ops, SparseCore 0:
  103.3 26.9 reduce-scatter.2
  234.3 26.9 reduce-scatter.4
where the time goes:
time: 298 us; the launch traced here: 297 us
  blocking collectives  141 us (47%)
  waiting for transfers between devices  83.4 us (28%)
  starting transfers between devices  37.3 us (13%)
  between operations  14.2 us (5%)
  local copies, waits for them, and re-layouts  8.18 us (3%)
  matrix products  6.84 us (2%)
  other arithmetic  5.54 us (2%)
    reduce_scatter x2, waiting for transfers between devices, shards(): lax.psum_scatter(jnp.concatenate([out_re, out_im], axis=1).astype(jnp.bfl...  54.3 us
    all_gather x2, blocking collectives, shards(): full = lax.all_gather(convolve_owned, 'rcv', axis=3, tiled=True)  49.9 us
    all_to_all x2, blocking collectives, to_trace(): lax.all_to_all(owned, 'freq', split_axis=3, concat_axis=1, tiled=True)  46.4 us
    all_to_all x3, blocking collectives, to_owners(): return lax.all_to_all(spec, 'freq', split_axis=1, concat_axis=3, tiled=True)  45.1 us
    all_to_all x2, starting transfers between devices, to_trace(): lax.all_to_all(owned, 'freq', split_axis=3, concat_axis=1, tiled=True)  25.6 us
    all_to_all x2, waiting for transfers between devices, to_trace(): lax.all_to_all(owned, 'freq', split_axis=3, concat_axis=1, tiled=True)  19.9 us
    all_to_all x1, starting transfers between devices, to_owners(): return lax.all_to_all(spec, 'freq', split_axis=1, concat_axis=3, tiled=True)  11.6 us
    all_to_all x1, waiting for transfers between devices, to_owners(): return lax.all_to_all(spec, 'freq', split_axis=1, concat_axis=3, tiled=True)  9.22 us
  transfers between devices with their start and end apart: 5, of which 5 were waited for; matrix products, arithmetic and copies ran while one was open for 1% of the time, Pallas kernels for 0%

commit v1 on v0

v1 whole, which is shorter than its diff:
```python
import math

import jax
import jax.numpy as jnp
import numpy as np
from jax import lax
from jax.sharding import Mesh
from jax.sharding import PartitionSpec as P

FLO = 8
ITERS = 2
NX, NY, NC, NZ = 4, 8, 2, 8
BF = jnp.bfloat16
F32 = jnp.float32
ONSET_MID = 256


def base_tables(nsamp, nfreq):
    waves = FLO + np.arange(nfreq)
    phase = (np.arange(nsamp)[None, :] * waves[:, None]) % nsamp
    angle = phase.astype(np.float32) * np.float32(2.0 * math.pi / nsamp)
    rows = np.concatenate([np.cos(angle), -np.sin(angle)], axis=0)
    return (
        (rows * np.float32(1.0 / math.sqrt(nsamp))).astype(BF),
        (rows * np.float32(math.sqrt(2.0 / nfreq))).astype(BF),
    )


def pick(slab_bins, nfreq):
    want = jnp.stack([slab_bins, slab_bins + nfreq], axis=1).reshape(1, -1)
    have = lax.broadcasted_iota(jnp.int32, (2 * nfreq, want.shape[1]), 0)
    return (have == want).astype(BF)


def dot(a, b, dims):
    return lax.dot_general(a, b, (dims, ((), ())), preferred_element_type=F32)


def exchange(values, axes):
    return lax.all_to_all(values, axes, 0, 0, tiled=True)


def shards(focus_start, onset, bins, refl_real, refl_imag):
    points, own, nsamp = focus_start.shape
    nfreq = bins.shape[0]
    rows, cols = refl_real.shape[1:]
    mat_re, mat_im = refl_real[0], refl_imag[0]
    ngrp = NX * NC
    sub = points // ngrp
    base_fwd, base_inv = base_tables(nsamp, nfreq)
    grid_bins = bins.reshape(NX, NY, NC)
    zi, yi = lax.axis_index("z"), lax.axis_index("y")

    fwd_start = dot(pick(grid_bins.transpose(1, 2, 0).reshape(-1), nfreq), base_fwd, ((0,), (0,))).astype(BF)
    order = pick(grid_bins.transpose(1, 0, 2).reshape(-1), nfreq)
    inv = dot(base_inv, order, ((0,), (0,))).astype(BF)
    mine = lax.dynamic_index_in_dim(grid_bins, yi, 1, keepdims=False).reshape(-1)
    fwd_mine = dot(pick(mine, nfreq), base_fwd, ((0,), (0,))).astype(BF)

    spec = dot(fwd_start, focus_start, ((1,), (2,))).astype(BF)
    spec = spec.reshape(NY * NC, NX * 2, points * own)
    marks = (onset - ONSET_MID).astype(BF).reshape(NX, NC, sub * own)
    marks = jnp.broadcast_to(marks.transpose(1, 0, 2)[None], (NY, NC, NX, sub * own))
    marks = marks.reshape(NY * NC, 1, NX * sub * own)
    marks = jnp.pad(marks, ((0, 0), (0, 0), (0, points * own - NX * sub * own)))
    got = exchange(jnp.concatenate([spec, marks], axis=1), ("y", "c"))
    half = NY * NC * own
    send = got[:, : NX * 2].reshape(NY * NC, NX, 2, ngrp, sub, own)
    send = send.transpose(1, 3, 2, 4, 0, 5).reshape(NX, 2 * points, half)
    marks = got[:, NX * 2, : NX * sub * own].reshape(NY * NC, NX, sub, own).transpose(1, 2, 0, 3).reshape(NX, sub, half)
    send = jnp.concatenate([send, marks], axis=1)[:, None]
    send = jnp.broadcast_to(send, (NX, NZ, 2 * points + sub, half))
    got = exchange(send.reshape(NX * NZ, 2 * points + sub, half), ("x", "z"))
    got = got.reshape(NX, NZ, 2 * points + sub, half)
    src0 = got[:, :, : 2 * points].transpose(2, 1, 0, 3).reshape(2 * points, cols)
    marks = lax.dynamic_index_in_dim(got[:, :, 2 * points :], zi, 1, keepdims=False)
    marks = marks.transpose(1, 0, 2).reshape(1, sub * rows).astype(jnp.int32) + ONSET_MID
    times = lax.broadcasted_iota(jnp.int32, (nsamp, 1), 0)
    keep = (times < marks) | (times >= nsamp - marks)

    def convolve(src):
        a = dot(src, mat_re, ((1,), (1,))).reshape(ngrp, 2, sub, rows)
        b = dot(src, mat_im, ((1,), (1,))).reshape(ngrp, 2, sub, rows)
        out = jnp.stack([a[:, 0] - b[:, 1], a[:, 1] + b[:, 0]], axis=1)
        return out.astype(BF)

    def correlate(src):
        turned = jnp.stack([src[:, 1], -src[:, 0]], axis=1).reshape(2 * points, rows)
        src = src.reshape(2 * points, rows)
        out = dot(src, mat_re, ((1,), (0,))) + dot(turned, mat_im, ((1,), (0,)))
        return out.astype(BF)

    def windowed(spectra):
        trace = dot(inv, spectra, ((1,), (0,)))
        trace = jnp.where(keep, trace, 0.0).astype(BF)
        return dot(fwd_mine, trace, ((1,), (0,))).astype(BF)

    def own_trace(spectra):
        flat = spectra.transpose(0, 2, 1, 3, 4).reshape(2 * nfreq, points * own)
        trace = dot(flat, inv, ((0,), (1,))).reshape(points, own, nsamp)
        when = lax.broadcasted_iota(jnp.int32, (1, 1, nsamp), 2)
        inside = (when < onset[:, :, None]) | (when >= nsamp - onset[:, :, None])
        return jnp.where(inside, trace, 0.0)

    src = src0
    for step in range(ITERS):
        last = step == ITERS - 1
        out = convolve(src)
        send = out.reshape(1, NX, NC, 2, sub * rows)
        send = jnp.broadcast_to(send, (NY, NX, NC, 2, sub * rows)).reshape(nfreq, 2 * sub * rows // 128, 128)
        if last:
            tail = out.reshape(2 * points, NX, NY, NC, own).transpose(2, 1, 3, 0, 4)
            send = jnp.concatenate([send, tail.reshape(nfreq, 2 * points * own // 128, 128)], axis=1)
        got = exchange(send, ("y", "x", "c"))
        if last:
            tail = got[:, 2 * sub * rows // 128 :].reshape(nfreq, ngrp, 2, sub, own)
            focus_minus = own_trace(tail).astype(BF)
            got = got[:, : 2 * sub * rows // 128]
        back = windowed(got.reshape(2 * nfreq, sub * rows))
        got = exchange(back.reshape(ngrp, 2, sub * rows), ("x", "c"))
        part = correlate(got.reshape(ngrp, 2, sub, rows))
        if not last:
            send = part.reshape(ngrp, 2 * sub, NZ, rows).transpose(0, 2, 1, 3)
            got = exchange(send.reshape(ngrp * NZ, 2 * sub, rows), ("x", "c", "z"))
            total = got.reshape(ngrp, NZ, 2, sub * rows).astype(F32).sum(axis=1).astype(BF)
            send = jnp.broadcast_to(total[None], (NY, ngrp, 2, sub * rows))
            got = exchange(send, "y")
            back = windowed(got.reshape(2 * nfreq, sub * rows))
            send = jnp.broadcast_to(back.reshape(ngrp, 1, 2, sub * rows), (ngrp, NZ, 2, sub * rows))
            got = exchange(send.reshape(ngrp * NZ, 2, sub * rows), ("x", "c", "z"))
            more = got.reshape(ngrp, NZ, 2 * sub, rows).transpose(0, 2, 1, 3).reshape(2 * points, cols)
            src = (src0.astype(F32) + more.astype(F32)).astype(BF)
    send = part.reshape(2 * points, NZ, NX, half).transpose(2, 1, 0, 3).reshape(NX * NZ, 2 * points, half)
    got = exchange(send, ("x", "z")).reshape(NX, NZ, 2 * points, half)
    total = got.astype(F32).sum(axis=1).astype(BF)
    send = total.reshape(NX, 2 * points, NY * NC, own).transpose(2, 0, 1, 3)
    got = exchange(send.reshape(NY * NC, NX, 2 * points * own), ("y", "c"))
    got = got.reshape(NY, NC, NX, ngrp, 2, sub, own).transpose(0, 2, 1, 3, 4, 5, 6)
    update = own_trace(got.reshape(nfreq, ngrp, 2, sub, own))
    focus_plus = (focus_start.astype(F32) + update).astype(BF)
    return (focus_plus, focus_minus)


def solution(mesh):
    fine = Mesh(mesh.devices.reshape(NX, NY, NC, NZ), ("x", "y", "c", "z"))
    receivers = ("z", "x", "y", "c")
    slabs = ("x", "y", "c")
    return jax.shard_map(
        shards,
        mesh=fine,
        in_specs=(
            P(None, receivers, None),
            P(None, receivers),
            P(),
            P(slabs, "z", None),
            P(slabs, "z", None),
        ),
        out_specs=(P(None, receivers, None), P(None, receivers, None)),
        check_vma=False,
    )
```

time: 298 us -> 188 us (0.63)
  blocking collectives: 141 us -> 74.8 us
  waiting for transfers between devices: 83.4 us -> 41 us
  local copies, waits for them, and re-layouts: 8.18 us -> 24.4 us
  between operations: 14.2 us -> 1.42 us
  other arithmetic: 5.54 us -> 1.37 us
    reduce_scatter x2 -> x0, waiting for transfers between devices: 54.3 us -> none  [shards(): lax.psum_scatter(jnp.concatenate([out_re, out_im], axis=1).astype(jnp.bfl...]
    all_gather x2 -> x0, blocking collectives: 49.9 us -> none  [shards(): full = lax.all_gather(convolve_owned, 'rcv', axis=3, tiled=True)]
    all_to_all x5 -> x6, blocking collectives: 91.5 us -> 74.8 us  [exchange(): return lax.all_to_all(values, axes, 0, 0, tiled=True)]
    all_to_all x3 -> x5, waiting for transfers between devices: 29.1 us -> 41 us  [exchange(): return lax.all_to_all(values, axes, 0, 0, tiled=True)]
    transpose x0 -> x12, local copies, waits for them, and re-layouts: none -> 6.72 us  [the longest x1 2.38 us: shards(): got.reshape(NY, NC, NX, ngrp, 2, sub, own).transpose(0, 2, 1, 3, 4, 5, 6)]
    reshape x8 -> x28, local copies, waits for them, and re-layouts: 1.57 us -> 7.49 us  [the longest x1 1.13 us: shards(): got.reshape(NY, NC, NX, ngrp, 2, sub, own).transpose(0, 2, 1, 3, 4, 5, 6)]
    cos x2 -> x0, other arithmetic: 3.18 us -> none  [make_tables(): jnp.cos(angle)]
    dot_general x22 -> x16, matrix products: 6.84 us -> 7.82 us  [dot(): return lax.dot_general(a, b, (dims, ((), ())), preferred_element_type=F32)]
  transfers between devices with their start and end apart: 5 -> 5, of which waited for: 5 -> 5; matrix products, arithmetic and copies ran while one was open for 1% -> 2% of each run, Pallas kernels for 0% -> 0%
where the time goes in v1:
time: 188 us
  blocking collectives  74.8 us (40%)
  waiting for transfers between devices  41 us (22%)
  starting transfers between devices  37 us (20%)
  local copies, waits for them, and re-layouts  24.4 us (13%)
  matrix products  7.82 us (4%)
    all_to_all x6, blocking collectives, exchange(): return lax.all_to_all(values, axes, 0, 0, tiled=True)  74.8 us
    all_to_all x5, waiting for transfers between devices, exchange(): return lax.all_to_all(values, axes, 0, 0, tiled=True)  41 us
    all_to_all x5, starting transfers between devices, exchange(): return lax.all_to_all(values, axes, 0, 0, tiled=True)  37 us
    dot_general x16, matrix products, dot(): return lax.dot_general(a, b, (dims, ((), ())), preferred_element_type=F32)  7.82 us
    unnamed x23, local copies, waits for them, and re-layouts  5.64 us
  transfers between devices with their start and end apart: 5, of which 5 were waited for; matrix products, arithmetic and copies ran while one was open for 2% of the time, Pallas kernels for 0%

profile of v1, /device:TPU:1, one launch (start us, length us, event | category | flops | bytes accessed | tf_op | source)
XLA Modules:
  0.0 187.8 jit_solution(12169055055534970260)
XLA Ops:
  0.6 0.8 reshape.247
  1.5 0.7 add_convert_fusion
  2.5 0.2 copy.166
  3.2 1.5 convolution_convert_fusion.3
  4.7 0.3 reshape.248
  5.1 0.3 copy.167
  5.5 0.7 reshape.296
  6.2 10.2 %all-to-all-start = ((bf16[16,2,288]{2,1,0:T(2,128)(2,1)}), bf16[16,2,288]{2,1,0:T(2,128)(2,1)S(1)}, u32[]{:S(2)}, u32[]{:S(2)}) async-start(bf16[16,2,288]{2,1,0:T(2,128)(2,1)} %reshape.296), calls=%async_computation | async-start | bytes 49152 | tf_op jit(solution)/shard_map/all_to_all | solution.py:40
  16.8 0.2 convolution_convert_fusion.2
  17.0 6.9 %all-to-all-done = bf16[16,2,288]{2,1,0:T(2,128)(2,1)S(1)} async-done(((bf16[16,2,288]{2,1,0:T(2,128)(2,1)}), bf16[16,2,288]{2,1,0:T(2,128)(2,1)S(1)}, u32[]{:S(2)}, u32[]{:S(2)}) %all-to-all-start) | async-done | bytes 18464 | tf_op jit(solution)/shard_map/all_to_all | solution.py:40
  24.0 0.1 copy.171
  24.4 0.8 copy.169
  25.3 0.5 reshape.252
  25.9 0.9 reshape.298
  26.7 11.2 %all-to-all-start.1 = ((bf16[32,2,1088]{2,1,0:T(2,128)(2,1)}), bf16[32,2,1088]{2,1,0:T(2,128)(2,1)S(1)}, u32[]{:S(2)}, u32[]{:S(2)}) async-start(bf16[32,2,1088]{2,1,0:T(2,128)(2,1)} %reshape.298), calls=%async_computation.1 | async-start | bytes 294912 | tf_op jit(solution)/shard_map/all_to_all | solution.py:40
  38.2 0.3 convolution_convert_fusion
  38.5 8.7 %all-to-all-done.1 = bf16[32,2,1088]{2,1,0:T(2,128)(2,1)S(1)} async-done(((bf16[32,2,1088]{2,1,0:T(2,128)(2,1)}), bf16[32,2,1088]{2,1,0:T(2,128)(2,1)S(1)}, u32[]{:S(2)}, u32[]{:S(2)}) %all-to-all-start.1) | async-done | bytes 139296 | tf_op jit(solution)/shard_map/all_to_all | solution.py:40
  47.2 0.3 reshape.299
  47.7 0.2 dot_general.74
  47.9 0.8 copy-done.1
  48.7 0.4 fusion.22
  49.1 0.4 fusion.18
  49.8 0.7 reshape.256
  50.5 6.4 %all-to-all-start.2 = ((bf16[64,8,128]{2,1,0:T(8,128)(2,1)}), bf16[64,8,128]{2,1,0:T(8,128)(2,1)S(1)}, u32[]{:S(2)}, u32[]{:S(2)}) async-start(bf16[64,8,128]{2,1,0:T(8,128)(2,1)} %reshape.256), calls=%async_computation.2 | async-start | bytes 262144 | tf_op jit(solution)/shard_map/all_to_all | solution.py:40
  57.0 11.2 %all-to-all-done.2 = bf16[64,8,128]{2,1,0:T(8,128)(2,1)S(1)} async-done(((bf16[64,8,128]{2,1,0:T(8,128)(2,1)}), bf16[64,8,128]{2,1,0:T(8,128)(2,1)S(1)}, u32[]{:S(2)}, u32[]{:S(2)}) %all-to-all-start.2) | async-done | bytes 131104 | tf_op jit(solution)/shard_map/all_to_all | solution.py:40
  68.3 0.9 fusion.15
  69.2 7.4 %all_to_all.55 = bf16[8,2,512]{2,1,0:T(2,128)(2,1)S(1)} all-to-all(bf16[8,2,512]{2,1,0:T(2,128)(2,1)S(1)} %reshape.258), channel_id=1, replica_groups=mesh['x'=4,'y'=8,'c'=2,'z'=8] {'x','c'}, dimensions={0} | all-to-all | bytes 32768 | tf_op jit(solution)/shard_map/all_to_all | solution.py:40
  76.7 0.3 fusion.26
  77.0 0.3 fusion
  77.5 14.3 %all_to_all.56 = bf16[64,4,256]{2,1,0:T(4,128)(2,1)S(1)} all-to-all(bf16[64,4,256]{2,1,0:T(4,128)(2,1)S(1)} %copy.182), channel_id=1, replica_groups=mesh['x'=4,'y'=8,'c'=2,'z'=8] {'x','c','z'}, dimensions={0} | all-to-all | bytes 262144 | tf_op jit(solution)/shard_map/all_to_all | solution.py:40
  92.1 10.3 %all_to_all.57 = bf16[8,8,2,512]{3,2,1,0:T(2,128)(2,1)S(1)} all-to-all(bf16[8,8,2,512]{3,2,1,0:T(2,128)(2,1)S(1)} %broadcast_in_dim.54), channel_id=1, replica_groups=mesh['x'=4,'y'=8,'c'=2,'z'=8] {'y'}, dimensions={0} | all-to-all | bytes 262144 | tf_op jit(solution)/shard_map/all_to_all | solution.py:40
  102.5 0.9 fusion.14
  103.5 16.5 %all_to_all.58 = bf16[64,2,512]{2,1,0:T(2,128)(2,1)S(1)} all-to-all(bf16[64,2,512]{2,1,0:T(2,128)(2,1)S(1)} %bitcast.136), channel_id=1, replica_groups=mesh['x'=4,'y'=8,'c'=2,'z'=8] {'x','c','z'}, dimensions={0} | all-to-all | bytes 262144 | tf_op jit(solution)/shard_map/all_to_all | solution.py:40
  120.2 0.2 reshape.282
  120.6 0.2 convert_element_type.136
  120.9 0.4 fusion.20
  121.3 0.4 fusion.16
  121.8 1.1 convert_element_type.137
  123.0 0.6 copy.192
  123.6 0.8 reshape.288
  124.7 18.2 %all_to_all.59 = bf16[64,9,128]{2,1,0:T(8,128)(2,1)S(1)} all-to-all(bf16[64,9,128]{2,1,0:T(8,128)(2,1)S(1)} %pad_maximum_fusion), channel_id=1, replica_groups=mesh['x'=4,'y'=8,'c'=2,'z'=8] {'y','x','c'}, dimensions={0} | all-to-all | bytes 294912 | tf_op jit(solution)/shard_map/all_to_all | solution.py:40
  143.0 0.9 fusion.13
  143.9 8.0 %all_to_all.60 = bf16[8,2,512]{2,1,0:T(2,128)(2,1)S(1)} all-to-all(bf16[8,2,512]{2,1,0:T(2,128)(2,1)S(1)} %reshape.269), channel_id=1, replica_groups=mesh['x'=4,'y'=8,'c'=2,'z'=8] {'x','c'}, dimensions={0} | all-to-all | bytes 32768 | tf_op jit(solution)/shard_map/all_to_all | solution.py:40
  152.0 0.3 fusion.28
  152.4 0.3 fusion.1
  152.7 0.2 reshape.272
  153.0 0.8 reshape.300
  153.9 3.9 %all-to-all-start.9 = ((bf16[32,2,1024]{2,1,0:T(2,128)(2,1)}), bf16[32,2,1024]{2,1,0:T(2,128)(2,1)S(1)}, u32[]{:S(2)}, u32[]{:S(2)}) async-start(bf16[32,2,1024]{2,1,0:T(2,128)(2,1)} %reshape.300), calls=%async_computation.9 | async-start | bytes 262144 | tf_op jit(solution)/shard_map/all_to_all | solution.py:40
  157.9 0.6 copy.204
  158.5 0.5 reshape.281
  159.1 7.8 %all-to-all-done.9 = bf16[32,2,1024]{2,1,0:T(2,128)(2,1)S(1)} async-done(((bf16[32,2,1024]{2,1,0:T(2,128)(2,1)}), bf16[32,2,1024]{2,1,0:T(2,128)(2,1)S(1)}, u32[]{:S(2)}, u32[]{:S(2)}) %all-to-all-start.9) | async-done | bytes 131104 | tf_op jit(solution)/shard_map/all_to_all | solution.py:40
  166.9 0.2 reshape.301
  167.3 0.1 copy.196
  167.4 0.7 copy.197
  168.1 5.4 %all-to-all-start.10 = ((bf16[16,4,128]{2,1,0:T(4,128)(2,1)}), bf16[16,4,128]{2,1,0:T(4,128)(2,1)S(1)}, u32[]{:S(2)}, u32[]{:S(2)}) async-start(bf16[16,4,128]{2,1,0:T(4,128)(2,1)} %copy.197), calls=%async_computation.10 | async-start | bytes 32768 | tf_op jit(solution)/shard_map/all_to_all | solution.py:40
  173.5 0.2 fusion.12
  173.7 0.8 copy.208
  174.5 6.4 %all-to-all-done.10 = bf16[16,4,128]{2,1,0:T(4,128)(2,1)S(1)} async-done(((bf16[16,4,128]{2,1,0:T(4,128)(2,1)}), bf16[16,4,128]{2,1,0:T(4,128)(2,1)S(1)}, u32[]{:S(2)}, u32[]{:S(2)}) %all-to-all-start.10) | async-done | bytes 16416 | tf_op jit(solution)/shard_map/all_to_all | solution.py:40
  180.9 1.1 reshape.277
  182.1 2.4 %copy.199 = bf16[8,4,2,8,2,2,4]{3,2,1,0,6,5,4:T(2,128)(2,1)S(1)} copy(bf16[8,4,2,8,2,2,4]{6,5,4,3,2,0,1:T(2,128)(2,1)S(1)} %bitcast.126) | data formatting | bytes 32768 | tf_op jit(solution)/shard_map/transpose | solution.py:138
  184.4 1.7 copy.200
  186.2 0.5 reshape.279
  186.8 0.2 fusion.11
  187.0 0.8 copy.207
  (107 shorter events, 4.8 us)
Async XLA Ops:
  0.6 48.5 %copy-start = (bf16[1,256,2048]{2,1,0:T(8,128)(2,1)S(1)}, bf16[1,256,2048]{2,1,0:T(8,128)(2,1)}, u32[]{:S(2)}) copy-start(bf16[1,256,2048]{2,1,0:T(8,128)(2,1)} %param.10) | copy-start | bytes 3145732
  2.7 14.1 %copy-start.2 = (bf16[128,1024]{1,0:T(8,128)(2,1)S(1)}, bf16[128,1024]{1,0:T(8,128)(2,1)}, u32[]{:S(2)}) copy-start(bf16[128,1024]{1,0:T(8,128)(2,1)} %constant.40.clone) | copy-start | bytes 786436
  6.2 17.6 %all-to-all-start = ((bf16[16,2,288]{2,1,0:T(2,128)(2,1)}), bf16[16,2,288]{2,1,0:T(2,128)(2,1)S(1)}, u32[]{:S(2)}, u32[]{:S(2)}) async-start(bf16[16,2,288]{2,1,0:T(2,128)(2,1)} %reshape.296), calls=%async_computation | async-start | bytes 49152 | tf_op jit(solution)/shard_map/all_to_all | solution.py:40
  25.3 12.9 %copy-start.3 = (bf16[128,1024]{1,0:T(8,128)(2,1)S(1)}, bf16[128,1024]{1,0:T(8,128)(2,1)}, u32[]{:S(2)}) copy-start(bf16[128,1024]{1,0:T(8,128)(2,1)} %constant.41.clone) | copy-start | bytes 786436
  26.7 20.4 %all-to-all-start.1 = ((bf16[32,2,1088]{2,1,0:T(2,128)(2,1)}), bf16[32,2,1088]{2,1,0:T(2,128)(2,1)S(1)}, u32[]{:S(2)}, u32[]{:S(2)}) async-start(bf16[32,2,1088]{2,1,0:T(2,128)(2,1)} %reshape.298), calls=%async_computation.1 | async-start | bytes 294912 | tf_op jit(solution)/shard_map/all_to_all | solution.py:40
  47.5 1.2 copy-start.1
  50.5 17.7 %all-to-all-start.2 = ((bf16[64,8,128]{2,1,0:T(8,128)(2,1)}), bf16[64,8,128]{2,1,0:T(8,128)(2,1)S(1)}, u32[]{:S(2)}, u32[]{:S(2)}) async-start(bf16[64,8,128]{2,1,0:T(8,128)(2,1)} %reshape.256), calls=%async_computation.2 | async-start | bytes 262144 | tf_op jit(solution)/shard_map/all_to_all | solution.py:40
  153.9 13.0 %all-to-all-start.9 = ((bf16[32,2,1024]{2,1,0:T(2,128)(2,1)}), bf16[32,2,1024]{2,1,0:T(2,128)(2,1)S(1)}, u32[]{:S(2)}, u32[]{:S(2)}) async-start(bf16[32,2,1024]{2,1,0:T(2,128)(2,1)} %reshape.300), calls=%async_computation.9 | async-start | bytes 262144 | tf_op jit(solution)/shard_map/all_to_all | solution.py:40
  157.9 15.6 %copy-start.5 = (s32[16,4]{0,1:T(4,128)S(1)}, s32[16,4]{0,1:T(4,128)}, u32[]{:S(2)}) copy-start(s32[16,4]{0,1:T(4,128)} %param.8) | copy-start | bytes 772
  168.1 12.8 %all-to-all-start.10 = ((bf16[16,4,128]{2,1,0:T(4,128)(2,1)}), bf16[16,4,128]{2,1,0:T(4,128)(2,1)S(1)}, u32[]{:S(2)}, u32[]{:S(2)}) async-start(bf16[16,4,128]{2,1,0:T(4,128)(2,1)} %copy.197), calls=%async_computation.10 | async-start | bytes 32768 | tf_op jit(solution)/shard_map/all_to_all | solution.py:40
  182.0 4.7 %copy-start.4 = (bf16[16,4,1024]{2,1,0:T(4,128)(2,1)S(1)}, bf16[16,4,1024]{2,1,0:T(4,128)(2,1)}, u32[]{:S(2)}) copy-start(bf16[16,4,1024]{2,1,0:T(4,128)(2,1)} %param.7) | copy-start | bytes 393220

commit v2 on v0

v2 whole, which is shorter than its diff:
```python
import math

import jax
import jax.numpy as jnp
import numpy as np
from jax import lax
from jax.experimental import pallas as pl
from jax.experimental.pallas import tpu as pltpu
from jax.sharding import Mesh
from jax.sharding import PartitionSpec as P

FLO = 8
ITERS = 2
NX, NY, NC, NZ = 4, 8, 2, 8
NA, NG, NI = NY * NC, NX * NC, 4
NF, POINTS, NT = 64, 16, 1024
BLOCK, COLS = 256, 2048
LO, HI = 384, 640
KEPT = NT - (HI - LO)
ONSET_MID = 256
LANES = 128
BF, F32, I32 = jnp.bfloat16, jnp.float32, jnp.int32
VMEM_LIMIT = 8 * 1024 * 1024


def base_tables():
    phase = (np.arange(NT)[None, :] * (FLO + np.arange(NF))[:, None]) % NT
    angle = phase.astype(np.float32) * np.float32(2.0 * math.pi / NT)
    rows = np.concatenate([np.cos(angle), -np.sin(angle)], axis=0)
    forward = (rows * np.float32(1.0 / math.sqrt(NT))).astype(BF)
    inverse = (rows * np.float32(math.sqrt(2.0 / NF))).astype(BF)
    inverse = np.concatenate([inverse[:, :LO], inverse[:, HI:]], axis=1)
    return forward, np.ascontiguousarray(inverse.T)


def iota(shape, dim):
    return lax.broadcasted_iota(I32, shape, dim)


def grid(rows, cols):
    return iota((rows, cols), 0), iota((rows, cols), 1)


def hot(mask):
    return jnp.where(mask, jnp.float32(1), jnp.float32(0)).astype(BF)


def nn(a, b):
    return lax.dot_general(a, b, (((1,), (0,)), ((), ())), preferred_element_type=F32)


def nt(a, b):
    return lax.dot_general(a, b, (((1,), (1,)), ((), ())), preferred_element_type=F32)


def slab_of_bin(bins):
    k, _ = grid(NF, NF)
    return hot(k == bins)


def start_kernel(bins, onset, focus, base, out, flat):
    for p in range(POINTS):
        flat[NI * p : NI * (p + 1), :] = focus[p].astype(F32)
    rows = flat[...].astype(BF)
    none = jnp.zeros_like(rows)
    spec = nt(base[:NF], jnp.concatenate([rows, none], axis=0))
    spec = spec + nt(base[NF:], jnp.concatenate([none, rows], axis=0))
    m, j = grid(8 * NA, NF)
    place = hot(((m & 7) < NX) & (j == (m & 7) * NA + (m >> 3)))
    order = nt(place, slab_of_bin(bins[...])).astype(BF)
    sent = nn(order, spec.astype(BF))
    lane = iota((POINTS, LANES), 1)
    marks = jnp.zeros((POINTS, LANES), F32)
    for i in range(NI):
        marks = marks + jnp.where((lane & 63) == i, (onset[:, i : i + 1] - ONSET_MID).astype(F32), 0.0)
    m, p = grid(8 * NA, POINTS)
    group = ((m & 7) - NX) * NC + ((m >> 3) & 1)
    for h in range(2):
        mine = hot(((m & 7) >= NX) & (p == group + NG * h))
        sent = sent + nn(mine, jnp.where((lane >> 6) == h, marks, 0.0).astype(BF))
    out[...] = sent.reshape(NA, 8, LANES).astype(BF)


def tables_kernel(where, bins, forward, inverse, fwd, inv):
    holds = slab_of_bin(bins[...])
    j, f = grid(NF, NF)
    order = nn(holds, hot(j == ((f >> 1) & 3) * NA + (f >> 3) * NC + (f & 1))).astype(BF)
    r64, c128 = grid(NF, LANES)
    r128, c64 = grid(LANES, NF)
    both = jnp.zeros((LANES, LANES), F32)
    for part in range(2):
        wide = nn(order, hot(c128 == r64 + NF * part)).astype(BF)
        both = both + nn(hot(r128 == c64 + NF * part), wide)
    inv[...] = nn(inverse[...], both.astype(BF)).astype(BF)
    m, j = grid(2 * NG, NF)
    mine = hot(j == ((m & 7) >> 1) * NA + where[0] * NC + (m & 1))
    mine = nt(mine, holds).astype(BF)
    m, k = grid(2 * NG, LANES)
    wide = nn(mine, hot((c128 & 63) == r64))
    wide = jnp.where((k >> 6) == (m >> 3), wide, 0.0).astype(BF)
    fwd[:, :LO] = nn(wide, forward[:, :LO]).astype(BF)
    fwd[:, LO:] = nn(wide, forward[:, HI:]).astype(BF)


def middle_kernel(got, out, rows):
    rows[...] = got[...].astype(F32).reshape(8 * NA, LANES)
    line = jnp.concatenate([rows[pl.ds(e, NA, stride=8), :] for e in range(8)], axis=1).astype(BF)
    m, a = grid(NA * NI, NA)
    spread = nn(hot((m >> 2) == a), line)
    m, lane = grid(NA * NI, LANES)
    stacked = []
    for e in range(8):
        piece = spread[:, LANES * e : LANES * (e + 1)]
        for part in range(2):
            fits = ((lane & 3) == (m & 3)) & ((lane >> 6) == part)
            stacked.append(jnp.where(fits, piece, 0.0))
    stacked = jnp.concatenate(stacked, axis=0).astype(BF)
    p, lane = grid(POINTS, LANES)
    turned = nt(hot(((lane >> 2) & 15) == p), stacked)
    for x in range(NX):
        spec = turned[:, LANES * x : LANES * (x + 1)]
        mark = turned[:8, LANES * (NX + x) : LANES * (NX + x + 1)]
        message = jnp.concatenate([spec, mark], axis=0).astype(BF)
        for z in range(NZ):
            out[x, z] = message


def swap(a, b):
    lane = iota(a.shape, 1)
    low = lane < LANES // 2
    return (
        jnp.where(low, a, pltpu.roll(b, LANES // 2, 1)),
        jnp.where(low, pltpu.roll(a, LANES // 2, 1), b),
    )


def convolve(src, mat_re, mat_im, out, turn):
    a = nt(src, mat_re[...])
    b = nt(src, mat_im[...])
    parts = (a[:POINTS] - b[POINTS:], a[POINTS:] + b[:POINTS])
    for part in range(2):
        for h in range(2):
            for half in range(2):
                q = 4 * part + 2 * h + half
                turn[pl.ds(q, NG, stride=8), :] = parts[part][NG * h : NG * (h + 1), LANES * half : LANES * (half + 1)]
    message = turn[...].reshape(NG, 8, LANES).astype(BF)
    for y in range(NY):
        out[y] = message


def first_conv_kernel(where, got, mat_re, mat_im, out, src, marks, turn):
    for z in range(NZ):
        for half in range(2):
            a = got[2 * half, z].astype(F32)[:POINTS]
            b = got[2 * half + 1, z].astype(F32)[:POINTS]
            at = LANES * (2 * z + half)
            re, im = swap(a, b)
            src[:POINTS, at : at + LANES] = re.astype(BF)
            src[POINTS:, at : at + LANES] = im.astype(BF)
    for half in range(2):
        a = got[2 * half, where[1]].astype(F32)[POINTS:]
        b = got[2 * half + 1, where[1]].astype(F32)[POINTS:]
        for h, row in enumerate(swap(a, b)):
            at = LANES * (2 * h + half)
            marks[:, at : at + LANES] = row.astype(I32) + ONSET_MID
    convolve(src[...], mat_re, mat_im, out, turn)


def next_conv_kernel(got, first, mat_re, mat_im, out, rows, src, turn):
    rows[...] = got[...].astype(F32).reshape(NG * NZ * 8, LANES)
    for part in range(2):
        for z in range(NZ):
            for half in range(2):
                more = [rows[pl.ds(8 * z + 4 * part + 2 * h + half, NG, stride=8 * NZ), :] for h in range(2)]
                more = jnp.concatenate(more, axis=0)
                at = LANES * (2 * z + half)
                old = first[POINTS * part : POINTS * (part + 1), at : at + LANES].astype(F32)
                src[POINTS * part : POINTS * (part + 1), at : at + LANES] = (old + more).astype(BF)
    convolve(src[...], mat_re, mat_im, out, turn)


def window_traces(got, inv, fwd, marks, rows, turn):
    rows[...] = got[...].astype(F32).reshape(NF * 8, LANES)
    spectra = []
    for n in range(4):
        parts = [rows[pl.ds(4 * part + n, NF, stride=8), :] for part in range(2)]
        spectra.append(jnp.concatenate(parts, axis=0))
    spectra = jnp.concatenate(spectra, axis=1).astype(BF)
    trace = nn(inv[...], spectra)
    t = iota((KEPT, 1), 0)
    t = jnp.where(t < LO, t, t + (HI - LO))
    mark = marks[:1, :]
    trace = jnp.where((t < mark) | (t >= NT - mark), trace, 0.0).astype(BF)
    spec = nn(fwd[...], trace)
    for part in range(2):
        for n in range(4):
            turn[pl.ds(4 * part + n, NG, stride=8), :] = spec[NG * part : NG * (part + 1), LANES * n : LANES * (n + 1)]
    return spectra, turn[...].reshape(NG, 8, LANES)


def time_kernel(got, inv, fwd, marks, out, rows, turn):
    out[...] = window_traces(got, inv, fwd, marks, rows, turn)[1].astype(BF)


def time_copies_kernel(got, inv, fwd, marks, out, rows, turn):
    message = window_traces(got, inv, fwd, marks, rows, turn)[1].astype(BF)
    for z in range(NZ):
        out[:, z] = message


def last_time_kernel(where, got, inv, fwd, marks, out, rows, turn):
    spectra, message = window_traces(got, inv, fwd, marks, rows, turn)
    m, n = grid(8 * NG, 2 * BLOCK)
    own = ((m >> 2) & 1) * BLOCK + (m >> 4) * 64 + where[0] * 8 + ((m >> 3) & 1) * 4 + (m & 3)
    own = nt(hot(n == own), spectra).reshape(NG, 8, LANES)
    out[...] = jnp.concatenate([message, own], axis=1).astype(BF)


def correlate(got, mat_re, mat_im, rows, height):
    rows[...] = got[...].astype(F32).reshape(NG * height, LANES)
    parts = []
    for part in range(2):
        halves = []
        for half in range(2):
            both = [rows[pl.ds(4 * part + 2 * h + half, NG, stride=height), :] for h in range(2)]
            halves.append(jnp.concatenate(both, axis=0))
        parts.append(jnp.concatenate(halves, axis=1))
    straight = jnp.concatenate(parts, axis=0).astype(BF)
    turned = jnp.concatenate([parts[1], -parts[0]], axis=0).astype(BF)
    for z in range(NZ):
        at = slice(BLOCK * z, BLOCK * (z + 1))
        yield z, nn(straight, mat_re[:, at]) + nn(turned, mat_im[:, at])


def corr_kernel(got, mat_re, mat_im, out, rows, turn):
    for z, block in correlate(got, mat_re, mat_im, rows, 8):
        for part in range(2):
            for h in range(2):
                for half in range(2):
                    q = 4 * part + 2 * h + half
                    at = POINTS * part + NG * h
                    turn[pl.ds(8 * z + q, NG, stride=8 * NZ), :] = block[at : at + NG, LANES * half : LANES * (half + 1)]
    out[...] = turn[...].reshape(NG * NZ, 8, LANES).astype(BF)


def last_corr_kernel(got, mat_re, mat_im, out, rows):
    for z, block in correlate(got, mat_re, mat_im, rows, 16):
        for half in range(2):
            at = slice(LANES * half, LANES * (half + 1))
            a, b = swap(block[:POINTS, at], block[POINTS:, at])
            out[2 * half, z] = a.astype(BF)
            out[2 * half + 1, z] = b.astype(BF)


def sum_kernel(got, out):
    total = got[...].astype(F32).reshape(NG, NZ, 8, LANES).sum(axis=1)
    total = total.reshape(NG * 8, LANES).astype(BF)
    for y in range(NY):
        out[y] = total


def last_sum_kernel(got, out):
    total = got[...].astype(F32).sum(axis=1).astype(BF)
    p, lane = grid(POINTS, LANES)
    spread = hot(((lane >> 2) & 15) == p)
    m, lane = grid(LANES, LANES)
    fits = ((lane & 3) == (m & 3)) & ((lane >> 6) == (m >> 6))
    sent = jnp.zeros((8 * NA, LANES), F32)
    for x in range(NX):
        turned = nn(total[x].astype(F32).T.astype(BF), spread)
        turned = jnp.where(fits, turned, 0.0).astype(BF)
        pick = hot(((m & 7) == x) & ((m >> 3) == ((lane >> 2) & 15)))
        sent = sent + nn(pick, turned)
    out[...] = sent.reshape(NA, 8, LANES).astype(BF)


def keep_own(trace, onset, p):
    t = iota((NI, KEPT), 1)
    t = jnp.where(t < LO, t, t + (HI - LO))
    mark = onset[:, p : p + 1]
    return jnp.where((t < mark) | (t >= NT - mark), trace, 0.0)


def minus_kernel(got, inv, onset, out):
    own = got[...].astype(F32)[:, 8:].reshape(8 * NG, LANES).astype(BF)
    trace = nt(own, inv[...])
    for p in range(POINTS):
        at = 8 * (p % NG) + NI * (p // NG)
        kept = keep_own(trace[at : at + NI], onset, p).astype(BF)
        out[p, :, :LO] = kept[:, :LO]
        out[p, :, LO:HI] = jnp.zeros((NI, HI - LO), BF)
        out[p, :, HI:] = kept[:, LO:]


def plus_kernel(got, inv, onset, focus, out):
    rows = got[...].astype(F32).reshape(8 * NA, LANES).T.astype(BF)
    m, k = grid(8 * NA, LANES)
    arrival = ((m >> 4) << 3) + ((m & 7) << 1) + ((m >> 3) & 1)
    spectra = jnp.zeros((POINTS * NI, LANES), F32)
    for part in range(2):
        place = hot(((m & 7) < NX) & (k == arrival + NF * part))
        spectra = spectra + nn(rows[NF * part : NF * (part + 1)], place)
    trace = nt(spectra.astype(BF), inv[...])
    for p in range(POINTS):
        kept = keep_own(trace[NI * p : NI * (p + 1)], onset, p)
        start = focus[p]
        out[p, :, :LO] = (start[:, :LO].astype(F32) + kept[:, :LO]).astype(BF)
        out[p, :, LO:HI] = start[:, LO:HI]
        out[p, :, HI:] = (start[:, HI:].astype(F32) + kept[:, LO:]).astype(BF)


def call(kernel, outs, scratch=(), scalars=0):
    single = not isinstance(outs, list)
    shapes = [jax.ShapeDtypeStruct(shape, dtype) for shape, dtype in ([outs] if single else outs)]

    def run(*args):
        specs = [pl.BlockSpec(memory_space=pltpu.SMEM if n < scalars else pltpu.VMEM) for n in range(len(args))]
        got = pl.pallas_call(
            kernel,
            out_shape=shapes,
            in_specs=specs,
            out_specs=[pl.BlockSpec(memory_space=pltpu.VMEM)] * len(shapes),
            scratch_shapes=[pltpu.VMEM(shape, dtype) for shape, dtype in scratch],
            compiler_params=pltpu.CompilerParams(vmem_limit_bytes=VMEM_LIMIT),
        )(*args)
        return got[0] if single else got

    return run


def exchange(values, axes):
    return lax.all_to_all(values, axes, 0, 0, tiled=True)


def shards(focus_start, onset, bins, refl_real, refl_imag):
    mats = (refl_real[0], refl_imag[0])
    where = jnp.stack([lax.axis_index("y"), lax.axis_index("z")]).astype(I32)
    bins = bins.reshape(1, NF)
    onset_turned = onset.T
    forward, inverse = base_tables()
    full = ((8 * NF, LANES), F32)
    small = ((8 * NG, LANES), F32)

    send = call(start_kernel, ((NA, 8, LANES), BF), [((POINTS * NI, NT), F32)])(bins, onset, focus_start, forward)
    got = exchange(send, ("y", "c"))
    fwd, inv = call(tables_kernel, [((2 * NG, KEPT), BF), ((KEPT, LANES), BF)], scalars=1)(where, bins, forward, inverse)
    send = call(middle_kernel, ((NX, NZ, POINTS + 8, LANES), BF), [((8 * NA, LANES), F32)])(got)
    got = exchange(send.reshape(NX * NZ, POINTS + 8, LANES), ("x", "z")).reshape(NX, NZ, POINTS + 8, LANES)
    outs = [((NY, NG, 8, LANES), BF), ((2 * POINTS, COLS), BF), ((8, 2 * BLOCK), I32)]
    send, first, marks = call(first_conv_kernel, outs, [small], scalars=1)(where, got, *mats)
    for step in range(ITERS):
        got = exchange(send.reshape(NF, 8, LANES), ("y", "x", "c"))
        if step == ITERS - 1:
            send = call(last_time_kernel, ((NG, 16, LANES), BF), [full, small], scalars=1)(where, got, inv, fwd, marks)
            got = exchange(send, ("x", "c"))
            focus_minus = call(minus_kernel, ((POINTS, NI, NT), BF))(got, inv, onset_turned)
            break
        send = call(time_kernel, ((NG, 8, LANES), BF), [full, small])(got, inv, fwd, marks)
        got = exchange(send, ("x", "c"))
        send = call(corr_kernel, ((NG * NZ, 8, LANES), BF), [small, full])(got, *mats)
        got = exchange(send, ("x", "c", "z"))
        send = call(sum_kernel, ((NY, NG * 8, LANES), BF))(got)
        got = exchange(send, "y")
        send = call(time_copies_kernel, ((NG, NZ, 8, LANES), BF), [full, small])(got, inv, fwd, marks)
        got = exchange(send.reshape(NG * NZ, 8, LANES), ("x", "c", "z"))
        scratch = [full, ((2 * POINTS, COLS), BF), small]
        send = call(next_conv_kernel, ((NY, NG, 8, LANES), BF), scratch)(got, first, *mats)
    send = call(last_corr_kernel, ((NX, NZ, POINTS, LANES), BF), [((16 * NG, LANES), F32)])(got, *mats)
    got = exchange(send.reshape(NX * NZ, POINTS, LANES), ("x", "z")).reshape(NX, NZ, POINTS, LANES)
    send = call(last_sum_kernel, ((NA, 8, LANES), BF))(got)
    got = exchange(send, ("y", "c"))
    focus_plus = call(plus_kernel, ((POINTS, NI, NT), BF))(got, inv, onset_turned, focus_start)
    return (focus_plus, focus_minus)


def solution(mesh):
    fine = Mesh(mesh.devices.reshape(NX, NY, NC, NZ), ("x", "y", "c", "z"))
    receivers = ("z", "x", "y", "c")
    slabs = ("x", "y", "c")
    return jax.shard_map(
        shards,
        mesh=fine,
        in_specs=(
            P(None, receivers, None),
            P(None, receivers),
            P(),
            P(slabs, "z", None),
            P(slabs, "z", None),
        ),
        out_specs=(P(None, receivers, None), P(None, receivers, None)),
        check_vma=False,
    )
```

time: 298 us -> 170 us (0.57)
  waiting for transfers between devices: 83.4 us -> 26 us
  blocking collectives: 141 us -> 101 us
  between operations: 14.2 us -> 0.76 us
  starting transfers between devices: 37.3 us -> 24.3 us
  Pallas kernels: 0 us -> 12.2 us
  matrix products: 6.84 us -> 0 us
  other arithmetic: 5.54 us -> 0.08 us
  local copies, waits for them, and re-layouts: 8.18 us -> 4.61 us
    reduce_scatter x2 -> x0, waiting for transfers between devices: 54.3 us -> none  [shards(): lax.psum_scatter(jnp.concatenate([out_re, out_im], axis=1).astype(jnp.bfl...]
    all_gather x2 -> x0, blocking collectives: 49.9 us -> none  [shards(): full = lax.all_gather(convolve_owned, 'rcv', axis=3, tiled=True)]
    all_to_all x3, starting transfers between devices: 37.2 us -> 24.3 us  [exchange(): return lax.all_to_all(values, axes, 0, 0, tiled=True)]
    pallas_call x0 -> x14, Pallas kernels: none -> 12.2 us  [run(): pl.pallas_call(kernel, out_shape=shapes, in_specs=specs, out_specs=[pl.Bl...]
    all_to_all x5 -> x8, blocking collectives: 91.5 us -> 101 us  [exchange(): return lax.all_to_all(values, axes, 0, 0, tiled=True)]
    dot_general x22 -> x0, matrix products: 6.84 us -> none  [the longest x4 1.07 us: spectrum(): jnp.einsum('prt,tk->kpr', traces, forward, preferred_element_type=jnp.flo...]
    cos x2 -> x0, other arithmetic: 3.18 us -> none  [make_tables(): jnp.cos(angle)]
    all_to_all x3, waiting for transfers between devices: 29.1 us -> 26 us  [exchange(): return lax.all_to_all(values, axes, 0, 0, tiled=True)]
  transfers between devices with their start and end apart: 5 -> 3, of which waited for: 5 -> 3; matrix products, arithmetic and copies ran while one was open for 1% -> 0% of each run, Pallas kernels for 0% -> 1%
where the time goes in v2:
time: 170 us; the launch traced here: 169 us
  blocking collectives  101 us (59%)
  waiting for transfers between devices  26 us (15%)
  starting transfers between devices  24.3 us (14%)
  Pallas kernels  12.2 us (7%)
  local copies, waits for them, and re-layouts  4.61 us (3%)
    all_to_all x8, blocking collectives, exchange(): return lax.all_to_all(values, axes, 0, 0, tiled=True)  101 us
    all_to_all x3, waiting for transfers between devices, exchange(): return lax.all_to_all(values, axes, 0, 0, tiled=True)  26 us
    all_to_all x3, starting transfers between devices, exchange(): return lax.all_to_all(values, axes, 0, 0, tiled=True)  24.3 us
    pallas_call x14, Pallas kernels, run(): pl.pallas_call(kernel, out_shape=shapes, in_specs=specs, out_specs=[pl.Bl...  12.2 us
    unnamed x23, local copies, waits for them, and re-layouts  4.61 us
  transfers between devices with their start and end apart: 3, of which 3 were waited for; matrix products, arithmetic and copies ran while one was open for 0% of the time, Pallas kernels for 1%

profile of v2, /device:TPU:1, one launch (start us, length us, event | category | flops | bytes accessed | tf_op | source)
XLA Modules:
  0.0 169.4 jit_solution(16332042207935465575)
XLA Ops:
  0.6 0.0 copy-start
  0.6 0.8 copy.9.onset
  1.5 0.0 copy-start.3
  1.5 0.9 copy-done.3
  2.4 0.0 copy-start.5
  2.4 0.9 copy-done.5
  3.3 0.0 copy-start.9
  3.3 0.7 copy-done.9
  4.0 0.5 shard_map.86
  4.5 16.7 %all_to_all.55.got = bf16[16,8,128]{2,1,0:T(8,128)(2,1)S(1)} all-to-all(bf16[16,8,128]{2,1,0:T(8,128)(2,1)S(1)} %shard_map.86), channel_id=1, replica_groups=mesh['x'=4,'y'=8,'c'=2,'z'=8] {'y','c'}, dimensions={0} | all-to-all | bytes 65536 | tf_op jit(solution)/shard_map/all_to_all | solution.py:332
  21.2 1.0 shard_map.87
  22.2 11.9 %all-to-all-start.1 = ((bf16[32,24,128]{2,1,0:T(8,128)(2,1)}), bf16[32,24,128]{2,1,0:T(8,128)(2,1)S(1)}, u32[]{:S(2)}, u32[]{:S(2)}) async-start(bf16[32,24,128]{2,1,0:T(8,128)(2,1)} %bitcast.3), calls=%async_computation.1 | async-start | bytes 393216 | tf_op jit(solution)/shard_map/all_to_all | solution.py:332
  34.2 0.1 pad_add_fusion.where
  34.2 9.3 %all-to-all-done.1 = bf16[32,24,128]{2,1,0:T(8,128)(2,1)S(1)} async-done(((bf16[32,24,128]{2,1,0:T(8,128)(2,1)}), bf16[32,24,128]{2,1,0:T(8,128)(2,1)S(1)}, u32[]{:S(2)}, u32[]{:S(2)}) %all-to-all-start.1) | async-done | bytes 196640 | tf_op jit(solution)/shard_map/all_to_all | solution.py:332
  43.6 0.0 copy-done
  43.6 0.0 copy-start.1
  43.6 1.2 copy-done.1
  44.8 0.0 copy-start.4
  44.8 0.0 copy-start.7
  44.8 0.0 copy-start.10
  44.8 2.0 %shard_map.88 = (bf16[8,8,8,128]{3,2,1,0:T(8,128)(2,1)}, bf16[32,2048]{1,0:T(8,128)(2,1)S(1)}, s32[8,512]{1,0:T(8,128)S(1)}) custom-call(s32[2]{0:T(128)S(1)} %pad_add_fusion.where, bf16[4,8,24,128]{3,2,1,0:T(8,128)(2,1)S(1)} %bitcast.21, bf16[256,2048]{1,0:T(8,128)(2,1)S(1)} %bitcast.13, bf16[256,2048]{1,0:T(8,128)(2,1)S(1)} %bitcast.17), custom_call_target="tpu_custom_call" | custom-call | tf_op jit(solution)/shard_map/pallas_call | solution.py:318
  46.8 0.0 copy-start.2
  46.8 7.1 %all-to-all-start.2 = ((bf16[64,8,128]{2,1,0:T(8,128)(2,1)}), bf16[64,8,128]{2,1,0:T(8,128)(2,1)S(1)}, u32[]{:S(2)}, u32[]{:S(2)}) async-start(bf16[64,8,128]{2,1,0:T(8,128)(2,1)} %bitcast.7), calls=%async_computation.2 | async-start | bytes 262144 | tf_op jit(solution)/shard_map/all_to_all | solution.py:332
  53.9 0.0 copy-done.4
  53.9 0.0 copy-done.7
  53.9 0.0 copy-done.10
  53.9 1.2 shard_map.89
  55.1 10.1 %all-to-all-done.2.got = bf16[64,8,128]{2,1,0:T(8,128)(2,1)S(1)} async-done(((bf16[64,8,128]{2,1,0:T(8,128)(2,1)}), bf16[64,8,128]{2,1,0:T(8,128)(2,1)S(1)}, u32[]{:S(2)}, u32[]{:S(2)}) %all-to-all-start.2) | async-done | bytes 131104 | tf_op jit(solution)/shard_map/all_to_all | solution.py:332
  65.2 0.7 shard_map.90
  65.9 7.4 %all_to_all.56.got = bf16[8,8,128]{2,1,0:T(8,128)(2,1)S(1)} all-to-all(bf16[8,8,128]{2,1,0:T(8,128)(2,1)S(1)} %shard_map.90), channel_id=1, replica_groups=mesh['x'=4,'y'=8,'c'=2,'z'=8] {'x','c'}, dimensions={0} | all-to-all | bytes 32768 | tf_op jit(solution)/shard_map/all_to_all | solution.py:332
  73.3 0.0 copy-done.2
  73.3 0.6 shard_map.91
  73.8 14.6 %all_to_all.57.got = bf16[64,8,128]{2,1,0:T(8,128)(2,1)S(1)} all-to-all(bf16[64,8,128]{2,1,0:T(8,128)(2,1)S(1)} %shard_map.91), channel_id=1, replica_groups=mesh['x'=4,'y'=8,'c'=2,'z'=8] {'x','c','z'}, dimensions={0} | all-to-all | bytes 262144 | tf_op jit(solution)/shard_map/all_to_all | solution.py:332
  88.4 10.3 %all_to_all.58.got = bf16[8,64,128]{2,1,0:T(8,128)(2,1)S(1)} all-to-all(bf16[8,64,128]{2,1,0:T(8,128)(2,1)S(1)} %shard_map.92), channel_id=1, replica_groups=mesh['x'=4,'y'=8,'c'=2,'z'=8] {'y'}, dimensions={0} | all-to-all | bytes 262144 | tf_op jit(solution)/shard_map/all_to_all | solution.py:332
  98.8 0.7 shard_map.93
  99.4 16.5 %all_to_all.59.got = bf16[64,8,128]{2,1,0:T(8,128)(2,1)S(1)} all-to-all(bf16[64,8,128]{2,1,0:T(8,128)(2,1)S(1)} %bitcast.25), channel_id=1, replica_groups=mesh['x'=4,'y'=8,'c'=2,'z'=8] {'x','c','z'}, dimensions={0} | all-to-all | bytes 262144 | tf_op jit(solution)/shard_map/all_to_all | solution.py:332
  115.9 0.8 shard_map.94
  116.7 16.1 %all_to_all.60.got = bf16[64,8,128]{2,1,0:T(8,128)(2,1)S(1)} all-to-all(bf16[64,8,128]{2,1,0:T(8,128)(2,1)S(1)} %bitcast.22), channel_id=1, replica_groups=mesh['x'=4,'y'=8,'c'=2,'z'=8] {'y','x','c'}, dimensions={0} | all-to-all | bytes 262144 | tf_op jit(solution)/shard_map/all_to_all | solution.py:332
  132.8 1.2 shard_map.95
  134.0 7.7 %all_to_all.61.got = bf16[8,16,128]{2,1,0:T(8,128)(2,1)S(1)} all-to-all(bf16[8,16,128]{2,1,0:T(8,128)(2,1)S(1)} %shard_map.95), channel_id=1, replica_groups=mesh['x'=4,'y'=8,'c'=2,'z'=8] {'x','c'}, dimensions={0} | all-to-all | bytes 65536 | tf_op jit(solution)/shard_map/all_to_all | solution.py:332
  141.7 0.5 shard_map.96
  142.3 12.1 %all_to_all.62 = bf16[32,16,128]{2,1,0:T(8,128)(2,1)S(1)} all-to-all(bf16[32,16,128]{2,1,0:T(8,128)(2,1)S(1)} %bitcast.23), channel_id=1, replica_groups=mesh['x'=4,'y'=8,'c'=2,'z'=8] {'x','z'}, dimensions={0} | all-to-all | bytes 262144 | tf_op jit(solution)/shard_map/all_to_all | solution.py:332
  154.4 0.0 copy-start.8
  154.4 1.2 shard_map.97
  155.6 5.3 %all-to-all-start.10 = ((bf16[16,8,128]{2,1,0:T(8,128)(2,1)}), bf16[16,8,128]{2,1,0:T(8,128)(2,1)S(1)}, u32[]{:S(2)}, u32[]{:S(2)}) async-start(bf16[16,8,128]{2,1,0:T(8,128)(2,1)} %shard_map.97), calls=%async_computation.10 | async-start | bytes 65536 | tf_op jit(solution)/shard_map/all_to_all | solution.py:332
  160.8 0.0 copy-done.8
  160.8 0.0 copy-start.6
  160.8 0.9 shard_map.99
  161.7 6.6 %all-to-all-done.10.got = bf16[16,8,128]{2,1,0:T(8,128)(2,1)S(1)} async-done(((bf16[16,8,128]{2,1,0:T(8,128)(2,1)}), bf16[16,8,128]{2,1,0:T(8,128)(2,1)S(1)}, u32[]{:S(2)}, u32[]{:S(2)}) %all-to-all-start.10) | async-done | bytes 32800 | tf_op jit(solution)/shard_map/all_to_all | solution.py:332
  168.3 0.0 copy-done.6
  168.3 1.1 shard_map.98
  (1 shorter events, 0.0 us)
Async XLA Ops:
  0.6 42.9 %copy-start = (bf16[1,256,2048]{2,1,0:T(8,128)(2,1)S(1)}, bf16[1,256,2048]{2,1,0:T(8,128)(2,1)}, u32[]{:S(2)}) copy-start(bf16[1,256,2048]{2,1,0:T(8,128)(2,1)} %param.10) | copy-start | bytes 3145732
  1.5 0.9 copy-start.3
  2.4 0.9 copy-start.5
  3.3 0.7 copy-start.9
  22.2 21.3 %all-to-all-start.1 = ((bf16[32,24,128]{2,1,0:T(8,128)(2,1)}), bf16[32,24,128]{2,1,0:T(8,128)(2,1)S(1)}, u32[]{:S(2)}, u32[]{:S(2)}) async-start(bf16[32,24,128]{2,1,0:T(8,128)(2,1)} %bitcast.3), calls=%async_computation.1 | async-start | bytes 393216 | tf_op jit(solution)/shard_map/all_to_all | solution.py:332
  43.6 1.2 copy-start.1
  44.8 9.1 %copy-start.4 = (bf16[128,1024]{1,0:T(8,128)(2,1)S(1)}, bf16[128,1024]{1,0:T(8,128)(2,1)}, u32[]{:S(2)}) copy-start(bf16[128,1024]{1,0:T(8,128)(2,1)} %constant.12.clone.base.forward) | copy-start | bytes 786436
  44.8 9.1 %copy-start.7 = (bf16[768,128]{1,0:T(8,128)(2,1)S(1)}, bf16[768,128]{1,0:T(8,128)(2,1)}, u32[]{:S(2)}) copy-start(bf16[768,128]{1,0:T(8,128)(2,1)} %constant.13.clone.inverse) | copy-start | bytes 589828
  44.8 9.1 %copy-start.10 = (s32[64]{0:T(128)S(1)}, s32[64]{0:T(128)}, u32[]{:S(2)}) copy-start(s32[64]{0:T(128)} %param.9) | copy-start | bytes 772
  46.8 26.5 %copy-start.2 = (bf16[1,256,2048]{2,1,0:T(8,128)(2,1)S(1)}, bf16[1,256,2048]{2,1,0:T(8,128)(2,1)}, u32[]{:S(2)}) copy-start(bf16[1,256,2048]{2,1,0:T(8,128)(2,1)} %param.11) | copy-start | bytes 3145732
  46.8 18.5 %all-to-all-start.2 = ((bf16[64,8,128]{2,1,0:T(8,128)(2,1)}), bf16[64,8,128]{2,1,0:T(8,128)(2,1)S(1)}, u32[]{:S(2)}, u32[]{:S(2)}) async-start(bf16[64,8,128]{2,1,0:T(8,128)(2,1)} %bitcast.7), calls=%async_computation.2 | async-start | bytes 262144 | tf_op jit(solution)/shard_map/all_to_all | solution.py:332
  154.4 6.4 %copy-start.8 = (s32[16,4]{0,1:T(4,128)S(1)}, s32[16,4]{0,1:T(4,128)}, u32[]{:S(2)}) copy-start(s32[16,4]{0,1:T(4,128)} %param.8) | copy-start | bytes 772
  155.6 12.7 %all-to-all-start.10 = ((bf16[16,8,128]{2,1,0:T(8,128)(2,1)}), bf16[16,8,128]{2,1,0:T(8,128)(2,1)S(1)}, u32[]{:S(2)}, u32[]{:S(2)}) async-start(bf16[16,8,128]{2,1,0:T(8,128)(2,1)} %shard_map.97), calls=%async_computation.10 | async-start | bytes 65536 | tf_op jit(solution)/shard_map/all_to_all | solution.py:332
  160.8 7.5 %copy-start.6 = (bf16[16,4,1024]{2,1,0:T(4,128)(2,1)S(1)}, bf16[16,4,1024]{2,1,0:T(4,128)(2,1)}, u32[]{:S(2)}) copy-start(bf16[16,4,1024]{2,1,0:T(4,128)(2,1)} %focus.3) | copy-start | bytes 393220

commit v3 on v2

v3 whole, which is shorter than its diff:
```python
import math

import jax
import jax.numpy as jnp
import numpy as np
from jax import lax
from jax.experimental import pallas as pl
from jax.experimental.pallas import tpu as pltpu
from jax.sharding import Mesh
from jax.sharding import PartitionSpec as P

FLO = 8
ITERS = 2
NX, NY, NC, NZ = 4, 8, 2, 8
NA, NG, NI = NY * NC, NX * NC, 4
NF, POINTS, NT = 64, 16, 1024
BLOCK, COLS = 256, 2048
LANES = 128
SPANS = ((128, 384), (640, 896), (0, 128), (896, 1024))
CUT = 512
KEPT = 768
ONSET_MID = 256
BF, F32, I32 = jnp.bfloat16, jnp.float32, jnp.int32
VMEM_LIMIT = 8 * 1024 * 1024


def base_tables():
    phase = (np.arange(NT)[None, :] * (FLO + np.arange(NF))[:, None]) % NT
    angle = phase.astype(np.float32) * np.float32(2.0 * math.pi / NT)
    rows = np.concatenate([np.cos(angle), -np.sin(angle)], axis=0)
    forward = (rows * np.float32(1.0 / math.sqrt(NT))).astype(BF)
    inverse = (rows * np.float32(math.sqrt(2.0 / NF))).astype(BF)
    inverse = np.concatenate([inverse[:, a:b] for a, b in SPANS], axis=1)
    wide = np.concatenate([forward[:NF], forward[NF:]], axis=1)
    return forward, wide, np.ascontiguousarray(inverse.T)


def iota(shape, dim):
    return lax.broadcasted_iota(I32, shape, dim)


def grid(rows, cols):
    return iota((rows, cols), 0), iota((rows, cols), 1)


def hot(mask):
    return jnp.where(mask, jnp.float32(1), jnp.float32(0)).astype(BF)


def nn(a, b):
    return lax.dot_general(a, b, (((1,), (0,)), ((), ())), preferred_element_type=F32)


def nt(a, b):
    return lax.dot_general(a, b, (((1,), (1,)), ((), ())), preferred_element_type=F32)


def two_terms(value):
    high = value.astype(BF)
    return high, (value - high.astype(F32)).astype(BF)


def slab_of_bin(bins):
    row, _ = grid(NF, NF)
    return hot(row == bins)


def fetch(pairs, sems):
    copies = [pltpu.make_async_copy(src, dst, sems.at[n]) for n, (src, dst) in enumerate(pairs)]
    for copy in copies:
        copy.start()
    return copies


def start_kernel(bins_in, onset_in, focus_in, base_in, out, bins, onset, focus, base, flat, sems):
    copies = fetch([(bins_in, bins), (onset_in, onset), (focus_in, focus), (base_in, base)], sems)
    copies[0].wait()
    m, j = grid(8 * NA, NF)
    place = hot(((m & 7) < NX) & (j == ((m & 7) << 4) + (m >> 3)))
    order = nt(place, slab_of_bin(bins[...])).astype(BF)
    copies[1].wait()
    p, lane = grid(POINTS, LANES)
    spread = hot((((lane >> 2) & 15) == p) & ((lane >> 6) == (p >> 3)))
    marks = nn((onset[...] - ONSET_MID).astype(F32).astype(BF), spread)
    i, lane = grid(NI, LANES)
    marks = jnp.where((lane & 3) == i, marks, 0.0).sum(axis=0, keepdims=True)
    copies[2].wait()
    for p in range(POINTS):
        flat[NI * p : NI * (p + 1), :] = focus[p].astype(F32)
    rows = flat[...].astype(BF)
    none = jnp.zeros_like(rows)
    copies[3].wait()
    spec = nt(base[:, :NT], jnp.concatenate([rows, none], axis=0))
    spec = spec + nt(base[:, NT:], jnp.concatenate([none, rows], axis=0))
    sent = nn(order, spec.astype(BF))
    sent = jnp.where((iota((8 * NA, LANES), 0) & 7) == NX, marks, sent)
    out[...] = sent.reshape(NA, 8, LANES).astype(BF)


def tables_kernel(
    where, bins_in, forward_in, inverse_in, re_in, im_in, inv, own_inv, turned_inv, fwd, own_fwd, fixed, own_fixed, re, im,
    bins, forward, inverse, sems,
):
    pairs = [(bins_in, bins), (forward_in, forward), (inverse_in, inverse), (re_in, re), (im_in, im)]
    copies = fetch(pairs, sems)
    for copy in copies[:3]:
        copy.wait()
    x, y, c = where[0], where[1], where[2]
    holds = slab_of_bin(bins[...])
    j, k = grid(NF, LANES)
    arrival = hot(j == ((k >> 5) << 4) + (k & 15))
    order = nn(holds, arrival)
    _, k = grid(NF, LANES)
    part = (k >> 4) & 1
    order = jnp.concatenate([jnp.where(part == 0, order, 0.0), jnp.where(part == 1, order, 0.0)], axis=0)
    table = nn(inverse[...], order.astype(BF)).astype(BF)
    inv[...] = table
    k, n = grid(LANES, 2 * NA)
    mine = hot(k == 2 * NA * x + n)
    own_inv[...] = nn(table[:CUT], mine).astype(BF)
    k, n = grid(LANES, LANES)
    turn = hot(k == ((n >> 4) << 4) + ((n & 7) << 1) + ((n >> 3) & 1))
    turned_inv[...] = nn(table[:CUT], turn).astype(BF)
    m, j = grid(2 * NG, NF)
    slabs = hot(j == (((m & 7) >> 1) << 4) + (y << 1) + (m & 1))
    slabs = nt(slabs, holds)
    m, _ = grid(2 * NG, NF)
    pick = jnp.concatenate([jnp.where(m < NG, slabs, 0.0), jnp.where(m < NG, 0.0, slabs)], axis=1)
    picked = nn(pick.astype(BF), forward[...]).astype(BF)
    picked = jnp.concatenate([picked[:, a:b] for a, b in SPANS], axis=1)
    m, n = grid(2 * NX, 2 * NG)
    mine_rows = hot(n == ((m >> 2) << 3) + ((m & 3) << 1) + c)
    ours = nn(mine_rows, picked).astype(BF)
    fwd[...] = picked[:, :CUT]
    own_fwd[...] = ours[:, :CUT]
    all_fixed = nn(picked[:, CUT:], table[CUT:])
    for n, term in enumerate(two_terms(all_fixed)):
        fixed[n] = nn(term, mine).astype(BF)
    for n, term in enumerate(two_terms(nn(ours[:, CUT:], table[CUT:]))):
        own_fixed[n] = nn(term, turn).astype(BF)
    copies[3].wait()
    copies[4].wait()


def middle_kernel(got, out, rows):
    rows[...] = got[...].astype(F32).reshape(8 * NA, LANES)
    line = jnp.concatenate([rows[pl.ds(e, NA, stride=8), :] for e in range(NX + 1)], axis=1).astype(BF)
    m, a = grid(NA * NI, NA)
    spread = nn(hot((m >> 2) == a), line)
    m, lane = grid(NA * NI, LANES)
    stacked = []
    for e in range(NX + 1):
        piece = spread[:, LANES * e : LANES * (e + 1)]
        for part in range(2):
            fits = ((lane & 3) == (m & 3)) & ((lane >> 6) == part)
            stacked.append(jnp.where(fits, piece, 0.0))
    stacked = jnp.concatenate(stacked, axis=0).astype(BF)
    p, lane = grid(POINTS, LANES)
    turned = nt(hot(((lane >> 2) & 15) == p), stacked)
    marks = turned[:8, LANES * NX :] + turned[8:, LANES * NX :]
    for x in range(NX):
        message = jnp.concatenate([turned[:, LANES * x : LANES * (x + 1)], marks], axis=0).astype(BF)
        for z in range(NZ):
            out[x, z] = message


def swap(a, b):
    low = iota(a.shape, 1) < LANES // 2
    return (
        jnp.where(low, a, pltpu.roll(b, LANES // 2, 1)),
        jnp.where(low, pltpu.roll(a, LANES // 2, 1), b),
    )


def convolve(src, mat_re, mat_im, out):
    a = nt(src, mat_re[...])
    b = nt(src, mat_im[...])
    parts = (a[:POINTS] - b[POINTS:], a[POINTS:] + b[:POINTS])
    for c in range(NC):
        at = slice(8 * c, 8 * (c + 1))
        slabs = [part[at, LANES * half : LANES * (half + 1)] for part in parts for half in range(2)]
        message = jnp.concatenate(slabs, axis=0).astype(BF)
        for y in range(NY):
            out[y, c] = message


def first_conv_kernel(where, got, mat_re, mat_im, out, src, marks, rows):
    height = POINTS + 8
    rows[...] = got[...].astype(F32).reshape(NX * NZ * height, LANES)
    for z in range(NZ):
        for half in range(2):
            a = rows[pl.ds((2 * half * NZ + z) * height, POINTS), :]
            b = rows[pl.ds(((2 * half + 1) * NZ + z) * height, POINTS), :]
            at = LANES * (2 * z + half)
            re, im = swap(a, b)
            src[:POINTS, at : at + LANES] = re.astype(BF)
            src[POINTS:, at : at + LANES] = im.astype(BF)
    for half in range(2):
        at = (2 * half * NZ + where[3]) * height + POINTS
        a = rows[pl.ds(pl.multiple_of(at, 8), 8), :]
        b = rows[pl.ds(pl.multiple_of(at + NZ * height, 8), 8), :]
        for h, block in enumerate(swap(a, b)):
            marks[8 * h : 8 * (h + 1), LANES * half : LANES * (half + 1)] = block.astype(I32) + ONSET_MID
    convolve(src[...], mat_re, mat_im, out)


def next_conv_kernel(got, first, mat_re, mat_im, out, rows, more):
    rows[...] = got[...].astype(F32).reshape(NX * NZ * 16, LANES)
    for x in range(NX):
        for z in range(NZ):
            for part in range(2):
                for half in range(2):
                    at = (x * NZ + z) * 16 + (2 * part + half) * 4
                    lanes = slice(LANES * (2 * z + half), LANES * (2 * z + half + 1))
                    more[POINTS * part + 4 * x : POINTS * part + 4 * (x + 1), lanes] = rows[at : at + 4, :]
    src = (first[...].astype(F32) + more[...]).astype(BF)
    convolve(src, mat_re, mat_im, out)


def window(spectra, marks, inv, fwd, fixed):
    t = iota((BLOCK, 1), 0)
    front = jnp.where(t + SPANS[0][0] < marks, nn(inv[:BLOCK], spectra), 0.0).astype(BF)
    back = jnp.where(t + SPANS[1][0] >= NT - marks, nn(inv[BLOCK:], spectra), 0.0).astype(BF)
    spec = nn(fwd[:, :BLOCK], front) + nn(fwd[:, BLOCK:], back)
    return spec + nn(fixed[0], spectra) + nn(fixed[1], spectra)


def points_window(marks, first, count, every, inv, fwd, fixed):
    mark = jnp.concatenate([marks[pl.ds(first + p, 1), :] for p in range(count)], axis=1)
    spec = window(jnp.concatenate(every, axis=1), mark, inv, fwd, fixed)
    return [spec[:, BLOCK * p : BLOCK * (p + 1)] for p in range(count)]


def window_slabs(where, got, inv, fwd, fixed, marks, rows, turn):
    rows[...] = got[...].astype(F32).reshape(NA * 32, LANES)
    every = []
    for p in range(8):
        parts = []
        for part in range(2):
            halves = [rows[pl.ds(16 * part + 8 * half + p, NA, stride=32), :] for half in range(2)]
            parts.append(jnp.concatenate(halves, axis=1))
        every.append(jnp.concatenate(parts, axis=0).astype(BF))
    for p, spec in enumerate(points_window(marks, 8 * where[2], 8, every, inv, fwd, fixed)):
        for part in range(2):
            for half in range(2):
                at = 16 * part + 8 * half + p
                slab = spec[NG * part : NG * (part + 1), LANES * half : LANES * (half + 1)]
                turn[pl.ds(at, NG, stride=32), :] = slab
    return every, turn[...].reshape(NG, 32, LANES)


def time_kernel(where, got, inv, fwd, fixed, marks, out, rows, turn):
    out[...] = window_slabs(where, got, inv, fwd, fixed, marks, rows, turn)[1].astype(BF)


def last_time_kernel(where, got, inv, fwd, fixed, marks, out, rows, turn, tail):
    every, message = window_slabs(where, got, inv, fwd, fixed, marks, rows, turn)
    m, r = grid(NG * NI, BLOCK)
    own = hot(r == ((m >> 3) << 6) + (where[1] << 3) + (((m >> 2) & 1) << 2) + (m & 3))
    taken = [nt(own, spectra) for spectra in every]
    taken = jnp.concatenate(taken, axis=0).astype(BF)
    n, k = grid(2 * NA, LANES)
    taken = nn(taken, hot(k == 2 * NA * where[0] + n))
    for p in range(8):
        for g in range(NG):
            at = NG * NI * p + NI * g
            tail[32 * g + NI * p : 32 * g + NI * (p + 1), :] = taken[at : at + NI]
    own = tail[...].reshape(NG, 32, LANES)
    out[...] = jnp.concatenate([message, own], axis=1).astype(BF)


def time_copies_kernel(where, got, inv, fwd, fixed, marks, out, rows, turn):
    rows[...] = got[...].astype(F32).reshape(NF * 16, LANES)
    every = []
    for p in range(4):
        parts = []
        for x in range(NX):
            for part in range(2):
                at = [16 * x + 8 * part + 4 * half + p for half in range(2)]
                halves = [rows[pl.ds(n, NA, stride=16 * NX), :] for n in at]
                parts.append(jnp.concatenate(halves, axis=1))
        every.append(jnp.concatenate(parts, axis=0).astype(BF))
    for p, spec in enumerate(points_window(marks, 4 * where[0], 4, every, inv, fwd, fixed)):
        for part in range(2):
            for half in range(2):
                slab = spec[NX * part : NX * (part + 1), LANES * half : LANES * (half + 1)]
                turn[pl.ds(8 * part + 4 * half + p, NX, stride=16), :] = slab
    message = turn[...].reshape(NX, 16, LANES).astype(BF)
    for z in range(NZ):
        out[:, z] = message


def correlate(got, mat_re, mat_im):
    parts = []
    for part in range(2):
        halves = []
        for half in range(2):
            at = 8 * (2 * part + half)
            both = [sum(got[NC * x + c].astype(F32)[at : at + 8] for x in range(NX)) for c in range(NC)]
            halves.append(jnp.concatenate(both, axis=0))
        parts.append(jnp.concatenate(halves, axis=1))
    straight = jnp.concatenate(parts, axis=0).astype(BF)
    turned = jnp.concatenate([parts[1], -parts[0]], axis=0).astype(BF)
    for z in range(NZ):
        at = slice(BLOCK * z, BLOCK * (z + 1))
        yield z, nn(straight, mat_re[:, at]) + nn(turned, mat_im[:, at])


def corr_kernel(got, mat_re, mat_im, out, turn):
    for z, block in correlate(got, mat_re, mat_im):
        for x in range(NX):
            for part in range(2):
                for half in range(2):
                    at = (x * NZ + z) * 16 + (2 * part + half) * 4
                    row = POINTS * part + 4 * x
                    turn[at : at + 4, :] = block[row : row + 4, LANES * half : LANES * (half + 1)]
    out[...] = turn[...].reshape(NX * NZ, 16, LANES).astype(BF)


def last_corr_kernel(got, mat_re, mat_im, out):
    for z, block in correlate(got, mat_re, mat_im):
        for half in range(2):
            at = slice(LANES * half, LANES * (half + 1))
            a, b = swap(block[:POINTS, at], block[POINTS:, at])
            out[2 * half, z] = a.astype(BF)
            out[2 * half + 1, z] = b.astype(BF)


def sum_kernel(got, out):
    total = got[...].astype(F32).reshape(NX, NZ, 16, LANES).sum(axis=1)
    total = total.reshape(NX * 16, LANES).astype(BF)
    for y in range(NY):
        out[y] = total


def last_sum_kernel(got, out):
    total = got[...].astype(F32).sum(axis=1)
    turned = jnp.concatenate([total[x].T for x in range(NX)], axis=0).astype(BF)
    p, lane = grid(POINTS, LANES)
    turned = nn(turned, hot(((lane >> 2) & 15) == p))
    m, lane = grid(NX * LANES, LANES)
    turned = jnp.where(((lane & 3) == (m & 3)) & ((lane >> 6) == ((m >> 6) & 1)), turned, 0.0).astype(BF)
    m, n = grid(8 * NA, NX * LANES)
    sent = nn(hot(((m & 7) == (n >> 7)) & ((m >> 3) == ((n >> 2) & 15))), turned)
    out[...] = sent.reshape(NA, 8, LANES).astype(BF)


def keep_own(trace, onset, p):
    t = iota((NI, BLOCK), 1)
    mark = onset[:, p : p + 1]
    front = jnp.where(t + SPANS[0][0] < mark, trace[:, :BLOCK], 0.0)
    back = jnp.where(t + SPANS[1][0] >= NT - mark, trace[:, BLOCK:CUT], 0.0)
    return front, back, trace[:, CUT : CUT + LANES], trace[:, CUT + LANES :]


def minus_kernel(got, inv, onset, out):
    own = [sum(got[NC * x + c].astype(F32)[32:] for x in range(NX)) for c in range(NC)]
    own = jnp.concatenate(own, axis=0).astype(BF)
    trace = nt(own, inv[...])
    for p in range(POINTS):
        for (a, b), piece in zip(SPANS, keep_own(trace[NI * p : NI * (p + 1)], onset, p)):
            out[p, :, a:b] = piece.astype(BF)
        out[p, :, 384:640] = jnp.zeros((NI, BLOCK), BF)


def plus_kernel(got, inv, onset, focus, out):
    rows = got[...].astype(F32).reshape(8 * NA, LANES).T.astype(BF)
    m, k = grid(8 * NA, LANES)
    spectra = jnp.zeros((POINTS * NI, LANES), F32)
    for part in range(2):
        place = hot(((m & 7) < NX) & (k == ((m & 7) << 5) + 16 * part + (m >> 3)))
        spectra = spectra + nn(rows[NF * part : NF * (part + 1)], place)
    trace = nt(spectra.astype(BF), inv[...])
    for p in range(POINTS):
        for (a, b), piece in zip(SPANS, keep_own(trace[NI * p : NI * (p + 1)], onset, p)):
            out[p, :, a:b] = (focus[p, :, a:b].astype(F32) + piece).astype(BF)
        out[p, :, 384:640] = focus[p, :, 384:640]


def call(kernel, outs, scratch=(), scalars=0, far=0, copies=0):
    single = not isinstance(outs, list)
    shapes = [jax.ShapeDtypeStruct(shape, dtype) for shape, dtype in ([outs] if single else outs)]

    def run(*args):
        spaces = [pltpu.SMEM] * scalars + [pltpu.HBM] * far + [pltpu.VMEM] * (len(args) - scalars - far)
        args = [
            pltpu.with_memory_space_constraint(arg, pltpu.HBM) if space is pltpu.HBM else arg
            for arg, space in zip(args, spaces)
        ]
        got = pl.pallas_call(
            kernel,
            out_shape=shapes,
            in_specs=[pl.BlockSpec(memory_space=space) for space in spaces],
            out_specs=[pl.BlockSpec(memory_space=pltpu.VMEM)] * len(shapes),
            scratch_shapes=[pltpu.VMEM(shape, dtype) for shape, dtype in scratch]
            + [pltpu.SemaphoreType.DMA((copies,))] * (copies > 0),
            compiler_params=pltpu.CompilerParams(vmem_limit_bytes=VMEM_LIMIT),
        )(*args)
        return got[0] if single else got

    return run


def exchange(values, axes):
    return lax.all_to_all(values, axes, 0, 0, tiled=True)


def shards(focus_start, onset, bins, refl_real, refl_imag):
    mats = (refl_real[0], refl_imag[0])
    where = jnp.stack([lax.axis_index(axis) for axis in ("x", "y", "c", "z")]).astype(I32)
    bins = bins.reshape(1, NF)
    onset = onset.T
    forward, wide, inverse = base_tables()
    own = (POINTS, NI, NT)

    scratch = [((1, NF), I32), ((NI, POINTS), I32), (own, BF), ((NF, 2 * NT), BF), ((POINTS * NI, NT), F32)]
    run = call(start_kernel, ((NA, 8, LANES), BF), scratch, far=4, copies=4)
    got = exchange(run(bins, onset, focus_start, wide), ("y", "c"))
    send = call(middle_kernel, ((NX, NZ, POINTS + 8, LANES), BF), [((8 * NA, LANES), F32)])(got)
    outs = [((KEPT, LANES), BF), ((CUT, 2 * NA), BF), ((CUT, LANES), BF), ((2 * NG, CUT), BF), ((2 * NX, CUT), BF)]
    outs += [((2, 2 * NG, 2 * NA), BF), ((2, 2 * NX, LANES), BF), ((BLOCK, COLS), BF), ((BLOCK, COLS), BF)]
    scratch = [((1, NF), I32), ((2 * NF, NT), BF), ((KEPT, LANES), BF)]
    run = call(tables_kernel, outs, scratch, scalars=1, far=5, copies=5)
    inv, own_inv, turned_inv, fwd, own_fwd, fixed, own_fixed, *mats = run(where, bins, forward, inverse, *mats)
    got = exchange(send.reshape(NX * NZ, POINTS + 8, LANES), ("x", "z"))
    outs = [((NY, NC, 32, LANES), BF), ((2 * POINTS, COLS), BF), ((POINTS, BLOCK), I32)]
    scratch = [((NX * NZ * (POINTS + 8), LANES), F32)]
    send, first, marks = call(first_conv_kernel, outs, scratch, scalars=1)(where, got, *mats)
    for step in range(ITERS):
        got = exchange(send.reshape(NA, 32, LANES), ("y", "c"))
        scratch = [((NA * 32, LANES), F32), ((NG * 32, LANES), F32)]
        tables = (own_inv, fwd, fixed, marks)
        if step == ITERS - 1:
            scratch = scratch + [((NG * 32, LANES), F32)]
            send = call(last_time_kernel, ((NG, 64, LANES), BF), scratch, scalars=1)(where, got, *tables)
            got = exchange(send, ("x", "c"))
            focus_minus = call(minus_kernel, (own, BF))(got, inv, onset)
            break
        send = call(time_kernel, ((NG, 32, LANES), BF), scratch, scalars=1)(where, got, *tables)
        got = exchange(send, ("x", "c"))
        send = call(corr_kernel, ((NX * NZ, 16, LANES), BF), [((NX * NZ * 16, LANES), F32)])(got, *mats)
        got = exchange(send, ("x", "z"))
        send = call(sum_kernel, ((NY, NX * 16, LANES), BF))(got)
        got = lax.all_gather(exchange(send, "y"), "c")
        scratch = [((NF * 16, LANES), F32), ((NX * 16, LANES), F32)]
        run = call(time_copies_kernel, ((NX, NZ, 16, LANES), BF), scratch, scalars=1)
        send = run(where, got, turned_inv, own_fwd, own_fixed, marks)
        got = exchange(send.reshape(NX * NZ, 16, LANES), ("x", "z"))
        scratch = [((NX * NZ * 16, LANES), F32), ((2 * POINTS, COLS), F32)]
        send = call(next_conv_kernel, ((NY, NC, 32, LANES), BF), scratch)(got, first, *mats)
    send = call(last_corr_kernel, ((NX, NZ, POINTS, LANES), BF))(got, *mats)
    got = exchange(send.reshape(NX * NZ, POINTS, LANES), ("x", "z")).reshape(NX, NZ, POINTS, LANES)
    send = call(last_sum_kernel, ((NA, 8, LANES), BF))(got)
    got = exchange(send, ("y", "c"))
    focus_plus = call(plus_kernel, (own, BF))(got, inv, onset, focus_start)
    return (focus_plus, focus_minus)


def solution(mesh):
    fine = Mesh(mesh.devices.reshape(NX, NY, NC, NZ), ("x", "y", "c", "z"))
    receivers = ("z", "x", "y", "c")
    slabs = ("x", "y", "c")
    return jax.shard_map(
        shards,
        mesh=fine,
        in_specs=(
            P(None, receivers, None),
            P(None, receivers),
            P(),
            P(slabs, "z", None),
            P(slabs, "z", None),
        ),
        out_specs=(P(None, receivers, None), P(None, receivers, None)),
        check_vma=False,
    )
```

time: 170 us -> 161 us (0.947)
  waiting for transfers between devices: 26 us -> 13.3 us
  blocking collectives: 101 us -> 113 us
  starting transfers between devices: 24.3 us -> 17.5 us
  local copies, waits for them, and re-layouts: 4.61 us -> 0.01 us
  Pallas kernels: 12.2 us -> 16.1 us
    all_to_all x3 -> x2, waiting for transfers between devices: 26 us -> 13.3 us  [exchange(): return lax.all_to_all(values, axes, 0, 0, tiled=True)]
    all_to_all x3 -> x2, starting transfers between devices: 24.3 us -> 17.5 us  [exchange(): return lax.all_to_all(values, axes, 0, 0, tiled=True)]
    all_to_all x8 -> x9, blocking collectives: 101 us -> 108 us  [exchange(): return lax.all_to_all(values, axes, 0, 0, tiled=True)]
    all_gather x0 -> x1, blocking collectives: none -> 4.84 us  [shards(): got = lax.all_gather(exchange(send, 'y'), 'c')]
    unnamed x23 -> x4, local copies, waits for them, and re-layouts: 4.61 us -> 0.01 us
    pallas_call x14, Pallas kernels: 12.2 us -> 16.1 us  [run(): pl.pallas_call(kernel, out_shape=shapes, in_specs=[pl.BlockSpec(memory_sp...]
  transfers between devices with their start and end apart: 3 -> 2, of which waited for: 3 -> 2; matrix products, arithmetic and copies ran while one was open for 0% -> 0% of each run, Pallas kernels for 1% -> 2%
where the time goes in v3:
time: 161 us; the launch traced here: 160 us
  blocking collectives  113 us (70%)
  starting transfers between devices  17.5 us (11%)
  Pallas kernels  16.1 us (10%)
  waiting for transfers between devices  13.3 us (8%)
    all_to_all x9, blocking collectives, exchange(): return lax.all_to_all(values, axes, 0, 0, tiled=True)  108 us
    all_to_all x2, starting transfers between devices, exchange(): return lax.all_to_all(values, axes, 0, 0, tiled=True)  17.5 us
    pallas_call x14, Pallas kernels, run(): pl.pallas_call(kernel, out_shape=shapes, in_specs=[pl.BlockSpec(memory_sp...  16.1 us
    all_to_all x2, waiting for transfers between devices, exchange(): return lax.all_to_all(values, axes, 0, 0, tiled=True)  13.3 us
    all_gather x1, blocking collectives, shards(): got = lax.all_gather(exchange(send, 'y'), 'c')  4.84 us
  transfers between devices with their start and end apart: 2, of which 2 were waited for; matrix products, arithmetic and copies ran while one was open for 0% of the time, Pallas kernels for 2%

profile of v3, /device:TPU:1, one launch (start us, length us, event | category | flops | bytes accessed | tf_op | source)
XLA Modules:
  0.0 160.5 jit_solution(15017694931645980917)
XLA Ops:
  0.6 1.5 shard_map.95
  2.1 16.7 %all_to_all.55.got = bf16[16,8,128]{2,1,0:T(8,128)(2,1)S(1)} all-to-all(bf16[16,8,128]{2,1,0:T(8,128)(2,1)S(1)} %shard_map.95), channel_id=1, replica_groups=mesh['x'=4,'y'=8,'c'=2,'z'=8] {'y','c'}, dimensions={0} | all-to-all | bytes 65536 | tf_op jit(solution)/shard_map/all_to_all | solution.py:405
  18.9 1.0 shard_map.96
  19.9 11.9 %all-to-all-start.1 = ((bf16[32,24,128]{2,1,0:T(8,128)(2,1)}), bf16[32,24,128]{2,1,0:T(8,128)(2,1)S(1)}, u32[]{:S(2)}, u32[]{:S(2)}) async-start(bf16[32,24,128]{2,1,0:T(8,128)(2,1)} %bitcast.6), calls=%async_computation.1 | async-start | bytes 393216 | tf_op jit(solution)/shard_map/all_to_all | solution.py:405
  31.8 0.1 pad_add_fusion.where
  31.9 2.6 %shard_map.97 = (bf16[768,128]{1,0:T(8,128)(2,1)S(1)}, bf16[512,32]{1,0:T(8,128)(2,1)S(1)}, bf16[512,128]{1,0:T(8,128)(2,1)S(1)}, bf16[16,512]{1,0:T(8,128)(2,1)...) custom-call(s32[4]{0:T(128)S(1)} %pad_add_fusion.where, ...), custom_call_target="tpu_custom_call" | custom-call | tf_op jit(solution)/shard_map/pallas_call | solution.py:390
  34.5 6.7 %all-to-all-done.1.got = bf16[32,24,128]{2,1,0:T(8,128)(2,1)S(1)} async-done(((bf16[32,24,128]{2,1,0:T(8,128)(2,1)}), bf16[32,24,128]{2,1,0:T(8,128)(2,1)S(1)}, u32[]{:S(2)}, u32[]{:S(2)}) %all-to-all-start.1) | async-done | bytes 196640 | tf_op jit(solution)/shard_map/all_to_all | solution.py:405
  41.2 1.3 shard_map.98
  42.5 14.5 %all_to_all.56.got = bf16[16,32,128]{2,1,0:T(8,128)(2,1)S(1)} all-to-all(bf16[16,32,128]{2,1,0:T(8,128)(2,1)S(1)} %bitcast.20), channel_id=1, replica_groups=mesh['x'=4,'y'=8,'c'=2,'z'=8] {'y','c'}, dimensions={0} | all-to-all | bytes 262144 | tf_op jit(solution)/shard_map/all_to_all | solution.py:405
  57.1 1.7 %shard_map.99 = bf16[8,32,128]{2,1,0:T(8,128)(2,1)S(1)} custom-call(s32[4]{0:T(128)S(1)} %pad_add_fusion.where, bf16[16,32,128]{2,1,0:T(8,128)(2,1)S(1)} %all_to_all.56.got, bf16[512,32]{1,0:T(8,128)(2,1)S(1)} %get-tuple-element.17.inv, bf16[16,512]{1,0:T(8,128)(2,1)S(1)} %get-tuple-element.18.fwd, bf16[2,16,32]{2,1,0:T(8,128)(2,1)S(1)} %get-tuple-element.19.fixed, ...), custom_call_target="tpu_custom_call" | custom-call | tf_op jit(solution)/shard_map/pallas_call | solution.py:390
  58.7 7.6 %all_to_all.57.got = bf16[8,32,128]{2,1,0:T(8,128)(2,1)S(1)} all-to-all(bf16[8,32,128]{2,1,0:T(8,128)(2,1)S(1)} %shard_map.99), channel_id=1, replica_groups=mesh['x'=4,'y'=8,'c'=2,'z'=8] {'x','c'}, dimensions={0} | all-to-all | bytes 131072 | tf_op jit(solution)/shard_map/all_to_all | solution.py:405
  66.4 0.5 shard_map.100
  66.9 12.3 %all_to_all.58.got = bf16[32,16,128]{2,1,0:T(8,128)(2,1)S(1)} all-to-all(bf16[32,16,128]{2,1,0:T(8,128)(2,1)S(1)} %shard_map.100), channel_id=1, replica_groups=mesh['x'=4,'y'=8,'c'=2,'z'=8] {'x','z'}, dimensions={0} | all-to-all | bytes 262144 | tf_op jit(solution)/shard_map/all_to_all | solution.py:405
  79.2 10.4 %all_to_all.59 = bf16[8,64,128]{2,1,0:T(8,128)(2,1)S(1)} all-to-all(bf16[8,64,128]{2,1,0:T(8,128)(2,1)S(1)} %shard_map.101), channel_id=1, replica_groups=mesh['x'=4,'y'=8,'c'=2,'z'=8] {'y'}, dimensions={0} | all-to-all | bytes 262144 | tf_op jit(solution)/shard_map/all_to_all | solution.py:405
  89.6 4.8 %all-gather = bf16[16,64,128]{2,1,0:T(8,128)(2,1)S(1)} all-gather(bf16[8,64,128]{2,1,0:T(8,128)(2,1)S(1)} %all_to_all.59), channel_id=2, replica_groups=mesh['x'=4,'y'=8,'c'=2,'z'=8] {'c'}, dimensions={0}, use_global_device_ids=true | all-gather | bytes 393216 | tf_op jit(solution)/shard_map/all_gather | solution.py:444
  94.5 1.5 shard_map.102
  96.0 12.5 %all_to_all.60.got = bf16[32,16,128]{2,1,0:T(8,128)(2,1)S(1)} all-to-all(bf16[32,16,128]{2,1,0:T(8,128)(2,1)S(1)} %bitcast.16), channel_id=1, replica_groups=mesh['x'=4,'y'=8,'c'=2,'z'=8] {'x','z'}, dimensions={0} | all-to-all | bytes 262144 | tf_op jit(solution)/shard_map/all_to_all | solution.py:405
  108.4 0.8 shard_map.103
  109.2 13.7 %all_to_all.61.got = bf16[16,32,128]{2,1,0:T(8,128)(2,1)S(1)} all-to-all(bf16[16,32,128]{2,1,0:T(8,128)(2,1)S(1)} %bitcast.17), channel_id=1, replica_groups=mesh['x'=4,'y'=8,'c'=2,'z'=8] {'y','c'}, dimensions={0} | all-to-all | bytes 262144 | tf_op jit(solution)/shard_map/all_to_all | solution.py:405
  123.0 1.8 %shard_map.104 = bf16[8,64,128]{2,1,0:T(8,128)(2,1)S(1)} custom-call(s32[4]{0:T(128)S(1)} %pad_add_fusion.where, bf16[16,32,128]{2,1,0:T(8,128)(2,1)S(1)} %all_to_all.61.got, bf16[512,32]{1,0:T(8,128)(2,1)S(1)} %get-tuple-element.17.inv, bf16[16,512]{1,0:T(8,128)(2,1)S(1)} %get-tuple-element.18.fwd, bf16[2,16,32]{2,1,0:T(8,128)(2,1)S(1)} %get-tuple-element.19.fixed, ...), custom_call_target="tpu_custom_call" | custom-call | tf_op jit(solution)/shard_map/pallas_call | solution.py:390
  124.7 7.8 %all_to_all.62.got = bf16[8,64,128]{2,1,0:T(8,128)(2,1)S(1)} all-to-all(bf16[8,64,128]{2,1,0:T(8,128)(2,1)S(1)} %shard_map.104), channel_id=1, replica_groups=mesh['x'=4,'y'=8,'c'=2,'z'=8] {'x','c'}, dimensions={0} | all-to-all | bytes 262144 | tf_op jit(solution)/shard_map/all_to_all | solution.py:405
  132.6 0.5 shard_map.105
  133.1 12.2 %all_to_all.63 = bf16[32,16,128]{2,1,0:T(8,128)(2,1)S(1)} all-to-all(bf16[32,16,128]{2,1,0:T(8,128)(2,1)S(1)} %bitcast.18), channel_id=1, replica_groups=mesh['x'=4,'y'=8,'c'=2,'z'=8] {'x','z'}, dimensions={0} | all-to-all | bytes 262144 | tf_op jit(solution)/shard_map/all_to_all | solution.py:405
  145.3 0.0 copy-start.1
  145.3 1.1 shard_map.106
  146.4 5.5 %all-to-all-start.10 = ((bf16[16,8,128]{2,1,0:T(8,128)(2,1)}), bf16[16,8,128]{2,1,0:T(8,128)(2,1)S(1)}, u32[]{:S(2)}, u32[]{:S(2)}) async-start(bf16[16,8,128]{2,1,0:T(8,128)(2,1)} %shard_map.106), calls=%async_computation.10 | async-start | bytes 65536 | tf_op jit(solution)/shard_map/all_to_all | solution.py:405
  152.0 0.0 copy-done.1
  152.0 0.0 copy-start
  152.0 0.9 shard_map.108
  152.8 6.6 %all-to-all-done.10.got = bf16[16,8,128]{2,1,0:T(8,128)(2,1)S(1)} async-done(((bf16[16,8,128]{2,1,0:T(8,128)(2,1)}), bf16[16,8,128]{2,1,0:T(8,128)(2,1)S(1)}, u32[]{:S(2)}, u32[]{:S(2)}) %all-to-all-start.10) | async-done | bytes 32800 | tf_op jit(solution)/shard_map/all_to_all | solution.py:405
  159.4 0.0 copy-done
  159.4 1.1 shard_map.107
  (1 shorter events, 0.0 us)
Async XLA Ops:
  19.9 21.3 %all-to-all-start.1 = ((bf16[32,24,128]{2,1,0:T(8,128)(2,1)}), bf16[32,24,128]{2,1,0:T(8,128)(2,1)S(1)}, u32[]{:S(2)}, u32[]{:S(2)}) async-start(bf16[32,24,128]{2,1,0:T(8,128)(2,1)} %bitcast.6), calls=%async_computation.1 | async-start | bytes 393216 | tf_op jit(solution)/shard_map/all_to_all | solution.py:405
  145.3 6.6 %copy-start.1 = (s32[16,4]{0,1:T(4,128)S(1)}, s32[16,4]{0,1:T(4,128)}, u32[]{:S(2)}) copy-start(s32[16,4]{0,1:T(4,128)} %param.9) | copy-start | bytes 772
  146.4 13.0 %all-to-all-start.10 = ((bf16[16,8,128]{2,1,0:T(8,128)(2,1)}), bf16[16,8,128]{2,1,0:T(8,128)(2,1)S(1)}, u32[]{:S(2)}, u32[]{:S(2)}) async-start(bf16[16,8,128]{2,1,0:T(8,128)(2,1)} %shard_map.106), calls=%async_computation.10 | async-start | bytes 65536 | tf_op jit(solution)/shard_map/all_to_all | solution.py:405
  152.0 7.5 %copy-start = (bf16[16,4,1024]{2,1,0:T(4,128)(2,1)S(1)}, bf16[16,4,1024]{2,1,0:T(4,128)(2,1)}, u32[]{:S(2)}) copy-start(bf16[16,4,1024]{2,1,0:T(4,128)(2,1)} %focus.1) | copy-start | bytes 393220

commit v4 on v3

--- a/solution.py
+++ b/solution.py
@@ -98,51 +98,43 @@
 
 
 def tables_kernel(
-    where, bins_in, forward_in, inverse_in, re_in, im_in, inv, own_inv, turned_inv, fwd, own_fwd, fixed, own_fixed, re, im,
-    bins, forward, inverse, sems,
+    where, bins_in, onset_in, forward_in, inverse_in, re_in, im_in,
+    inv, own_inv, fwd, fixed, own_fixed, own_marks, re, im,
+    bins, onset, forward, inverse, sems,
 ):
-    pairs = [(bins_in, bins), (forward_in, forward), (inverse_in, inverse), (re_in, re), (im_in, im)]
+    pairs = [(bins_in, bins), (onset_in, onset), (forward_in, forward), (inverse_in, inverse), (re_in, re), (im_in, im)]
     copies = fetch(pairs, sems)
-    for copy in copies[:3]:
+    for copy in copies[:4]:
         copy.wait()
-    x, y, c = where[0], where[1], where[2]
     holds = slab_of_bin(bins[...])
     j, k = grid(NF, LANES)
-    arrival = hot(j == ((k >> 5) << 4) + (k & 15))
-    order = nn(holds, arrival)
-    _, k = grid(NF, LANES)
+    order = nn(holds, hot(j == ((k >> 5) << 4) + (k & 15)))
     part = (k >> 4) & 1
     order = jnp.concatenate([jnp.where(part == 0, order, 0.0), jnp.where(part == 1, order, 0.0)], axis=0)
     table = nn(inverse[...], order.astype(BF)).astype(BF)
     inv[...] = table
     k, n = grid(LANES, 2 * NA)
-    mine = hot(k == 2 * NA * x + n)
+    mine = hot(k == 2 * NA * where[0] + n)
     own_inv[...] = nn(table[:CUT], mine).astype(BF)
-    k, n = grid(LANES, LANES)
-    turn = hot(k == ((n >> 4) << 4) + ((n & 7) << 1) + ((n >> 3) & 1))
-    turned_inv[...] = nn(table[:CUT], turn).astype(BF)
     m, j = grid(2 * NG, NF)
-    slabs = hot(j == (((m & 7) >> 1) << 4) + (y << 1) + (m & 1))
-    slabs = nt(slabs, holds)
-    m, _ = grid(2 * NG, NF)
+    slabs = nt(hot(j == (((m & 7) >> 1) << 4) + (where[1] << 1) + (m & 1)), holds)
     pick = jnp.concatenate([jnp.where(m < NG, slabs, 0.0), jnp.where(m < NG, 0.0, slabs)], axis=1)
     picked = nn(pick.astype(BF), forward[...]).astype(BF)
     picked = jnp.concatenate([picked[:, a:b] for a, b in SPANS], axis=1)
-    m, n = grid(2 * NX, 2 * NG)
-    mine_rows = hot(n == ((m >> 2) << 3) + ((m & 3) << 1) + c)
-    ours = nn(mine_rows, picked).astype(BF)
     fwd[...] = picked[:, :CUT]
-    own_fwd[...] = ours[:, :CUT]
-    all_fixed = nn(picked[:, CUT:], table[CUT:])
-    for n, term in enumerate(two_terms(all_fixed)):
-        fixed[n] = nn(term, mine).astype(BF)
-    for n, term in enumerate(two_terms(nn(ours[:, CUT:], table[CUT:]))):
-        own_fixed[n] = nn(term, turn).astype(BF)
-    copies[3].wait()
+    for n, term in enumerate(two_terms(nn(picked[:, CUT:], table[CUT:]))):
+        fixed[n] = term
+        own_fixed[n] = nn(term, mine).astype(BF)
+    m, p = grid(POINTS * NI, POINTS)
+    marks = nt(hot((m >> 2) == p), (onset[...] - ONSET_MID).astype(F32).astype(BF))
+    m, i = grid(POINTS * NI, NI)
+    marks = jnp.where((m & 3) == i, marks, 0.0).sum(axis=1, keepdims=True)
+    own_marks[...] = jnp.broadcast_to(marks, (POINTS * NI, LANES)).astype(I32) + ONSET_MID
     copies[4].wait()
-
-
-def middle_kernel(got, out, rows):
+    copies[5].wait()
+
+
+def middle_kernel(got, _, out, rows):
     rows[...] = got[...].astype(F32).reshape(8 * NA, LANES)
     line = jnp.concatenate([rows[pl.ds(e, NA, stride=8), :] for e in range(NX + 1)], axis=1).astype(BF)
     m, a = grid(NA * NI, NA)
@@ -205,22 +197,22 @@
 
 
 def next_conv_kernel(got, first, mat_re, mat_im, out, rows, more):
-    rows[...] = got[...].astype(F32).reshape(NX * NZ * 16, LANES)
-    for x in range(NX):
-        for z in range(NZ):
+    rows[...] = got[...].astype(F32).reshape(NG * NZ * 8, LANES)
+    for z in range(NZ):
+        for p in range(2):
             for part in range(2):
                 for half in range(2):
-                    at = (x * NZ + z) * 16 + (2 * part + half) * 4
-                    lanes = slice(LANES * (2 * z + half), LANES * (2 * z + half + 1))
-                    more[POINTS * part + 4 * x : POINTS * part + 4 * (x + 1), lanes] = rows[at : at + 4, :]
-    src = (first[...].astype(F32) + more[...]).astype(BF)
+                    slab = rows[pl.ds(8 * z + 4 * p + 2 * part + half, NG, stride=8 * NZ), :]
+                    more[pl.ds(2 * POINTS * (2 * z + half) + POINTS * part + p, NG, stride=2), :] = slab
+    blocks = [more[2 * POINTS * n : 2 * POINTS * (n + 1), :] for n in range(COLS // LANES)]
+    src = (first[...].astype(F32) + jnp.concatenate(blocks, axis=1)).astype(BF)
     convolve(src, mat_re, mat_im, out)
 
 
 def window(spectra, marks, inv, fwd, fixed):
     t = iota((BLOCK, 1), 0)
     front = jnp.where(t + SPANS[0][0] < marks, nn(inv[:BLOCK], spectra), 0.0).astype(BF)
-    back = jnp.where(t + SPANS[1][0] >= NT - marks, nn(inv[BLOCK:], spectra), 0.0).astype(BF)
+    back = jnp.where(t + SPANS[1][0] >= NT - marks, nn(inv[BLOCK:CUT], spectra), 0.0).astype(BF)
     spec = nn(fwd[:, :BLOCK], front) + nn(fwd[:, BLOCK:], back)
     return spec + nn(fixed[0], spectra) + nn(fixed[1], spectra)
 
@@ -270,22 +262,23 @@
 
 
 def time_copies_kernel(where, got, inv, fwd, fixed, marks, out, rows, turn):
-    rows[...] = got[...].astype(F32).reshape(NF * 16, LANES)
+    rows[...] = got[...].astype(F32).reshape(NF * 8, LANES)
     every = []
-    for p in range(4):
+    for p in range(2):
         parts = []
         for x in range(NX):
             for part in range(2):
-                at = [16 * x + 8 * part + 4 * half + p for half in range(2)]
-                halves = [rows[pl.ds(n, NA, stride=16 * NX), :] for n in at]
+                at = [8 * x + 4 * p + 2 * part + half for half in range(2)]
+                halves = [rows[pl.ds(n, NA, stride=8 * NX), :] for n in at]
                 parts.append(jnp.concatenate(halves, axis=1))
         every.append(jnp.concatenate(parts, axis=0).astype(BF))
-    for p, spec in enumerate(points_window(marks, 4 * where[0], 4, every, inv, fwd, fixed)):
+    first = 4 * where[0] + 2 * where[2]
+    for p, spec in enumerate(points_window(marks, first, 2, every, inv, fwd, fixed)):
         for part in range(2):
             for half in range(2):
-                slab = spec[NX * part : NX * (part + 1), LANES * half : LANES * (half + 1)]
-                turn[pl.ds(8 * part + 4 * half + p, NX, stride=16), :] = slab
-    message = turn[...].reshape(NX, 16, LANES).astype(BF)
+                slab = spec[NG * part : NG * (part + 1), LANES * half : LANES * (half + 1)]
+                turn[pl.ds(4 * p + 2 * part + half, NG, stride=8), :] = slab
+    message = turn[...].reshape(NG, 8, LANES).astype(BF)
     for z in range(NZ):
         out[:, z] = message
 
@@ -311,9 +304,9 @@
         for x in range(NX):
             for part in range(2):
                 for half in range(2):
-                    at = (x * NZ + z) * 16 + (2 * part + half) * 4
+                    at = (x * NZ + z) * 16 + 2 * part + half
                     row = POINTS * part + 4 * x
-                    turn[at : at + 4, :] = block[row : row + 4, LANES * half : LANES * (half + 1)]
+                    turn[pl.ds(at, 4, stride=4), :] = block[row : row + 4, LANES * half : LANES * (half + 1)]
     out[...] = turn[...].reshape(NX * NZ, 16, LANES).astype(BF)
 
 
@@ -328,53 +321,51 @@
 
 def sum_kernel(got, out):
     total = got[...].astype(F32).reshape(NX, NZ, 16, LANES).sum(axis=1)
-    total = total.reshape(NX * 16, LANES).astype(BF)
-    for y in range(NY):
-        out[y] = total
+    for c in range(NC):
+        message = total[:, 8 * c : 8 * (c + 1)].reshape(NX * 8, LANES).astype(BF)
+        for y in range(NY):
+            out[y, c] = message
 
 
 def last_sum_kernel(got, out):
-    total = got[...].astype(F32).sum(axis=1)
-    turned = jnp.concatenate([total[x].T for x in range(NX)], axis=0).astype(BF)
-    p, lane = grid(POINTS, LANES)
-    turned = nn(turned, hot(((lane >> 2) & 15) == p))
-    m, lane = grid(NX * LANES, LANES)
-    turned = jnp.where(((lane & 3) == (m & 3)) & ((lane >> 6) == ((m >> 6) & 1)), turned, 0.0).astype(BF)
-    m, n = grid(8 * NA, NX * LANES)
-    sent = nn(hot(((m & 7) == (n >> 7)) & ((m >> 3) == ((n >> 2) & 15))), turned)
+    total = got[...].astype(F32).sum(axis=1).astype(BF)
+    total = jnp.concatenate([total[x] for x in range(NX)], axis=1)
+    m, p = grid(LANES, POINTS)
+    turned = nn(hot(((m >> 2) & 15) == p), total)
+    m, n = grid(LANES, NX * LANES)
+    turned = jnp.where(((n & 3) == (m & 3)) & (((n >> 6) & 1) == (m >> 6)), turned, 0.0).astype(BF)
+    sent = nt(hot(((m & 7) == (n >> 7)) & ((m >> 3) == ((n >> 2) & 15))), turned)
     out[...] = sent.reshape(NA, 8, LANES).astype(BF)
 
 
-def keep_own(trace, onset, p):
-    t = iota((NI, BLOCK), 1)
-    mark = onset[:, p : p + 1]
-    front = jnp.where(t + SPANS[0][0] < mark, trace[:, :BLOCK], 0.0)
-    back = jnp.where(t + SPANS[1][0] >= NT - mark, trace[:, BLOCK:CUT], 0.0)
-    return front, back, trace[:, CUT : CUT + LANES], trace[:, CUT + LANES :]
-
-
-def minus_kernel(got, inv, onset, out):
+def keep_own(spectra, inv, marks):
+    trace = nt(spectra, inv)
+    t = iota((POINTS * NI, LANES), 1)
+    pieces = [trace[:, LANES * n : LANES * (n + 1)] for n in range(KEPT // LANES)]
+    none = jnp.zeros_like(pieces[0])
+    front = [jnp.where(t + SPANS[0][0] + LANES * n < marks, pieces[n], 0.0) for n in range(2)]
+    back = [jnp.where(t + SPANS[1][0] + LANES * n >= NT - marks, pieces[2 + n], 0.0) for n in range(2)]
+    return jnp.concatenate([pieces[4], *front, none, none, *back, pieces[5]], axis=1)
+
+
+def minus_kernel(got, inv, marks, out):
     own = [sum(got[NC * x + c].astype(F32)[32:] for x in range(NX)) for c in range(NC)]
     own = jnp.concatenate(own, axis=0).astype(BF)
-    trace = nt(own, inv[...])
+    trace = keep_own(own, inv[...], marks[...])
     for p in range(POINTS):
-        for (a, b), piece in zip(SPANS, keep_own(trace[NI * p : NI * (p + 1)], onset, p)):
-            out[p, :, a:b] = piece.astype(BF)
-        out[p, :, 384:640] = jnp.zeros((NI, BLOCK), BF)
-
-
-def plus_kernel(got, inv, onset, focus, out):
+        out[p] = trace[NI * p : NI * (p + 1)].astype(BF)
+
+
+def plus_kernel(got, inv, marks, focus, out):
     rows = got[...].astype(F32).reshape(8 * NA, LANES).T.astype(BF)
     m, k = grid(8 * NA, LANES)
     spectra = jnp.zeros((POINTS * NI, LANES), F32)
     for part in range(2):
         place = hot(((m & 7) < NX) & (k == ((m & 7) << 5) + 16 * part + (m >> 3)))
         spectra = spectra + nn(rows[NF * part : NF * (part + 1)], place)
-    trace = nt(spectra.astype(BF), inv[...])
+    trace = keep_own(spectra.astype(BF), inv[...], marks[...])
     for p in range(POINTS):
-        for (a, b), piece in zip(SPANS, keep_own(trace[NI * p : NI * (p + 1)], onset, p)):
-            out[p, :, a:b] = (focus[p, :, a:b].astype(F32) + piece).astype(BF)
-        out[p, :, 384:640] = focus[p, :, 384:640]
+        out[p] = (focus[p].astype(F32) + trace[NI * p : NI * (p + 1)]).astype(BF)
 
 
 def call(kernel, outs, scratch=(), scalars=0, far=0, copies=0):
@@ -416,12 +407,12 @@
     scratch = [((1, NF), I32), ((NI, POINTS), I32), (own, BF), ((NF, 2 * NT), BF), ((POINTS * NI, NT), F32)]
     run = call(start_kernel, ((NA, 8, LANES), BF), scratch, far=4, copies=4)
     got = exchange(run(bins, onset, focus_start, wide), ("y", "c"))
-    send = call(middle_kernel, ((NX, NZ, POINTS + 8, LANES), BF), [((8 * NA, LANES), F32)])(got)
-    outs = [((KEPT, LANES), BF), ((CUT, 2 * NA), BF), ((CUT, LANES), BF), ((2 * NG, CUT), BF), ((2 * NX, CUT), BF)]
-    outs += [((2, 2 * NG, 2 * NA), BF), ((2, 2 * NX, LANES), BF), ((BLOCK, COLS), BF), ((BLOCK, COLS), BF)]
-    scratch = [((1, NF), I32), ((2 * NF, NT), BF), ((KEPT, LANES), BF)]
-    run = call(tables_kernel, outs, scratch, scalars=1, far=5, copies=5)
-    inv, own_inv, turned_inv, fwd, own_fwd, fixed, own_fixed, *mats = run(where, bins, forward, inverse, *mats)
+    outs = [((KEPT, LANES), BF), ((CUT, 2 * NA), BF), ((2 * NG, CUT), BF), ((2, 2 * NG, LANES), BF), ((2, 2 * NG, 2 * NA), BF)]
+    outs += [((POINTS * NI, LANES), I32), ((BLOCK, COLS), BF), ((BLOCK, COLS), BF)]
+    scratch = [((1, NF), I32), ((NI, POINTS), I32), ((2 * NF, NT), BF), ((KEPT, LANES), BF)]
+    run = call(tables_kernel, outs, scratch, scalars=1, far=6, copies=6)
+    inv, own_inv, fwd, fixed, own_fixed, own_marks, *mats = run(where, bins, onset, forward, inverse, *mats)
+    send = call(middle_kernel, ((NX, NZ, POINTS + 8, LANES), BF), [((8 * NA, LANES), F32)])(got, fwd)
     got = exchange(send.reshape(NX * NZ, POINTS + 8, LANES), ("x", "z"))
     outs = [((NY, NC, 32, LANES), BF), ((2 * POINTS, COLS), BF), ((POINTS, BLOCK), I32)]
     scratch = [((NX * NZ * (POINTS + 8), LANES), F32)]
@@ -429,30 +420,30 @@
     for step in range(ITERS):
         got = exchange(send.reshape(NA, 32, LANES), ("y", "c"))
         scratch = [((NA * 32, LANES), F32), ((NG * 32, LANES), F32)]
-        tables = (own_inv, fwd, fixed, marks)
+        tables = (own_inv, fwd, own_fixed, marks)
         if step == ITERS - 1:
             scratch = scratch + [((NG * 32, LANES), F32)]
             send = call(last_time_kernel, ((NG, 64, LANES), BF), scratch, scalars=1)(where, got, *tables)
             got = exchange(send, ("x", "c"))
-            focus_minus = call(minus_kernel, (own, BF))(got, inv, onset)
+            focus_minus = call(minus_kernel, (own, BF))(got, inv, own_marks)
             break
         send = call(time_kernel, ((NG, 32, LANES), BF), scratch, scalars=1)(where, got, *tables)
         got = exchange(send, ("x", "c"))
         send = call(corr_kernel, ((NX * NZ, 16, LANES), BF), [((NX * NZ * 16, LANES), F32)])(got, *mats)
         got = exchange(send, ("x", "z"))
-        send = call(sum_kernel, ((NY, NX * 16, LANES), BF))(got)
-        got = lax.all_gather(exchange(send, "y"), "c")
-        scratch = [((NF * 16, LANES), F32), ((NX * 16, LANES), F32)]
-        run = call(time_copies_kernel, ((NX, NZ, 16, LANES), BF), scratch, scalars=1)
-        send = run(where, got, turned_inv, own_fwd, own_fixed, marks)
-        got = exchange(send.reshape(NX * NZ, 16, LANES), ("x", "z"))
-        scratch = [((NX * NZ * 16, LANES), F32), ((2 * POINTS, COLS), F32)]
+        send = call(sum_kernel, ((NY, NC, NX * 8, LANES), BF))(got)
+        got = exchange(send.reshape(NA, NX * 8, LANES), ("y", "c"))
+        scratch = [((NF * 8, LANES), F32), ((NG * 8, LANES), F32)]
+        run = call(time_copies_kernel, ((NG, NZ, 8, LANES), BF), scratch, scalars=1)
+        send = run(where, got, inv, fwd, fixed, marks)
+        got = exchange(send.reshape(NG * NZ, 8, LANES), ("x", "c", "z"))
+        scratch = [((NG * NZ * 8, LANES), F32), ((2 * POINTS * COLS // LANES, LANES), F32)]
         send = call(next_conv_kernel, ((NY, NC, 32, LANES), BF), scratch)(got, first, *mats)
     send = call(last_corr_kernel, ((NX, NZ, POINTS, LANES), BF))(got, *mats)
     got = exchange(send.reshape(NX * NZ, POINTS, LANES), ("x", "z")).reshape(NX, NZ, POINTS, LANES)
     send = call(last_sum_kernel, ((NA, 8, LANES), BF))(got)
     got = exchange(send, ("y", "c"))
-    focus_plus = call(plus_kernel, (own, BF))(got, inv, onset, focus_start)
+    focus_plus = call(plus_kernel, (own, BF))(got, inv, own_marks, focus_start)
     return (focus_plus, focus_minus)
 
 

time: 161 us -> 160 us (level)
  blocking collectives: 113 us -> 116 us
  starting transfers between devices: 17.5 us -> 15.4 us
  waiting for transfers between devices: 13.3 us -> 11.4 us
    all_to_all x9, blocking collectives: 108 us -> 116 us  [exchange(): return lax.all_to_all(values, axes, 0, 0, tiled=True)]
    all_gather x1 -> x0, blocking collectives: 4.84 us -> none  [shards(): got = lax.all_gather(exchange(send, 'y'), 'c')]
    all_to_all x2, starting transfers between devices: 17.5 us -> 15.4 us  [exchange(): return lax.all_to_all(values, axes, 0, 0, tiled=True)]
    all_to_all x2, waiting for transfers between devices: 13.3 us -> 11.4 us  [exchange(): return lax.all_to_all(values, axes, 0, 0, tiled=True)]
where the time goes in v4:
time: 160 us; the launch traced here: 159 us
  blocking collectives  116 us (72%)
  Pallas kernels  15.7 us (10%)
  starting transfers between devices  15.4 us (10%)
  waiting for transfers between devices  11.4 us (7%)
    all_to_all x9, blocking collectives, exchange(): return lax.all_to_all(values, axes, 0, 0, tiled=True)  116 us
    pallas_call x14, Pallas kernels, run(): pl.pallas_call(kernel, out_shape=shapes, in_specs=[pl.BlockSpec(memory_sp...  15.7 us
    all_to_all x2, starting transfers between devices, exchange(): return lax.all_to_all(values, axes, 0, 0, tiled=True)  15.4 us
    all_to_all x2, waiting for transfers between devices, exchange(): return lax.all_to_all(values, axes, 0, 0, tiled=True)  11.4 us
  transfers between devices with their start and end apart: 2, of which 2 were waited for; matrix products, arithmetic and copies ran while one was open for 0% of the time, Pallas kernels for 2%

profile of v4, /device:TPU:1, one launch (start us, length us, event | category | flops | bytes accessed | tf_op | source)
XLA Modules:
  0.0 159.5 jit_solution(10747826096019803778)
XLA Ops:
  0.6 2.1 %shard_map.95 = bf16[16,8,128]{2,1,0:T(8,128)(2,1)} custom-call(s32[1,64]{1,0:T(1,128)} %bitcast.26, s32[4,16]{1,0:T(4,128)} %bitcast.24, bf16[16,4,1024]{2,1,0:T(4,128)(2,1)} %focus.1, bf16[64,2048]{1,0:T(8,128)(2,1)} %constant.23.clone.base_in), custom_call_target="tpu_custom_call" | custom-call | tf_op jit(solution)/shard_map/pallas_call | solution.py:381
  2.7 10.2 %all-to-all-start = ((bf16[16,8,128]{2,1,0:T(8,128)(2,1)}), bf16[16,8,128]{2,1,0:T(8,128)(2,1)S(1)}, u32[]{:S(2)}, u32[]{:S(2)}) async-start(bf16[16,8,128]{2,1,0:T(8,128)(2,1)} %shard_map.95), calls=%async_computation | async-start | bytes 65536 | tf_op jit(solution)/shard_map/all_to_all | solution.py:396
  12.9 0.1 pad_add_fusion.where
  13.0 2.6 %shard_map.96 = (bf16[768,128]{1,0:T(8,128)(2,1)S(1)}, bf16[512,32]{1,0:T(8,128)(2,1)S(1)}, bf16[16,512]{1,0:T(8,128)(2,1)S(1)}, bf16[2,16,128]{2,1,0:T(8,128)(2...) custom-call(s32[4]{0:T(128)S(1)} %pad_add_fusion.where, ...), custom_call_target="tpu_custom_call" | custom-call | tf_op jit(solution)/shard_map/pallas_call | solution.py:381
  15.6 4.8 %all-to-all-done.got = bf16[16,8,128]{2,1,0:T(8,128)(2,1)S(1)} async-done(((bf16[16,8,128]{2,1,0:T(8,128)(2,1)}), bf16[16,8,128]{2,1,0:T(8,128)(2,1)S(1)}, u32[]{:S(2)}, u32[]{:S(2)}) %all-to-all-start) | async-done | bytes 32800 | tf_op jit(solution)/shard_map/all_to_all | solution.py:396
  20.4 0.3 shard_map.97
  20.7 20.4 %all_to_all.55.got = bf16[32,24,128]{2,1,0:T(8,128)(2,1)S(1)} all-to-all(bf16[32,24,128]{2,1,0:T(8,128)(2,1)S(1)} %bitcast.15), channel_id=1, replica_groups=mesh['x'=4,'y'=8,'c'=2,'z'=8] {'x','z'}, dimensions={0} | all-to-all | bytes 393216 | tf_op jit(solution)/shard_map/all_to_all | solution.py:396
  41.2 1.3 shard_map.98
  42.5 14.5 %all_to_all.56.got = bf16[16,32,128]{2,1,0:T(8,128)(2,1)S(1)} all-to-all(bf16[16,32,128]{2,1,0:T(8,128)(2,1)S(1)} %bitcast.21), channel_id=1, replica_groups=mesh['x'=4,'y'=8,'c'=2,'z'=8] {'y','c'}, dimensions={0} | all-to-all | bytes 262144 | tf_op jit(solution)/shard_map/all_to_all | solution.py:396
  57.0 1.7 %shard_map.99 = bf16[8,32,128]{2,1,0:T(8,128)(2,1)S(1)} custom-call(s32[4]{0:T(128)S(1)} %pad_add_fusion.where, bf16[16,32,128]{2,1,0:T(8,128)(2,1)S(1)} %all_to_all.56.got, bf16[512,32]{1,0:T(8,128)(2,1)S(1)} %get-tuple-element.17.inv, bf16[16,512]{1,0:T(8,128)(2,1)S(1)} %get-tuple-element.13._.fwd, bf16[2,16,32]{2,1,0:T(8,128)(2,1)S(1)} %get-tuple-element.18.fixed, ...), custom_call_target="tpu_custom_call" | custom-call | tf_op jit(solution)/shard_map/pallas_call | solution.py:381
  58.7 7.6 %all_to_all.57.got = bf16[8,32,128]{2,1,0:T(8,128)(2,1)S(1)} all-to-all(bf16[8,32,128]{2,1,0:T(8,128)(2,1)S(1)} %shard_map.99), channel_id=1, replica_groups=mesh['x'=4,'y'=8,'c'=2,'z'=8] {'x','c'}, dimensions={0} | all-to-all | bytes 131072 | tf_op jit(solution)/shard_map/all_to_all | solution.py:396
  66.3 0.5 shard_map.100
  66.8 12.3 %all_to_all.58.got = bf16[32,16,128]{2,1,0:T(8,128)(2,1)S(1)} all-to-all(bf16[32,16,128]{2,1,0:T(8,128)(2,1)S(1)} %shard_map.100), channel_id=1, replica_groups=mesh['x'=4,'y'=8,'c'=2,'z'=8] {'x','z'}, dimensions={0} | all-to-all | bytes 262144 | tf_op jit(solution)/shard_map/all_to_all | solution.py:396
  79.2 13.8 %all_to_all.59.got = bf16[16,32,128]{2,1,0:T(8,128)(2,1)S(1)} all-to-all(bf16[16,32,128]{2,1,0:T(8,128)(2,1)S(1)} %bitcast.20), channel_id=1, replica_groups=mesh['x'=4,'y'=8,'c'=2,'z'=8] {'y','c'}, dimensions={0} | all-to-all | bytes 262144 | tf_op jit(solution)/shard_map/all_to_all | solution.py:396
  93.0 1.2 shard_map.102
  94.1 13.8 %all_to_all.60.got = bf16[64,8,128]{2,1,0:T(8,128)(2,1)S(1)} all-to-all(bf16[64,8,128]{2,1,0:T(8,128)(2,1)S(1)} %bitcast.16), channel_id=1, replica_groups=mesh['x'=4,'y'=8,'c'=2,'z'=8] {'x','c','z'}, dimensions={0} | all-to-all | bytes 262144 | tf_op jit(solution)/shard_map/all_to_all | solution.py:396
  108.0 0.8 shard_map.103
  108.8 13.2 %all_to_all.61.got = bf16[16,32,128]{2,1,0:T(8,128)(2,1)S(1)} all-to-all(bf16[16,32,128]{2,1,0:T(8,128)(2,1)S(1)} %bitcast.17), channel_id=1, replica_groups=mesh['x'=4,'y'=8,'c'=2,'z'=8] {'y','c'}, dimensions={0} | all-to-all | bytes 262144 | tf_op jit(solution)/shard_map/all_to_all | solution.py:396
  121.9 1.8 %shard_map.104 = bf16[8,64,128]{2,1,0:T(8,128)(2,1)S(1)} custom-call(s32[4]{0:T(128)S(1)} %pad_add_fusion.where, bf16[16,32,128]{2,1,0:T(8,128)(2,1)S(1)} %all_to_all.61.got, bf16[512,32]{1,0:T(8,128)(2,1)S(1)} %get-tuple-element.17.inv, bf16[16,512]{1,0:T(8,128)(2,1)S(1)} %get-tuple-element.13._.fwd, bf16[2,16,32]{2,1,0:T(8,128)(2,1)S(1)} %get-tuple-element.18.fixed, ...), custom_call_target="tpu_custom_call" | custom-call | tf_op jit(solution)/shard_map/pallas_call | solution.py:381
  123.7 8.3 %all_to_all.62.got = bf16[8,64,128]{2,1,0:T(8,128)(2,1)S(1)} all-to-all(bf16[8,64,128]{2,1,0:T(8,128)(2,1)S(1)} %shard_map.104), channel_id=1, replica_groups=mesh['x'=4,'y'=8,'c'=2,'z'=8] {'x','c'}, dimensions={0} | all-to-all | bytes 262144 | tf_op jit(solution)/shard_map/all_to_all | solution.py:396
  132.0 0.5 shard_map.105
  132.5 12.2 %all_to_all.63 = bf16[32,16,128]{2,1,0:T(8,128)(2,1)S(1)} all-to-all(bf16[32,16,128]{2,1,0:T(8,128)(2,1)S(1)} %bitcast.18), channel_id=1, replica_groups=mesh['x'=4,'y'=8,'c'=2,'z'=8] {'x','z'}, dimensions={0} | all-to-all | bytes 262144 | tf_op jit(solution)/shard_map/all_to_all | solution.py:396
  144.8 1.0 shard_map.106
  145.7 5.2 %all-to-all-start.10 = ((bf16[16,8,128]{2,1,0:T(8,128)(2,1)}), bf16[16,8,128]{2,1,0:T(8,128)(2,1)S(1)}, u32[]{:S(2)}, u32[]{:S(2)}) async-start(bf16[16,8,128]{2,1,0:T(8,128)(2,1)} %shard_map.106), calls=%async_computation.10 | async-start | bytes 65536 | tf_op jit(solution)/shard_map/all_to_all | solution.py:396
  150.9 0.0 copy-start
  150.9 0.9 shard_map.108
  151.8 6.6 %all-to-all-done.10.got = bf16[16,8,128]{2,1,0:T(8,128)(2,1)S(1)} async-done(((bf16[16,8,128]{2,1,0:T(8,128)(2,1)}), bf16[16,8,128]{2,1,0:T(8,128)(2,1)S(1)}, u32[]{:S(2)}, u32[]{:S(2)}) %all-to-all-start.10) | async-done | bytes 32800 | tf_op jit(solution)/shard_map/all_to_all | solution.py:396
  158.4 0.0 copy-done
  158.4 1.1 shard_map.107
  (1 shorter events, 0.0 us)
Async XLA Ops:
  2.7 17.7 %all-to-all-start = ((bf16[16,8,128]{2,1,0:T(8,128)(2,1)}), bf16[16,8,128]{2,1,0:T(8,128)(2,1)S(1)}, u32[]{:S(2)}, u32[]{:S(2)}) async-start(bf16[16,8,128]{2,1,0:T(8,128)(2,1)} %shard_map.95), calls=%async_computation | async-start | bytes 65536 | tf_op jit(solution)/shard_map/all_to_all | solution.py:396
  145.7 12.7 %all-to-all-start.10 = ((bf16[16,8,128]{2,1,0:T(8,128)(2,1)}), bf16[16,8,128]{2,1,0:T(8,128)(2,1)S(1)}, u32[]{:S(2)}, u32[]{:S(2)}) async-start(bf16[16,8,128]{2,1,0:T(8,128)(2,1)} %shard_map.106), calls=%async_computation.10 | async-start | bytes 65536 | tf_op jit(solution)/shard_map/all_to_all | solution.py:396
  150.9 7.5 %copy-start = (bf16[16,4,1024]{2,1,0:T(4,128)(2,1)S(1)}, bf16[16,4,1024]{2,1,0:T(4,128)(2,1)}, u32[]{:S(2)}) copy-start(bf16[16,4,1024]{2,1,0:T(4,128)(2,1)} %focus.1) | copy-start | bytes 393220

commit v5 on v4

--- a/solution.py
+++ b/solution.py
@@ -19,6 +19,7 @@
 SPANS = ((128, 384), (640, 896), (0, 128), (896, 1024))
 CUT = 512
 KEPT = 768
+TIMES = CUT + 2 * 2 * NG
 ONSET_MID = 256
 BF, F32, I32 = jnp.bfloat16, jnp.float32, jnp.int32
 VMEM_LIMIT = 8 * 1024 * 1024
@@ -99,39 +100,44 @@
 
 def tables_kernel(
     where, bins_in, onset_in, forward_in, inverse_in, re_in, im_in,
-    inv, own_inv, fwd, fixed, own_fixed, own_marks, re, im,
+    inv, own_inv, fwd, own_marks, re, im,
     bins, onset, forward, inverse, sems,
 ):
     pairs = [(bins_in, bins), (onset_in, onset), (forward_in, forward), (inverse_in, inverse), (re_in, re), (im_in, im)]
     copies = fetch(pairs, sems)
     for copy in copies[:4]:
         copy.wait()
-    holds = slab_of_bin(bins[...])
+    held = bins[...].astype(F32).astype(BF)
     j, k = grid(NF, LANES)
-    order = nn(holds, hot(j == ((k >> 5) << 4) + (k & 15)))
-    part = (k >> 4) & 1
-    order = jnp.concatenate([jnp.where(part == 0, order, 0.0), jnp.where(part == 1, order, 0.0)], axis=0)
-    table = nn(inverse[...], order.astype(BF)).astype(BF)
-    inv[...] = table
-    k, n = grid(LANES, 2 * NA)
-    mine = hot(k == 2 * NA * where[0] + n)
-    own_inv[...] = nn(table[:CUT], mine).astype(BF)
+    arrival = ((k >> 5) << 4) + (k & 15)
+    at_k = nn(held, hot(j == arrival))
+    j, n = grid(NF, 2 * NA)
+    at_own = nn(held, hot(j == (where[0] << 4) + (n & 15)))
+    row, k = grid(LANES, LANES)
+    order = hot(((row >> 6) == ((k >> 4) & 1)) & ((row & 63).astype(F32) == at_k))
+    row, n = grid(LANES, 2 * NA)
+    own_order = hot(((row >> 6) == (n >> 4)) & ((row & 63).astype(F32) == at_own))
+    base = inverse[...]
+    table = nn(base, order).astype(BF)
+    own_table = nn(base, own_order).astype(BF)
     m, j = grid(2 * NG, NF)
-    slabs = nt(hot(j == (((m & 7) >> 1) << 4) + (where[1] << 1) + (m & 1)), holds)
-    pick = jnp.concatenate([jnp.where(m < NG, slabs, 0.0), jnp.where(m < NG, 0.0, slabs)], axis=1)
-    picked = nn(pick.astype(BF), forward[...]).astype(BF)
-    picked = jnp.concatenate([picked[:, a:b] for a, b in SPANS], axis=1)
-    fwd[...] = picked[:, :CUT]
-    for n, term in enumerate(two_terms(nn(picked[:, CUT:], table[CUT:]))):
-        fixed[n] = term
-        own_fixed[n] = nn(term, mine).astype(BF)
+    slabs = nt(hot(j == (((m & 7) >> 1) << 4) + (where[1] << 1) + (m & 1)), slab_of_bin(bins[...]))
+    pick = jnp.concatenate([jnp.where(m < NG, slabs, 0.0), jnp.where(m < NG, 0.0, slabs)], axis=1).astype(BF)
+    for n, (a, b) in enumerate(SPANS[:2]):
+        fwd[:, BLOCK * n : BLOCK * (n + 1)] = nn(pick, forward[:, a:b]).astype(BF)
+    picked = [nn(pick, forward[:, a:b]).astype(BF) for a, b in SPANS[2:]]
+    picked = jnp.concatenate(picked, axis=1)
+    for out, part in ((inv, table), (own_inv, own_table)):
+        out[:CUT] = part[:CUT]
+        out[CUT:TIMES] = jnp.concatenate(two_terms(nn(picked, part[CUT:])), axis=0)
+    inv[TIMES:] = table[CUT:]
     m, p = grid(POINTS * NI, POINTS)
     marks = nt(hot((m >> 2) == p), (onset[...] - ONSET_MID).astype(F32).astype(BF))
     m, i = grid(POINTS * NI, NI)
     marks = jnp.where((m & 3) == i, marks, 0.0).sum(axis=1, keepdims=True)
     own_marks[...] = jnp.broadcast_to(marks, (POINTS * NI, LANES)).astype(I32) + ONSET_MID
-    copies[4].wait()
-    copies[5].wait()
+    for copy in copies[4:]:
+        copy.wait()
 
 
 def middle_kernel(got, _, out, rows):
@@ -209,21 +215,22 @@
     convolve(src, mat_re, mat_im, out)
 
 
-def window(spectra, marks, inv, fwd, fixed):
+def window(spectra, marks, inv, fwd):
     t = iota((BLOCK, 1), 0)
     front = jnp.where(t + SPANS[0][0] < marks, nn(inv[:BLOCK], spectra), 0.0).astype(BF)
-    back = jnp.where(t + SPANS[1][0] >= NT - marks, nn(inv[BLOCK:CUT], spectra), 0.0).astype(BF)
-    spec = nn(fwd[:, :BLOCK], front) + nn(fwd[:, BLOCK:], back)
-    return spec + nn(fixed[0], spectra) + nn(fixed[1], spectra)
-
-
-def points_window(marks, first, count, every, inv, fwd, fixed):
+    rest = nn(inv[BLOCK:TIMES], spectra)
+    back = jnp.where(t + SPANS[1][0] >= NT - marks, rest[:BLOCK], 0.0).astype(BF)
+    fixed = rest[BLOCK : BLOCK + 2 * NG] + rest[BLOCK + 2 * NG :]
+    return nn(fwd[:, :BLOCK], front) + nn(fwd[:, BLOCK:], back) + fixed
+
+
+def points_window(marks, first, count, every, inv, fwd):
     mark = jnp.concatenate([marks[pl.ds(first + p, 1), :] for p in range(count)], axis=1)
-    spec = window(jnp.concatenate(every, axis=1), mark, inv, fwd, fixed)
+    spec = window(jnp.concatenate(every, axis=1), mark, inv, fwd)
     return [spec[:, BLOCK * p : BLOCK * (p + 1)] for p in range(count)]
 
 
-def window_slabs(where, got, inv, fwd, fixed, marks, rows, turn):
+def window_slabs(where, got, inv, fwd, marks, rows, turn):
     rows[...] = got[...].astype(F32).reshape(NA * 32, LANES)
     every = []
     for p in range(8):
@@ -232,7 +239,7 @@
             halves = [rows[pl.ds(16 * part + 8 * half + p, NA, stride=32), :] for half in range(2)]
             parts.append(jnp.concatenate(halves, axis=1))
         every.append(jnp.concatenate(parts, axis=0).astype(BF))
-    for p, spec in enumerate(points_window(marks, 8 * where[2], 8, every, inv, fwd, fixed)):
+    for p, spec in enumerate(points_window(marks, 8 * where[2], 8, every, inv, fwd)):
         for part in range(2):
             for half in range(2):
                 at = 16 * part + 8 * half + p
@@ -241,27 +248,22 @@
     return every, turn[...].reshape(NG, 32, LANES)
 
 
-def time_kernel(where, got, inv, fwd, fixed, marks, out, rows, turn):
-    out[...] = window_slabs(where, got, inv, fwd, fixed, marks, rows, turn)[1].astype(BF)
-
-
-def last_time_kernel(where, got, inv, fwd, fixed, marks, out, rows, turn, tail):
-    every, message = window_slabs(where, got, inv, fwd, fixed, marks, rows, turn)
+def time_kernel(where, got, inv, fwd, marks, out, rows, turn):
+    out[...] = window_slabs(where, got, inv, fwd, marks, rows, turn)[1].astype(BF)
+
+
+def last_time_kernel(where, got, inv, fwd, marks, out, rows, turn, tail):
+    every, message = window_slabs(where, got, inv, fwd, marks, rows, turn)
     m, r = grid(NG * NI, BLOCK)
     own = hot(r == ((m >> 3) << 6) + (where[1] << 3) + (((m >> 2) & 1) << 2) + (m & 3))
-    taken = [nt(own, spectra) for spectra in every]
-    taken = jnp.concatenate(taken, axis=0).astype(BF)
-    n, k = grid(2 * NA, LANES)
-    taken = nn(taken, hot(k == 2 * NA * where[0] + n))
-    for p in range(8):
+    for h in range(2):
+        taken = nt(own, jnp.concatenate(every[4 * h : 4 * (h + 1)], axis=0))
         for g in range(NG):
-            at = NG * NI * p + NI * g
-            tail[32 * g + NI * p : 32 * g + NI * (p + 1), :] = taken[at : at + NI]
-    own = tail[...].reshape(NG, 32, LANES)
-    out[...] = jnp.concatenate([message, own], axis=1).astype(BF)
-
-
-def time_copies_kernel(where, got, inv, fwd, fixed, marks, out, rows, turn):
+            tail[8 * g + NI * h : 8 * g + NI * (h + 1), :] = taken[NI * g : NI * (g + 1)]
+    out[...] = jnp.concatenate([message, tail[...].reshape(NG, 8, LANES)], axis=1).astype(BF)
+
+
+def time_copies_kernel(where, got, inv, fwd, marks, out, rows, turn):
     rows[...] = got[...].astype(F32).reshape(NF * 8, LANES)
     every = []
     for p in range(2):
@@ -273,7 +275,7 @@
                 parts.append(jnp.concatenate(halves, axis=1))
         every.append(jnp.concatenate(parts, axis=0).astype(BF))
     first = 4 * where[0] + 2 * where[2]
-    for p, spec in enumerate(points_window(marks, first, 2, every, inv, fwd, fixed)):
+    for p, spec in enumerate(points_window(marks, first, 2, every, inv, fwd)):
         for part in range(2):
             for half in range(2):
                 slab = spec[NG * part : NG * (part + 1), LANES * half : LANES * (half + 1)]
@@ -339,8 +341,9 @@
 
 
 def keep_own(spectra, inv, marks):
-    trace = nt(spectra, inv)
     t = iota((POINTS * NI, LANES), 1)
+    trace = [nt(spectra, inv[a:b]) for a, b in ((0, CUT), (TIMES, TIMES + KEPT - CUT))]
+    trace = jnp.concatenate(trace, axis=1)
     pieces = [trace[:, LANES * n : LANES * (n + 1)] for n in range(KEPT // LANES)]
     none = jnp.zeros_like(pieces[0])
     front = [jnp.where(t + SPANS[0][0] + LANES * n < marks, pieces[n], 0.0) for n in range(2)]
@@ -348,31 +351,40 @@
     return jnp.concatenate([pieces[4], *front, none, none, *back, pieces[5]], axis=1)
 
 
-def minus_kernel(got, inv, marks, out):
-    own = [sum(got[NC * x + c].astype(F32)[32:] for x in range(NX)) for c in range(NC)]
-    own = jnp.concatenate(own, axis=0).astype(BF)
-    trace = keep_own(own, inv[...], marks[...])
-    for p in range(POINTS):
-        out[p] = trace[NI * p : NI * (p + 1)].astype(BF)
-
-
-def plus_kernel(got, inv, marks, focus, out):
+def last_kernel(got, tail, inv, marks, focus, plus_out, minus_out, plus, minus, spectra, sems):
     rows = got[...].astype(F32).reshape(8 * NA, LANES).T.astype(BF)
     m, k = grid(8 * NA, LANES)
-    spectra = jnp.zeros((POINTS * NI, LANES), F32)
+    own = jnp.zeros((POINTS * NI, LANES), F32)
     for part in range(2):
         place = hot(((m & 7) < NX) & (k == ((m & 7) << 5) + 16 * part + (m >> 3)))
-        spectra = spectra + nn(rows[NF * part : NF * (part + 1)], place)
-    trace = keep_own(spectra.astype(BF), inv[...], marks[...])
+        own = own + nn(rows[NF * part : NF * (part + 1)], place)
+    trace = keep_own(own.astype(BF), inv[...], marks[...])
     for p in range(POINTS):
-        out[p] = (focus[p].astype(F32) + trace[NI * p : NI * (p + 1)]).astype(BF)
-
-
-def call(kernel, outs, scratch=(), scalars=0, far=0, copies=0):
+        plus[p] = (focus[p].astype(F32) + trace[NI * p : NI * (p + 1)]).astype(BF)
+    first = pltpu.make_async_copy(plus, plus_out, sems.at[0])
+    first.start()
+    own = [jnp.concatenate([tail[NC * x + c].astype(F32)[32:] for c in range(NC)], axis=0) for x in range(NX)]
+    own = jnp.concatenate(own, axis=1).astype(BF)
+    n, k = grid(NX * LANES, LANES)
+    same = (n >> 7) * 32 + (n & 31) == k
+    own = [nn(own, hot(same & (((n >> 5) & 3) == p))) for p in range(4)]
+    for p in range(POINTS):
+        spectra[NI * p : NI * (p + 1), :] = own[p & 3][NI * (p >> 2) : NI * ((p >> 2) + 1)]
+    trace = keep_own(spectra[...].astype(BF), inv[...], marks[...])
+    for p in range(POINTS):
+        minus[p] = trace[NI * p : NI * (p + 1)].astype(BF)
+    second = pltpu.make_async_copy(minus, minus_out, sems.at[1])
+    second.start()
+    first.wait()
+    second.wait()
+
+
+def call(kernel, outs, scratch=(), scalars=0, far=0, copies=0, far_outs=0):
     single = not isinstance(outs, list)
     shapes = [jax.ShapeDtypeStruct(shape, dtype) for shape, dtype in ([outs] if single else outs)]
 
     def run(*args):
+        out_spaces = [pltpu.VMEM] * (len(shapes) - far_outs) + [pltpu.HBM] * far_outs
         spaces = [pltpu.SMEM] * scalars + [pltpu.HBM] * far + [pltpu.VMEM] * (len(args) - scalars - far)
         args = [
             pltpu.with_memory_space_constraint(arg, pltpu.HBM) if space is pltpu.HBM else arg
@@ -382,7 +394,7 @@
             kernel,
             out_shape=shapes,
             in_specs=[pl.BlockSpec(memory_space=space) for space in spaces],
-            out_specs=[pl.BlockSpec(memory_space=pltpu.VMEM)] * len(shapes),
+            out_specs=[pl.BlockSpec(memory_space=space) for space in out_spaces],
             scratch_shapes=[pltpu.VMEM(shape, dtype) for shape, dtype in scratch]
             + [pltpu.SemaphoreType.DMA((copies,))] * (copies > 0),
             compiler_params=pltpu.CompilerParams(vmem_limit_bytes=VMEM_LIMIT),
@@ -407,11 +419,11 @@
     scratch = [((1, NF), I32), ((NI, POINTS), I32), (own, BF), ((NF, 2 * NT), BF), ((POINTS * NI, NT), F32)]
     run = call(start_kernel, ((NA, 8, LANES), BF), scratch, far=4, copies=4)
     got = exchange(run(bins, onset, focus_start, wide), ("y", "c"))
-    outs = [((KEPT, LANES), BF), ((CUT, 2 * NA), BF), ((2 * NG, CUT), BF), ((2, 2 * NG, LANES), BF), ((2, 2 * NG, 2 * NA), BF)]
+    outs = [((TIMES + KEPT - CUT, LANES), BF), ((TIMES, 2 * NA), BF), ((2 * NG, CUT), BF)]
     outs += [((POINTS * NI, LANES), I32), ((BLOCK, COLS), BF), ((BLOCK, COLS), BF)]
     scratch = [((1, NF), I32), ((NI, POINTS), I32), ((2 * NF, NT), BF), ((KEPT, LANES), BF)]
     run = call(tables_kernel, outs, scratch, scalars=1, far=6, copies=6)
-    inv, own_inv, fwd, fixed, own_fixed, own_marks, *mats = run(where, bins, onset, forward, inverse, *mats)
+    inv, own_inv, fwd, own_marks, *mats = run(where, bins, onset, forward, inverse, *mats)
     send = call(middle_kernel, ((NX, NZ, POINTS + 8, LANES), BF), [((8 * NA, LANES), F32)])(got, fwd)
     got = exchange(send.reshape(NX * NZ, POINTS + 8, LANES), ("x", "z"))
     outs = [((NY, NC, 32, LANES), BF), ((2 * POINTS, COLS), BF), ((POINTS, BLOCK), I32)]
@@ -420,12 +432,11 @@
     for step in range(ITERS):
         got = exchange(send.reshape(NA, 32, LANES), ("y", "c"))
         scratch = [((NA * 32, LANES), F32), ((NG * 32, LANES), F32)]
-        tables = (own_inv, fwd, own_fixed, marks)
+        tables = (own_inv, fwd, marks)
         if step == ITERS - 1:
-            scratch = scratch + [((NG * 32, LANES), F32)]
-            send = call(last_time_kernel, ((NG, 64, LANES), BF), scratch, scalars=1)(where, got, *tables)
+            scratch = scratch + [((NG * 8, LANES), F32)]
+            send = call(last_time_kernel, ((NG, 40, LANES), BF), scratch, scalars=1)(where, got, *tables)
             got = exchange(send, ("x", "c"))
-            focus_minus = call(minus_kernel, (own, BF))(got, inv, own_marks)
             break
         send = call(time_kernel, ((NG, 32, LANES), BF), scratch, scalars=1)(where, got, *tables)
         got = exchange(send, ("x", "c"))
@@ -435,15 +446,18 @@
         got = exchange(send.reshape(NA, NX * 8, LANES), ("y", "c"))
         scratch = [((NF * 8, LANES), F32), ((NG * 8, LANES), F32)]
         run = call(time_copies_kernel, ((NG, NZ, 8, LANES), BF), scratch, scalars=1)
-        send = run(where, got, inv, fwd, fixed, marks)
+        send = run(where, got, inv, fwd, marks)
         got = exchange(send.reshape(NG * NZ, 8, LANES), ("x", "c", "z"))
         scratch = [((NG * NZ * 8, LANES), F32), ((2 * POINTS * COLS // LANES, LANES), F32)]
         send = call(next_conv_kernel, ((NY, NC, 32, LANES), BF), scratch)(got, first, *mats)
+    tail = got
     send = call(last_corr_kernel, ((NX, NZ, POINTS, LANES), BF))(got, *mats)
     got = exchange(send.reshape(NX * NZ, POINTS, LANES), ("x", "z")).reshape(NX, NZ, POINTS, LANES)
     send = call(last_sum_kernel, ((NA, 8, LANES), BF))(got)
     got = exchange(send, ("y", "c"))
-    focus_plus = call(plus_kernel, (own, BF))(got, inv, own_marks, focus_start)
+    scratch = [(own, BF), (own, BF), ((POINTS * NI, LANES), F32)]
+    run = call(last_kernel, [(own, BF), (own, BF)], scratch, copies=2, far_outs=2)
+    focus_plus, focus_minus = run(got, tail, inv, own_marks, focus_start)
     return (focus_plus, focus_minus)
 
 

time: 160 us -> 158 us (0.988)
  blocking collectives: 116 us -> 128 us
  waiting for transfers between devices: 11.4 us -> 4.98 us
  starting transfers between devices: 15.4 us -> 10.2 us
    all_to_all x9 -> x10, blocking collectives: 116 us -> 128 us  [exchange(): return lax.all_to_all(values, axes, 0, 0, tiled=True)]
    all_to_all x2 -> x1, waiting for transfers between devices: 11.4 us -> 4.98 us  [exchange(): return lax.all_to_all(values, axes, 0, 0, tiled=True)]
    all_to_all x2 -> x1, starting transfers between devices: 15.4 us -> 10.2 us  [exchange(): return lax.all_to_all(values, axes, 0, 0, tiled=True)]
    pallas_call x14 -> x13, Pallas kernels: 15.7 us -> 14.1 us  [run(): pl.pallas_call(kernel, out_shape=shapes, in_specs=[pl.BlockSpec(memory_sp...]
  transfers between devices with their start and end apart: 2 -> 1, of which waited for: 2 -> 1; matrix products, arithmetic and copies ran while one was open for 0% -> 0% of each run, Pallas kernels for 2% -> 2%
where the time goes in v5:
time: 158 us
  blocking collectives  128 us (81%)
  Pallas kernels  14.1 us (9%)
  starting transfers between devices  10.2 us (6%)
  waiting for transfers between devices  4.98 us (3%)
    all_to_all x10, blocking collectives, exchange(): return lax.all_to_all(values, axes, 0, 0, tiled=True)  128 us
    pallas_call x13, Pallas kernels, run(): pl.pallas_call(kernel, out_shape=shapes, in_specs=[pl.BlockSpec(memory_sp...  14.1 us
    all_to_all x1, starting transfers between devices, exchange(): return lax.all_to_all(values, axes, 0, 0, tiled=True)  10.2 us
    all_to_all x1, waiting for transfers between devices, exchange(): return lax.all_to_all(values, axes, 0, 0, tiled=True)  4.98 us
  transfers between devices with their start and end apart: 1, of which 1 were waited for; matrix products, arithmetic and copies ran while one was open for 0% of the time, Pallas kernels for 2%

profile of v5, /device:TPU:1, one launch (start us, length us, event | category | flops | bytes accessed | tf_op | source)
XLA Modules:
  0.0 157.7 jit_solution(13389726170518741273)
XLA Ops:
  0.6 2.1 %shard_map.95 = bf16[16,8,128]{2,1,0:T(8,128)(2,1)} custom-call(s32[1,64]{1,0:T(1,128)} %bitcast.26, s32[4,16]{1,0:T(4,128)} %bitcast.24, bf16[16,4,1024]{2,1,0:T(4,128)(2,1)} %focus.1, bf16[64,2048]{1,0:T(8,128)(2,1)} %constant.23.clone.base_in), custom_call_target="tpu_custom_call" | custom-call | tf_op jit(solution)/shard_map/pallas_call | solution.py:393
  2.7 10.2 %all-to-all-start = ((bf16[16,8,128]{2,1,0:T(8,128)(2,1)}), bf16[16,8,128]{2,1,0:T(8,128)(2,1)S(1)}, u32[]{:S(2)}, u32[]{:S(2)}) async-start(bf16[16,8,128]{2,1,0:T(8,128)(2,1)} %shard_map.95), calls=%async_computation | async-start | bytes 65536 | tf_op jit(solution)/shard_map/all_to_all | solution.py:408
  12.9 0.1 pad_add_fusion.where
  13.0 2.4 %shard_map.96 = (bf16[800,128]{1,0:T(8,128)(2,1)S(1)}, bf16[544,32]{1,0:T(8,128)(2,1)S(1)}, bf16[16,512]{1,0:T(8,128)(2,1)S(1)}, s32[64,128]{1,0:T(8,128)S(1)}, ...) custom-call(s32[4]{0:T(128)S(1)} %pad_add_fusion.where, s32[1,64]{1,0:T(1,128)} %bitcast.27, ...), custom_call_target="tpu_custom_call" | custom-call | tf_op jit(solution)/shard_map/pallas_call | solution.py:393
  15.4 5.0 %all-to-all-done.got = bf16[16,8,128]{2,1,0:T(8,128)(2,1)S(1)} async-done(((bf16[16,8,128]{2,1,0:T(8,128)(2,1)}), bf16[16,8,128]{2,1,0:T(8,128)(2,1)S(1)}, u32[]{:S(2)}, u32[]{:S(2)}) %all-to-all-start) | async-done | bytes 32800 | tf_op jit(solution)/shard_map/all_to_all | solution.py:408
  20.4 0.3 shard_map.97
  20.7 20.4 %all_to_all.55.got = bf16[32,24,128]{2,1,0:T(8,128)(2,1)S(1)} all-to-all(bf16[32,24,128]{2,1,0:T(8,128)(2,1)S(1)} %bitcast.15), channel_id=1, replica_groups=mesh['x'=4,'y'=8,'c'=2,'z'=8] {'x','z'}, dimensions={0} | all-to-all | bytes 393216 | tf_op jit(solution)/shard_map/all_to_all | solution.py:408
  41.2 1.3 shard_map.98
  42.5 14.5 %all_to_all.56.got = bf16[16,32,128]{2,1,0:T(8,128)(2,1)S(1)} all-to-all(bf16[16,32,128]{2,1,0:T(8,128)(2,1)S(1)} %bitcast.21), channel_id=1, replica_groups=mesh['x'=4,'y'=8,'c'=2,'z'=8] {'y','c'}, dimensions={0} | all-to-all | bytes 262144 | tf_op jit(solution)/shard_map/all_to_all | solution.py:408
  57.0 1.6 %shard_map.99 = bf16[8,32,128]{2,1,0:T(8,128)(2,1)S(1)} custom-call(s32[4]{0:T(128)S(1)} %pad_add_fusion.where, bf16[16,32,128]{2,1,0:T(8,128)(2,1)S(1)} %all_to_all.56.got, bf16[544,32]{1,0:T(8,128)(2,1)S(1)} %get-tuple-element.15.inv, bf16[16,512]{1,0:T(8,128)(2,1)S(1)} %get-tuple-element.11._.fwd, s32[16,256]{1,0:T(8,128)S(1)} %get-tuple-element.16.marks), custom_call_target="tpu_custom_call" | custom-call | tf_op jit(solution)/shard_map/pallas_call | solution.py:393
  58.6 7.6 %all_to_all.57.got = bf16[8,32,128]{2,1,0:T(8,128)(2,1)S(1)} all-to-all(bf16[8,32,128]{2,1,0:T(8,128)(2,1)S(1)} %shard_map.99), channel_id=1, replica_groups=mesh['x'=4,'y'=8,'c'=2,'z'=8] {'x','c'}, dimensions={0} | all-to-all | bytes 131072 | tf_op jit(solution)/shard_map/all_to_all | solution.py:408
  66.3 0.5 shard_map.100
  66.8 12.3 %all_to_all.58.got = bf16[32,16,128]{2,1,0:T(8,128)(2,1)S(1)} all-to-all(bf16[32,16,128]{2,1,0:T(8,128)(2,1)S(1)} %shard_map.100), channel_id=1, replica_groups=mesh['x'=4,'y'=8,'c'=2,'z'=8] {'x','z'}, dimensions={0} | all-to-all | bytes 262144 | tf_op jit(solution)/shard_map/all_to_all | solution.py:408
  79.1 13.8 %all_to_all.59.got = bf16[16,32,128]{2,1,0:T(8,128)(2,1)S(1)} all-to-all(bf16[16,32,128]{2,1,0:T(8,128)(2,1)S(1)} %bitcast.20), channel_id=1, replica_groups=mesh['x'=4,'y'=8,'c'=2,'z'=8] {'y','c'}, dimensions={0} | all-to-all | bytes 262144 | tf_op jit(solution)/shard_map/all_to_all | solution.py:408
  92.9 1.1 shard_map.102
  94.1 13.8 %all_to_all.60.got = bf16[64,8,128]{2,1,0:T(8,128)(2,1)S(1)} all-to-all(bf16[64,8,128]{2,1,0:T(8,128)(2,1)S(1)} %bitcast.18), channel_id=1, replica_groups=mesh['x'=4,'y'=8,'c'=2,'z'=8] {'x','c','z'}, dimensions={0} | all-to-all | bytes 262144 | tf_op jit(solution)/shard_map/all_to_all | solution.py:408
  107.9 0.8 shard_map.103
  108.7 13.2 %all_to_all.61.got = bf16[16,32,128]{2,1,0:T(8,128)(2,1)S(1)} all-to-all(bf16[16,32,128]{2,1,0:T(8,128)(2,1)S(1)} %bitcast.16), channel_id=1, replica_groups=mesh['x'=4,'y'=8,'c'=2,'z'=8] {'y','c'}, dimensions={0} | all-to-all | bytes 262144 | tf_op jit(solution)/shard_map/all_to_all | solution.py:408
  121.8 1.6 %shard_map.104 = bf16[8,40,128]{2,1,0:T(8,128)(2,1)S(1)} custom-call(s32[4]{0:T(128)S(1)} %pad_add_fusion.where, bf16[16,32,128]{2,1,0:T(8,128)(2,1)S(1)} %all_to_all.61.got, bf16[544,32]{1,0:T(8,128)(2,1)S(1)} %get-tuple-element.15.inv, bf16[16,512]{1,0:T(8,128)(2,1)S(1)} %get-tuple-element.11._.fwd, s32[16,256]{1,0:T(8,128)S(1)} %get-tuple-element.16.marks), custom_call_target="tpu_custom_call" | custom-call | tf_op jit(solution)/shard_map/pallas_call | solution.py:393
  123.5 7.9 %all_to_all.62.got.tail = bf16[8,40,128]{2,1,0:T(8,128)(2,1)S(1)} all-to-all(bf16[8,40,128]{2,1,0:T(8,128)(2,1)S(1)} %shard_map.104), channel_id=1, replica_groups=mesh['x'=4,'y'=8,'c'=2,'z'=8] {'x','c'}, dimensions={0} | all-to-all | bytes 163840 | tf_op jit(solution)/shard_map/all_to_all | solution.py:408
  131.4 0.5 shard_map.105
  132.0 12.1 %all_to_all.63 = bf16[32,16,128]{2,1,0:T(8,128)(2,1)S(1)} all-to-all(bf16[32,16,128]{2,1,0:T(8,128)(2,1)S(1)} %bitcast.17), channel_id=1, replica_groups=mesh['x'=4,'y'=8,'c'=2,'z'=8] {'x','z'}, dimensions={0} | all-to-all | bytes 262144 | tf_op jit(solution)/shard_map/all_to_all | solution.py:408
  144.1 0.0 copy-start
  144.1 0.3 shard_map.106
  144.5 11.9 %all_to_all.64.got = bf16[16,8,128]{2,1,0:T(8,128)(2,1)S(1)} all-to-all(bf16[16,8,128]{2,1,0:T(8,128)(2,1)S(1)} %shard_map.106), channel_id=1, replica_groups=mesh['x'=4,'y'=8,'c'=2,'z'=8] {'y','c'}, dimensions={0} | all-to-all | bytes 65536 | tf_op jit(solution)/shard_map/all_to_all | solution.py:408
  156.3 0.0 copy-done
  156.3 1.3 shard_map.107
  (1 shorter events, 0.0 us)
Async XLA Ops:
  2.7 17.7 %all-to-all-start = ((bf16[16,8,128]{2,1,0:T(8,128)(2,1)}), bf16[16,8,128]{2,1,0:T(8,128)(2,1)S(1)}, u32[]{:S(2)}, u32[]{:S(2)}) async-start(bf16[16,8,128]{2,1,0:T(8,128)(2,1)} %shard_map.95), calls=%async_computation | async-start | bytes 65536 | tf_op jit(solution)/shard_map/all_to_all | solution.py:408
  144.1 12.2 %copy-start = (bf16[16,4,1024]{2,1,0:T(4,128)(2,1)S(1)}, bf16[16,4,1024]{2,1,0:T(4,128)(2,1)}, u32[]{:S(2)}) copy-start(bf16[16,4,1024]{2,1,0:T(4,128)(2,1)} %focus.1) | copy-start | bytes 393220

commit v6 on v5

--- a/solution.py
+++ b/solution.py
@@ -12,7 +12,9 @@
 FLO = 8
 ITERS = 2
 NX, NY, NC, NZ = 4, 8, 2, 8
+NW = 2
 NA, NG, NI = NY * NC, NX * NC, 4
+NU = NG * NW
 NF, POINTS, NT = 64, 16, 1024
 BLOCK, COLS = 256, 2048
 LANES = 128
@@ -20,6 +22,7 @@
 CUT = 512
 KEPT = 768
 TIMES = CUT + 2 * 2 * NG
+OWN_TIMES = CUT + 2 * 2 * NU
 ONSET_MID = 256
 BF, F32, I32 = jnp.bfloat16, jnp.float32, jnp.int32
 VMEM_LIMIT = 8 * 1024 * 1024
@@ -100,13 +103,18 @@
 
 def tables_kernel(
     where, bins_in, onset_in, forward_in, inverse_in, re_in, im_in,
-    inv, own_inv, fwd, own_marks, re, im,
+    place, inv, own_inv, fwd, own_fwd, own_marks, re, im,
     bins, onset, forward, inverse, sems,
 ):
     pairs = [(bins_in, bins), (onset_in, onset), (forward_in, forward), (inverse_in, inverse), (re_in, re), (im_in, im)]
     copies = fetch(pairs, sems)
     for copy in copies[:4]:
         copy.wait()
+    row, _ = grid(8, LANES)
+    value = jnp.zeros((8, LANES), I32)
+    for n in range(4):
+        value = jnp.where(row == n, where[n], value)
+    place[...] = value
     held = bins[...].astype(F32).astype(BF)
     j, k = grid(NF, LANES)
     arrival = ((k >> 5) << 4) + (k & 15)
@@ -120,17 +128,22 @@
     base = inverse[...]
     table = nn(base, order).astype(BF)
     own_table = nn(base, own_order).astype(BF)
+    holds = slab_of_bin(bins[...])
     m, j = grid(2 * NG, NF)
-    slabs = nt(hot(j == (((m & 7) >> 1) << 4) + (where[1] << 1) + (m & 1)), slab_of_bin(bins[...]))
-    pick = jnp.concatenate([jnp.where(m < NG, slabs, 0.0), jnp.where(m < NG, 0.0, slabs)], axis=1).astype(BF)
-    for n, (a, b) in enumerate(SPANS[:2]):
-        fwd[:, BLOCK * n : BLOCK * (n + 1)] = nn(pick, forward[:, a:b]).astype(BF)
-    picked = [nn(pick, forward[:, a:b]).astype(BF) for a, b in SPANS[2:]]
-    picked = jnp.concatenate(picked, axis=1)
-    for out, part in ((inv, table), (own_inv, own_table)):
-        out[:CUT] = part[:CUT]
-        out[CUT:TIMES] = jnp.concatenate(two_terms(nn(picked, part[CUT:])), axis=0)
+    slabs = hot(j == (((m & 7) >> 1) << 4) + (where[1] << 1) + (m & 1))
+    m, j = grid(2 * NU, NF)
+    own_slabs = hot(j == (((m & 15) >> 2) << 4) + ((where[1] >> 1) << 2) + ((m & 1) << 1) + ((m >> 1) & 1))
     inv[TIMES:] = table[CUT:]
+    for to_inv, to_fwd, part, rows in ((inv, fwd, table, slabs), (own_inv, own_fwd, own_table, own_slabs)):
+        count = rows.shape[0] // 2
+        rows = nt(rows, holds)
+        first = iota(rows.shape, 0) < count
+        pick = jnp.concatenate([jnp.where(first, rows, 0.0), jnp.where(first, 0.0, rows)], axis=1).astype(BF)
+        for n, (a, b) in enumerate(SPANS[:2]):
+            to_fwd[:, BLOCK * n : BLOCK * (n + 1)] = nn(pick, forward[:, a:b]).astype(BF)
+        picked = jnp.concatenate([nn(pick, forward[:, a:b]).astype(BF) for a, b in SPANS[2:]], axis=1)
+        to_inv[:CUT] = part[:CUT]
+        to_inv[CUT : CUT + 4 * count] = jnp.concatenate(two_terms(nn(picked, part[CUT:])), axis=0)
     m, p = grid(POINTS * NI, POINTS)
     marks = nt(hot((m >> 2) == p), (onset[...] - ONSET_MID).astype(F32).astype(BF))
     m, i = grid(POINTS * NI, NI)
@@ -176,13 +189,14 @@
     parts = (a[:POINTS] - b[POINTS:], a[POINTS:] + b[:POINTS])
     for c in range(NC):
         at = slice(8 * c, 8 * (c + 1))
-        slabs = [part[at, LANES * half : LANES * (half + 1)] for part in parts for half in range(2)]
-        message = jnp.concatenate(slabs, axis=0).astype(BF)
-        for y in range(NY):
-            out[y, c] = message
-
-
-def first_conv_kernel(where, got, mat_re, mat_im, out, src, marks, rows):
+        for w in range(NW):
+            slabs = [part[at, LANES * w : LANES * (w + 1)] for part in parts]
+            message = jnp.concatenate(slabs, axis=0).astype(BF)
+            for v in range(NY // NW):
+                out[NW * v + w, c] = message
+
+
+def first_conv_kernel(place, got, mat_re, mat_im, out, src, own_marks, marks, rows):
     height = POINTS + 8
     rows[...] = got[...].astype(F32).reshape(NX * NZ * height, LANES)
     for z in range(NZ):
@@ -193,12 +207,25 @@
             re, im = swap(a, b)
             src[:POINTS, at : at + LANES] = re.astype(BF)
             src[POINTS:, at : at + LANES] = im.astype(BF)
+    x, y, c, z = (place[n : n + 1, :] for n in range(4))
+    mine = (y & 1) + 2 * c
+    own = jnp.zeros((8, LANES), F32)
+    picked = []
+    p, _ = grid(POINTS, LANES)
     for half in range(2):
-        at = (2 * half * NZ + where[3]) * height + POINTS
-        a = rows[pl.ds(pl.multiple_of(at, 8), 8), :]
-        b = rows[pl.ds(pl.multiple_of(at + NZ * height, 8), 8), :]
-        for h, block in enumerate(swap(a, b)):
-            marks[8 * h : 8 * (h + 1), LANES * half : LANES * (half + 1)] = block.astype(I32) + ONSET_MID
+        a = b = jnp.zeros((8, LANES), F32)
+        for n in range(NZ):
+            at = (2 * half * NZ + n) * height + POINTS
+            a = jnp.where(z == n, rows[at : at + 8, :], a)
+            b = jnp.where(z == n, rows[at + NZ * height : at + NZ * height + 8, :], b)
+        blocks = swap(a, b)
+        for h in range(2):
+            own = jnp.where(mine == half + 2 * h, blocks[h], own)
+        blocks = jnp.concatenate(blocks, axis=0)
+        for n in range(2):
+            row = jnp.where(p == 4 * x + 2 * c + n, blocks, 0.0).sum(axis=0, keepdims=True)
+            marks[2 * n + half : 2 * n + half + 1, :] = row.astype(I32) + ONSET_MID
+    own_marks[...] = own.astype(I32) + ONSET_MID
     convolve(src[...], mat_re, mat_im, out)
 
 
@@ -217,53 +244,49 @@
 
 def window(spectra, marks, inv, fwd):
     t = iota((BLOCK, 1), 0)
+    count = fwd.shape[0]
     front = jnp.where(t + SPANS[0][0] < marks, nn(inv[:BLOCK], spectra), 0.0).astype(BF)
-    rest = nn(inv[BLOCK:TIMES], spectra)
+    rest = nn(inv[BLOCK : CUT + 2 * count], spectra)
     back = jnp.where(t + SPANS[1][0] >= NT - marks, rest[:BLOCK], 0.0).astype(BF)
-    fixed = rest[BLOCK : BLOCK + 2 * NG] + rest[BLOCK + 2 * NG :]
+    fixed = rest[BLOCK : BLOCK + count] + rest[BLOCK + count :]
     return nn(fwd[:, :BLOCK], front) + nn(fwd[:, BLOCK:], back) + fixed
 
 
-def points_window(marks, first, count, every, inv, fwd):
-    mark = jnp.concatenate([marks[pl.ds(first + p, 1), :] for p in range(count)], axis=1)
-    spec = window(jnp.concatenate(every, axis=1), mark, inv, fwd)
-    return [spec[:, BLOCK * p : BLOCK * (p + 1)] for p in range(count)]
-
-
-def window_slabs(where, got, inv, fwd, marks, rows, turn):
-    rows[...] = got[...].astype(F32).reshape(NA * 32, LANES)
+def window_slabs(got, inv, fwd, marks, rows, turn):
+    rows[...] = got[...].astype(F32).reshape(NA * 16, LANES)
     every = []
     for p in range(8):
-        parts = []
+        parts = [rows[pl.ds(8 * part + p, NA, stride=16), :] for part in range(2)]
+        every.append(jnp.concatenate(parts, axis=0).astype(BF))
+    mark = [marks[p : p + 1, :] for p in range(8)]
+    spec = window(jnp.concatenate(every, axis=1), jnp.concatenate(mark, axis=1), inv, fwd)
+    for p in range(8):
         for part in range(2):
-            halves = [rows[pl.ds(16 * part + 8 * half + p, NA, stride=32), :] for half in range(2)]
-            parts.append(jnp.concatenate(halves, axis=1))
-        every.append(jnp.concatenate(parts, axis=0).astype(BF))
-    for p, spec in enumerate(points_window(marks, 8 * where[2], 8, every, inv, fwd)):
-        for part in range(2):
-            for half in range(2):
-                at = 16 * part + 8 * half + p
-                slab = spec[NG * part : NG * (part + 1), LANES * half : LANES * (half + 1)]
-                turn[pl.ds(at, NG, stride=32), :] = slab
-    return every, turn[...].reshape(NG, 32, LANES)
-
-
-def time_kernel(where, got, inv, fwd, marks, out, rows, turn):
-    out[...] = window_slabs(where, got, inv, fwd, marks, rows, turn)[1].astype(BF)
-
-
-def last_time_kernel(where, got, inv, fwd, marks, out, rows, turn, tail):
-    every, message = window_slabs(where, got, inv, fwd, marks, rows, turn)
-    m, r = grid(NG * NI, BLOCK)
-    own = hot(r == ((m >> 3) << 6) + (where[1] << 3) + (((m >> 2) & 1) << 2) + (m & 3))
+            slab = spec[NU * part : NU * (part + 1), LANES * p : LANES * (p + 1)]
+            turn[pl.ds(8 * part + p, NU, stride=16), :] = slab
+    return every, turn[...].reshape(NU, 16, LANES)
+
+
+def time_kernel(got, inv, fwd, marks, out, rows, turn):
+    out[...] = window_slabs(got, inv, fwd, marks, rows, turn)[1].astype(BF)
+
+
+def last_time_kernel(got, inv, fwd, marks, place, out, rows, turn, tail):
+    every, message = window_slabs(got, inv, fwd, marks, rows, turn)
+    m, r = grid(NU * NI, LANES)
+    y = place[1:2, :]
+    w = y & 1
+    y = (y & 6) + ((m >> 2) & 1)
+    own = ((m >> 4) << 6) + (y << 3) + (((m >> 3) & 1) << 2) + (m & 3)
+    own = hot(r + LANES * w == own)
     for h in range(2):
         taken = nt(own, jnp.concatenate(every[4 * h : 4 * (h + 1)], axis=0))
-        for g in range(NG):
-            tail[8 * g + NI * h : 8 * g + NI * (h + 1), :] = taken[NI * g : NI * (g + 1)]
-    out[...] = jnp.concatenate([message, tail[...].reshape(NG, 8, LANES)], axis=1).astype(BF)
-
-
-def time_copies_kernel(where, got, inv, fwd, marks, out, rows, turn):
+        for u in range(NU):
+            tail[8 * u + NI * h : 8 * u + NI * (h + 1), :] = taken[NI * u : NI * (u + 1)]
+    out[...] = jnp.concatenate([message, tail[...].reshape(NU, 8, LANES)], axis=1).astype(BF)
+
+
+def time_copies_kernel(got, inv, fwd, marks, out, rows, turn):
     rows[...] = got[...].astype(F32).reshape(NF * 8, LANES)
     every = []
     for p in range(2):
@@ -274,8 +297,10 @@
                 halves = [rows[pl.ds(n, NA, stride=8 * NX), :] for n in at]
                 parts.append(jnp.concatenate(halves, axis=1))
         every.append(jnp.concatenate(parts, axis=0).astype(BF))
-    first = 4 * where[0] + 2 * where[2]
-    for p, spec in enumerate(points_window(marks, first, 2, every, inv, fwd)):
+    mark = [marks[n : n + 1, :] for n in range(4)]
+    spectra = window(jnp.concatenate(every, axis=1), jnp.concatenate(mark, axis=1), inv, fwd)
+    for p in range(2):
+        spec = spectra[:, BLOCK * p : BLOCK * (p + 1)]
         for part in range(2):
             for half in range(2):
                 slab = spec[NG * part : NG * (part + 1), LANES * half : LANES * (half + 1)]
@@ -290,8 +315,8 @@
     for part in range(2):
         halves = []
         for half in range(2):
-            at = 8 * (2 * part + half)
-            both = [sum(got[NC * x + c].astype(F32)[at : at + 8] for x in range(NX)) for c in range(NC)]
+            at = 8 * part
+            both = [sum(got[4 * x + 2 * c + half].astype(F32)[at : at + 8] for x in range(NX)) for c in range(NC)]
             halves.append(jnp.concatenate(both, axis=0))
         parts.append(jnp.concatenate(halves, axis=1))
     straight = jnp.concatenate(parts, axis=0).astype(BF)
@@ -363,7 +388,10 @@
         plus[p] = (focus[p].astype(F32) + trace[NI * p : NI * (p + 1)]).astype(BF)
     first = pltpu.make_async_copy(plus, plus_out, sems.at[0])
     first.start()
-    own = [jnp.concatenate([tail[NC * x + c].astype(F32)[32:] for c in range(NC)], axis=0) for x in range(NX)]
+    own = []
+    for x in range(NX):
+        both = [sum(tail[4 * x + 2 * c + w].astype(F32)[16:] for w in range(NW)) for c in range(NC)]
+        own.append(jnp.concatenate(both, axis=0))
     own = jnp.concatenate(own, axis=1).astype(BF)
     n, k = grid(NX * LANES, LANES)
     same = (n >> 7) * 32 + (n & 31) == k
@@ -410,7 +438,7 @@
 
 def shards(focus_start, onset, bins, refl_real, refl_imag):
     mats = (refl_real[0], refl_imag[0])
-    where = jnp.stack([lax.axis_index(axis) for axis in ("x", "y", "c", "z")]).astype(I32)
+    where = jnp.stack([lax.axis_index(axis) for axis in ("x", ("v", "w"), "c", "z")]).astype(I32)
     bins = bins.reshape(1, NF)
     onset = onset.T
     forward, wide, inverse = base_tables()
@@ -418,53 +446,52 @@
 
     scratch = [((1, NF), I32), ((NI, POINTS), I32), (own, BF), ((NF, 2 * NT), BF), ((POINTS * NI, NT), F32)]
     run = call(start_kernel, ((NA, 8, LANES), BF), scratch, far=4, copies=4)
-    got = exchange(run(bins, onset, focus_start, wide), ("y", "c"))
-    outs = [((TIMES + KEPT - CUT, LANES), BF), ((TIMES, 2 * NA), BF), ((2 * NG, CUT), BF)]
+    got = exchange(run(bins, onset, focus_start, wide), ("v", "w", "c"))
+    outs = [((8, LANES), I32), ((TIMES + KEPT - CUT, LANES), BF), ((OWN_TIMES, 2 * NA), BF), ((2 * NG, CUT), BF), ((2 * NU, CUT), BF)]
     outs += [((POINTS * NI, LANES), I32), ((BLOCK, COLS), BF), ((BLOCK, COLS), BF)]
     scratch = [((1, NF), I32), ((NI, POINTS), I32), ((2 * NF, NT), BF), ((KEPT, LANES), BF)]
     run = call(tables_kernel, outs, scratch, scalars=1, far=6, copies=6)
-    inv, own_inv, fwd, own_marks, *mats = run(where, bins, onset, forward, inverse, *mats)
+    place, inv, own_inv, fwd, own_fwd, kept, *mats = run(where, bins, onset, forward, inverse, *mats)
     send = call(middle_kernel, ((NX, NZ, POINTS + 8, LANES), BF), [((8 * NA, LANES), F32)])(got, fwd)
     got = exchange(send.reshape(NX * NZ, POINTS + 8, LANES), ("x", "z"))
-    outs = [((NY, NC, 32, LANES), BF), ((2 * POINTS, COLS), BF), ((POINTS, BLOCK), I32)]
+    outs = [((NY, NC, 16, LANES), BF), ((2 * POINTS, COLS), BF), ((8, LANES), I32), ((4, LANES), I32)]
     scratch = [((NX * NZ * (POINTS + 8), LANES), F32)]
-    send, first, marks = call(first_conv_kernel, outs, scratch, scalars=1)(where, got, *mats)
+    send, first, own_marks, marks = call(first_conv_kernel, outs, scratch)(place, got, *mats)
     for step in range(ITERS):
-        got = exchange(send.reshape(NA, 32, LANES), ("y", "c"))
-        scratch = [((NA * 32, LANES), F32), ((NG * 32, LANES), F32)]
-        tables = (own_inv, fwd, marks)
+        got = exchange(send.reshape(NA, 16, LANES), ("v", "w", "c"))
+        scratch = [((NA * 16, LANES), F32), ((NU * 16, LANES), F32)]
+        tables = (own_inv, own_fwd, own_marks)
         if step == ITERS - 1:
-            scratch = scratch + [((NG * 8, LANES), F32)]
-            send = call(last_time_kernel, ((NG, 40, LANES), BF), scratch, scalars=1)(where, got, *tables)
-            got = exchange(send, ("x", "c"))
+            scratch = scratch + [((NU * 8, LANES), F32)]
+            send = call(last_time_kernel, ((NU, 24, LANES), BF), scratch)(got, *tables, place)
+            got = exchange(send, ("x", "c", "w"))
             break
-        send = call(time_kernel, ((NG, 32, LANES), BF), scratch, scalars=1)(where, got, *tables)
-        got = exchange(send, ("x", "c"))
+        send = call(time_kernel, ((NU, 16, LANES), BF), scratch)(got, *tables)
+        got = exchange(send, ("x", "c", "w"))
         send = call(corr_kernel, ((NX * NZ, 16, LANES), BF), [((NX * NZ * 16, LANES), F32)])(got, *mats)
         got = exchange(send, ("x", "z"))
         send = call(sum_kernel, ((NY, NC, NX * 8, LANES), BF))(got)
-        got = exchange(send.reshape(NA, NX * 8, LANES), ("y", "c"))
+        got = exchange(send.reshape(NA, NX * 8, LANES), ("v", "w", "c"))
         scratch = [((NF * 8, LANES), F32), ((NG * 8, LANES), F32)]
-        run = call(time_copies_kernel, ((NG, NZ, 8, LANES), BF), scratch, scalars=1)
-        send = run(where, got, inv, fwd, marks)
+        send = call(time_copies_kernel, ((NG, NZ, 8, LANES), BF), scratch)(got, inv, fwd, marks)
         got = exchange(send.reshape(NG * NZ, 8, LANES), ("x", "c", "z"))
         scratch = [((NG * NZ * 8, LANES), F32), ((2 * POINTS * COLS // LANES, LANES), F32)]
-        send = call(next_conv_kernel, ((NY, NC, 32, LANES), BF), scratch)(got, first, *mats)
+        send = call(next_conv_kernel, ((NY, NC, 16, LANES), BF), scratch)(got, first, *mats)
     tail = got
     send = call(last_corr_kernel, ((NX, NZ, POINTS, LANES), BF))(got, *mats)
     got = exchange(send.reshape(NX * NZ, POINTS, LANES), ("x", "z")).reshape(NX, NZ, POINTS, LANES)
     send = call(last_sum_kernel, ((NA, 8, LANES), BF))(got)
-    got = exchange(send, ("y", "c"))
+    got = exchange(send, ("v", "w", "c"))
     scratch = [(own, BF), (own, BF), ((POINTS * NI, LANES), F32)]
     run = call(last_kernel, [(own, BF), (own, BF)], scratch, copies=2, far_outs=2)
-    focus_plus, focus_minus = run(got, tail, inv, own_marks, focus_start)
+    focus_plus, focus_minus = run(got, tail, inv, kept, focus_start)
     return (focus_plus, focus_minus)
 
 
 def solution(mesh):
-    fine = Mesh(mesh.devices.reshape(NX, NY, NC, NZ), ("x", "y", "c", "z"))
-    receivers = ("z", "x", "y", "c")
-    slabs = ("x", "y", "c")
+    fine = Mesh(mesh.devices.reshape(NX, NY // NW, NW, NC, NZ), ("x", "v", "w", "c", "z"))
+    receivers = ("z", "x", "v", "w", "c")
+    slabs = ("x", "v", "w", "c")
     return jax.shard_map(
         shards,
         mesh=fine,

time: 158 us -> 156 us (0.987)
  Pallas kernels: 14.1 us -> 11.2 us
    pallas_call x13, Pallas kernels: 14.1 us -> 11.2 us  [run(): pl.pallas_call(kernel, out_shape=shapes, in_specs=[pl.BlockSpec(memory_sp...]
where the time goes in v6:
time: 156 us
  blocking collectives  129 us (83%)
  Pallas kernels  11.2 us (7%)
  starting transfers between devices  10.2 us (7%)
  waiting for transfers between devices  4.86 us (3%)
    all_to_all x10, blocking collectives, exchange(): return lax.all_to_all(values, axes, 0, 0, tiled=True)  129 us
    pallas_call x13, Pallas kernels, run(): pl.pallas_call(kernel, out_shape=shapes, in_specs=[pl.BlockSpec(memory_sp...  11.2 us
    all_to_all x1, starting transfers between devices, exchange(): return lax.all_to_all(values, axes, 0, 0, tiled=True)  10.2 us
    all_to_all x1, waiting for transfers between devices, exchange(): return lax.all_to_all(values, axes, 0, 0, tiled=True)  4.86 us
  transfers between devices with their start and end apart: 1, of which 1 were waited for; matrix products, arithmetic and copies ran while one was open for 0% of the time, Pallas kernels for 2%

profile of v6, /device:TPU:1, one launch (start us, length us, event | category | flops | bytes accessed | tf_op | source)
XLA Modules:
  0.0 155.7 jit_solution(9668998678482861083)
XLA Ops:
  0.6 2.1 %shard_map.96 = bf16[16,8,128]{2,1,0:T(8,128)(2,1)} custom-call(s32[1,64]{1,0:T(1,128)} %bitcast.26, s32[4,16]{1,0:T(4,128)} %bitcast.24, bf16[16,4,1024]{2,1,0:T(4,128)(2,1)} %focus.1, bf16[64,2048]{1,0:T(8,128)(2,1)} %constant.29.clone.base_in), custom_call_target="tpu_custom_call" | custom-call | tf_op jit(solution)/shard_map/pallas_call | solution.py:421
  2.7 10.2 %all-to-all-start = ((bf16[16,8,128]{2,1,0:T(8,128)(2,1)}), bf16[16,8,128]{2,1,0:T(8,128)(2,1)S(1)}, u32[]{:S(2)}, u32[]{:S(2)}) async-start(bf16[16,8,128]{2,1,0:T(8,128)(2,1)} %shard_map.96), calls=%async_computation | async-start | bytes 65536 | tf_op jit(solution)/shard_map/all_to_all | solution.py:436
  12.9 0.1 pad_add_fusion.where
  13.0 2.5 %shard_map.95 = (s32[8,128]{1,0:T(8,128)S(1)}, bf16[800,128]{1,0:T(8,128)(2,1)S(1)}, bf16[576,32]{1,0:T(8,128)(2,1)S(1)}, bf16[16,512]{1,0:T(8,128)(2,1)S(1)}, b...) custom-call(s32[4]{0:T(128)S(1)} %pad_add_fusion.where, ...), custom_call_target="tpu_custom_call" | custom-call | tf_op jit(solution)/shard_map/pallas_call | solution.py:421
  15.5 4.9 %all-to-all-done.got = bf16[16,8,128]{2,1,0:T(8,128)(2,1)S(1)} async-done(((bf16[16,8,128]{2,1,0:T(8,128)(2,1)}), bf16[16,8,128]{2,1,0:T(8,128)(2,1)S(1)}, u32[]{:S(2)}, u32[]{:S(2)}) %all-to-all-start) | async-done | bytes 32800 | tf_op jit(solution)/shard_map/all_to_all | solution.py:436
  20.4 0.3 shard_map.97
  20.7 20.4 %all_to_all.55.got = bf16[32,24,128]{2,1,0:T(8,128)(2,1)S(1)} all-to-all(bf16[32,24,128]{2,1,0:T(8,128)(2,1)S(1)} %bitcast.15), channel_id=1, replica_groups=mesh['x'=4,'v'=4,'w'=2,'c'=2,'z'=8] {'x','z'}, dimensions={0} | all-to-all | bytes 393216 | tf_op jit(solution)/shard_map/all_to_all | solution.py:436
  41.2 0.7 shard_map.98
  41.9 13.2 %all_to_all.56.got = bf16[16,16,128]{2,1,0:T(8,128)(2,1)S(1)} all-to-all(bf16[16,16,128]{2,1,0:T(8,128)(2,1)S(1)} %bitcast.21), channel_id=1, replica_groups=mesh['x'=4,'v'=4,'w'=2,'c'=2,'z'=8] {'v','w','c'}, dimensions={0} | all-to-all | bytes 131072 | tf_op jit(solution)/shard_map/all_to_all | solution.py:436
  55.1 0.7 shard_map.99
  55.8 8.9 %all_to_all.57.got = bf16[16,16,128]{2,1,0:T(8,128)(2,1)S(1)} all-to-all(bf16[16,16,128]{2,1,0:T(8,128)(2,1)S(1)} %shard_map.99), channel_id=1, replica_groups=mesh['x'=4,'v'=4,'w'=2,'c'=2,'z'=8] {'x','c','w'}, dimensions={0} | all-to-all | bytes 131072 | tf_op jit(solution)/shard_map/all_to_all | solution.py:436
  64.6 0.5 shard_map.100
  65.1 12.4 %all_to_all.58.got = bf16[32,16,128]{2,1,0:T(8,128)(2,1)S(1)} all-to-all(bf16[32,16,128]{2,1,0:T(8,128)(2,1)S(1)} %shard_map.100), channel_id=1, replica_groups=mesh['x'=4,'v'=4,'w'=2,'c'=2,'z'=8] {'x','z'}, dimensions={0} | all-to-all | bytes 262144 | tf_op jit(solution)/shard_map/all_to_all | solution.py:436
  77.6 14.3 %all_to_all.59.got = bf16[16,32,128]{2,1,0:T(8,128)(2,1)S(1)} all-to-all(bf16[16,32,128]{2,1,0:T(8,128)(2,1)S(1)} %bitcast.18), channel_id=1, replica_groups=mesh['x'=4,'v'=4,'w'=2,'c'=2,'z'=8] {'v','w','c'}, dimensions={0} | all-to-all | bytes 262144 | tf_op jit(solution)/shard_map/all_to_all | solution.py:436
  91.9 0.6 shard_map.102
  92.5 13.8 %all_to_all.60.got = bf16[64,8,128]{2,1,0:T(8,128)(2,1)S(1)} all-to-all(bf16[64,8,128]{2,1,0:T(8,128)(2,1)S(1)} %bitcast.19), channel_id=1, replica_groups=mesh['x'=4,'v'=4,'w'=2,'c'=2,'z'=8] {'x','c','z'}, dimensions={0} | all-to-all | bytes 262144 | tf_op jit(solution)/shard_map/all_to_all | solution.py:436
  106.3 0.8 shard_map.103
  107.1 11.8 %all_to_all.61.got = bf16[16,16,128]{2,1,0:T(8,128)(2,1)S(1)} all-to-all(bf16[16,16,128]{2,1,0:T(8,128)(2,1)S(1)} %bitcast.20), channel_id=1, replica_groups=mesh['x'=4,'v'=4,'w'=2,'c'=2,'z'=8] {'v','w','c'}, dimensions={0} | all-to-all | bytes 131072 | tf_op jit(solution)/shard_map/all_to_all | solution.py:436
  118.8 0.7 shard_map.104
  119.6 9.2 %all_to_all.62.got.tail = bf16[16,24,128]{2,1,0:T(8,128)(2,1)S(1)} all-to-all(bf16[16,24,128]{2,1,0:T(8,128)(2,1)S(1)} %shard_map.104), channel_id=1, replica_groups=mesh['x'=4,'v'=4,'w'=2,'c'=2,'z'=8] {'x','c','w'}, dimensions={0} | all-to-all | bytes 196608 | tf_op jit(solution)/shard_map/all_to_all | solution.py:436
  128.8 0.5 shard_map.105
  129.3 12.1 %all_to_all.63 = bf16[32,16,128]{2,1,0:T(8,128)(2,1)S(1)} all-to-all(bf16[32,16,128]{2,1,0:T(8,128)(2,1)S(1)} %bitcast.16), channel_id=1, replica_groups=mesh['x'=4,'v'=4,'w'=2,'c'=2,'z'=8] {'x','z'}, dimensions={0} | all-to-all | bytes 262144 | tf_op jit(solution)/shard_map/all_to_all | solution.py:436
  141.4 0.0 copy-start
  141.4 0.3 shard_map.106
  141.8 12.5 %all_to_all.64.got = bf16[16,8,128]{2,1,0:T(8,128)(2,1)S(1)} all-to-all(bf16[16,8,128]{2,1,0:T(8,128)(2,1)S(1)} %shard_map.106), channel_id=1, replica_groups=mesh['x'=4,'v'=4,'w'=2,'c'=2,'z'=8] {'v','w','c'}, dimensions={0} | all-to-all | bytes 65536 | tf_op jit(solution)/shard_map/all_to_all | solution.py:436
  154.3 0.0 copy-done
  154.3 1.3 shard_map.107
  (1 shorter events, 0.0 us)
Async XLA Ops:
  2.7 17.7 %all-to-all-start = ((bf16[16,8,128]{2,1,0:T(8,128)(2,1)}), bf16[16,8,128]{2,1,0:T(8,128)(2,1)S(1)}, u32[]{:S(2)}, u32[]{:S(2)}) async-start(bf16[16,8,128]{2,1,0:T(8,128)(2,1)} %shard_map.96), calls=%async_computation | async-start | bytes 65536 | tf_op jit(solution)/shard_map/all_to_all | solution.py:436
  141.4 12.9 %copy-start = (bf16[16,4,1024]{2,1,0:T(4,128)(2,1)S(1)}, bf16[16,4,1024]{2,1,0:T(4,128)(2,1)}, u32[]{:S(2)}) copy-start(bf16[16,4,1024]{2,1,0:T(4,128)(2,1)} %focus.1) | copy-start | bytes 393220

commit v7 on v6

--- a/solution.py
+++ b/solution.py
@@ -91,7 +91,7 @@
     copies[2].wait()
     for p in range(POINTS):
         flat[NI * p : NI * (p + 1), :] = focus[p].astype(F32)
-    rows = flat[...].astype(BF)
+    rows = flat[: POINTS * NI, :].astype(BF)
     none = jnp.zeros_like(rows)
     copies[3].wait()
     spec = nt(base[:, :NT], jnp.concatenate([rows, none], axis=0))
@@ -154,7 +154,7 @@
 
 
 def middle_kernel(got, _, out, rows):
-    rows[...] = got[...].astype(F32).reshape(8 * NA, LANES)
+    rows[: 8 * NA, :] = got[...].astype(F32).reshape(8 * NA, LANES)
     line = jnp.concatenate([rows[pl.ds(e, NA, stride=8), :] for e in range(NX + 1)], axis=1).astype(BF)
     m, a = grid(NA * NI, NA)
     spread = nn(hot((m >> 2) == a), line)
@@ -210,7 +210,8 @@
     x, y, c, z = (place[n : n + 1, :] for n in range(4))
     mine = (y & 1) + 2 * c
     own = jnp.zeros((8, LANES), F32)
-    picked = []
+    line, _ = grid(8, LANES)
+    few = jnp.zeros((8, LANES), F32)
     p, _ = grid(POINTS, LANES)
     for half in range(2):
         a = b = jnp.zeros((8, LANES), F32)
@@ -224,13 +225,14 @@
         blocks = jnp.concatenate(blocks, axis=0)
         for n in range(2):
             row = jnp.where(p == 4 * x + 2 * c + n, blocks, 0.0).sum(axis=0, keepdims=True)
-            marks[2 * n + half : 2 * n + half + 1, :] = row.astype(I32) + ONSET_MID
+            few = jnp.where(line == 2 * n + half, row, few)
+    marks[...] = few.astype(I32) + ONSET_MID
     own_marks[...] = own.astype(I32) + ONSET_MID
     convolve(src[...], mat_re, mat_im, out)
 
 
 def next_conv_kernel(got, first, mat_re, mat_im, out, rows, more):
-    rows[...] = got[...].astype(F32).reshape(NG * NZ * 8, LANES)
+    rows[: NG * NZ * 8, :] = got[...].astype(F32).reshape(NG * NZ * 8, LANES)
     for z in range(NZ):
         for p in range(2):
             for part in range(2):
@@ -253,7 +255,7 @@
 
 
 def window_slabs(got, inv, fwd, marks, rows, turn):
-    rows[...] = got[...].astype(F32).reshape(NA * 16, LANES)
+    rows[: NA * 16, :] = got[...].astype(F32).reshape(NA * 16, LANES)
     every = []
     for p in range(8):
         parts = [rows[pl.ds(8 * part + p, NA, stride=16), :] for part in range(2)]
@@ -264,7 +266,7 @@
         for part in range(2):
             slab = spec[NU * part : NU * (part + 1), LANES * p : LANES * (p + 1)]
             turn[pl.ds(8 * part + p, NU, stride=16), :] = slab
-    return every, turn[...].reshape(NU, 16, LANES)
+    return every, turn[: NU * 16, :].reshape(NU, 16, LANES)
 
 
 def time_kernel(got, inv, fwd, marks, out, rows, turn):
@@ -283,11 +285,11 @@
         taken = nt(own, jnp.concatenate(every[4 * h : 4 * (h + 1)], axis=0))
         for u in range(NU):
             tail[8 * u + NI * h : 8 * u + NI * (h + 1), :] = taken[NI * u : NI * (u + 1)]
-    out[...] = jnp.concatenate([message, tail[...].reshape(NU, 8, LANES)], axis=1).astype(BF)
+    out[...] = jnp.concatenate([message, tail[: NU * 8, :].reshape(NU, 8, LANES)], axis=1).astype(BF)
 
 
 def time_copies_kernel(got, inv, fwd, marks, out, rows, turn):
-    rows[...] = got[...].astype(F32).reshape(NF * 8, LANES)
+    rows[: NF * 8, :] = got[...].astype(F32).reshape(NF * 8, LANES)
     every = []
     for p in range(2):
         parts = []
@@ -305,7 +307,7 @@
             for half in range(2):
                 slab = spec[NG * part : NG * (part + 1), LANES * half : LANES * (half + 1)]
                 turn[pl.ds(4 * p + 2 * part + half, NG, stride=8), :] = slab
-    message = turn[...].reshape(NG, 8, LANES).astype(BF)
+    message = turn[: NG * 8, :].reshape(NG, 8, LANES).astype(BF)
     for z in range(NZ):
         out[:, z] = message
 
@@ -334,7 +336,7 @@
                     at = (x * NZ + z) * 16 + 2 * part + half
                     row = POINTS * part + 4 * x
                     turn[pl.ds(at, 4, stride=4), :] = block[row : row + 4, LANES * half : LANES * (half + 1)]
-    out[...] = turn[...].reshape(NX * NZ, 16, LANES).astype(BF)
+    out[...] = turn[: NX * NZ * 16, :].reshape(NX * NZ, 16, LANES).astype(BF)
 
 
 def last_corr_kernel(got, mat_re, mat_im, out):
@@ -366,7 +368,7 @@
 
 
 def keep_own(spectra, inv, marks):
-    t = iota((POINTS * NI, LANES), 1)
+    t = iota((spectra.shape[0], LANES), 1)
     trace = [nt(spectra, inv[a:b]) for a, b in ((0, CUT), (TIMES, TIMES + KEPT - CUT))]
     trace = jnp.concatenate(trace, axis=1)
     pieces = [trace[:, LANES * n : LANES * (n + 1)] for n in range(KEPT // LANES)]
@@ -377,17 +379,6 @@
 
 
 def last_kernel(got, tail, inv, marks, focus, plus_out, minus_out, plus, minus, spectra, sems):
-    rows = got[...].astype(F32).reshape(8 * NA, LANES).T.astype(BF)
-    m, k = grid(8 * NA, LANES)
-    own = jnp.zeros((POINTS * NI, LANES), F32)
-    for part in range(2):
-        place = hot(((m & 7) < NX) & (k == ((m & 7) << 5) + 16 * part + (m >> 3)))
-        own = own + nn(rows[NF * part : NF * (part + 1)], place)
-    trace = keep_own(own.astype(BF), inv[...], marks[...])
-    for p in range(POINTS):
-        plus[p] = (focus[p].astype(F32) + trace[NI * p : NI * (p + 1)]).astype(BF)
-    first = pltpu.make_async_copy(plus, plus_out, sems.at[0])
-    first.start()
     own = []
     for x in range(NX):
         both = [sum(tail[4 * x + 2 * c + w].astype(F32)[16:] for w in range(NW)) for c in range(NC)]
@@ -398,13 +389,25 @@
     own = [nn(own, hot(same & (((n >> 5) & 3) == p))) for p in range(4)]
     for p in range(POINTS):
         spectra[NI * p : NI * (p + 1), :] = own[p & 3][NI * (p >> 2) : NI * ((p >> 2) + 1)]
-    trace = keep_own(spectra[...].astype(BF), inv[...], marks[...])
+    rows = got[...].astype(F32).reshape(8 * NA, LANES).T.astype(BF)
+    m, k = grid(8 * NA, LANES)
+    own = jnp.zeros((POINTS * NI, LANES), F32)
+    for part in range(2):
+        place = hot(((m & 7) < NX) & (k == ((m & 7) << 5) + 16 * part + (m >> 3)))
+        own = own + nn(rows[NF * part : NF * (part + 1)], place)
+    own = jnp.concatenate([own, spectra[: POINTS * NI, :]], axis=0).astype(BF)
+    trace = keep_own(own, inv[...], jnp.concatenate([marks[...], marks[...]], axis=0))
     for p in range(POINTS):
-        minus[p] = trace[NI * p : NI * (p + 1)].astype(BF)
-    second = pltpu.make_async_copy(minus, minus_out, sems.at[1])
-    second.start()
-    first.wait()
-    second.wait()
+        plus[p] = (focus[p].astype(F32) + trace[NI * p : NI * (p + 1)]).astype(BF)
+    copies = [pltpu.make_async_copy(plus, plus_out, sems.at[0])]
+    copies[0].start()
+    for p in range(POINTS):
+        at = NI * (POINTS + p)
+        minus[p] = trace[at : at + NI].astype(BF)
+    copies.append(pltpu.make_async_copy(minus, minus_out, sems.at[1]))
+    copies[1].start()
+    for copy in copies:
+        copy.wait()
 
 
 def call(kernel, outs, scratch=(), scalars=0, far=0, copies=0, far_outs=0):
@@ -444,7 +447,7 @@
     forward, wide, inverse = base_tables()
     own = (POINTS, NI, NT)
 
-    scratch = [((1, NF), I32), ((NI, POINTS), I32), (own, BF), ((NF, 2 * NT), BF), ((POINTS * NI, NT), F32)]
+    scratch = [((1, NF), I32), ((NI, POINTS), I32), (own, BF), ((NF, 2 * NT), BF), ((POINTS * NI + 8, NT), F32)]
     run = call(start_kernel, ((NA, 8, LANES), BF), scratch, far=4, copies=4)
     got = exchange(run(bins, onset, focus_start, wide), ("v", "w", "c"))
     outs = [((8, LANES), I32), ((TIMES + KEPT - CUT, LANES), BF), ((OWN_TIMES, 2 * NA), BF), ((2 * NG, CUT), BF), ((2 * NU, CUT), BF)]
@@ -452,37 +455,37 @@
     scratch = [((1, NF), I32), ((NI, POINTS), I32), ((2 * NF, NT), BF), ((KEPT, LANES), BF)]
     run = call(tables_kernel, outs, scratch, scalars=1, far=6, copies=6)
     place, inv, own_inv, fwd, own_fwd, kept, *mats = run(where, bins, onset, forward, inverse, *mats)
-    send = call(middle_kernel, ((NX, NZ, POINTS + 8, LANES), BF), [((8 * NA, LANES), F32)])(got, fwd)
+    send = call(middle_kernel, ((NX, NZ, POINTS + 8, LANES), BF), [((8 * NA + 8, LANES), F32)])(got, fwd)
     got = exchange(send.reshape(NX * NZ, POINTS + 8, LANES), ("x", "z"))
-    outs = [((NY, NC, 16, LANES), BF), ((2 * POINTS, COLS), BF), ((8, LANES), I32), ((4, LANES), I32)]
+    outs = [((NY, NC, 16, LANES), BF), ((2 * POINTS, COLS), BF), ((8, LANES), I32), ((8, LANES), I32)]
     scratch = [((NX * NZ * (POINTS + 8), LANES), F32)]
     send, first, own_marks, marks = call(first_conv_kernel, outs, scratch)(place, got, *mats)
     for step in range(ITERS):
         got = exchange(send.reshape(NA, 16, LANES), ("v", "w", "c"))
-        scratch = [((NA * 16, LANES), F32), ((NU * 16, LANES), F32)]
+        scratch = [((NA * 16 + 16, LANES), F32), ((NU * 16 + 16, LANES), F32)]
         tables = (own_inv, own_fwd, own_marks)
         if step == ITERS - 1:
-            scratch = scratch + [((NU * 8, LANES), F32)]
+            scratch = scratch + [((NU * 8 + 8, LANES), F32)]
             send = call(last_time_kernel, ((NU, 24, LANES), BF), scratch)(got, *tables, place)
             got = exchange(send, ("x", "c", "w"))
             break
         send = call(time_kernel, ((NU, 16, LANES), BF), scratch)(got, *tables)
         got = exchange(send, ("x", "c", "w"))
-        send = call(corr_kernel, ((NX * NZ, 16, LANES), BF), [((NX * NZ * 16, LANES), F32)])(got, *mats)
+        send = call(corr_kernel, ((NX * NZ, 16, LANES), BF), [((NX * NZ * 16 + 32, LANES), F32)])(got, *mats)
         got = exchange(send, ("x", "z"))
         send = call(sum_kernel, ((NY, NC, NX * 8, LANES), BF))(got)
         got = exchange(send.reshape(NA, NX * 8, LANES), ("v", "w", "c"))
-        scratch = [((NF * 8, LANES), F32), ((NG * 8, LANES), F32)]
+        scratch = [((NF * 8 + 32, LANES), F32), ((NG * 8 + 8, LANES), F32)]
         send = call(time_copies_kernel, ((NG, NZ, 8, LANES), BF), scratch)(got, inv, fwd, marks)
         got = exchange(send.reshape(NG * NZ, 8, LANES), ("x", "c", "z"))
-        scratch = [((NG * NZ * 8, LANES), F32), ((2 * POINTS * COLS // LANES, LANES), F32)]
+        scratch = [((NG * NZ * 8 + 64, LANES), F32), ((2 * POINTS * COLS // LANES + 16, LANES), F32)]
         send = call(next_conv_kernel, ((NY, NC, 16, LANES), BF), scratch)(got, first, *mats)
     tail = got
     send = call(last_corr_kernel, ((NX, NZ, POINTS, LANES), BF))(got, *mats)
     got = exchange(send.reshape(NX * NZ, POINTS, LANES), ("x", "z")).reshape(NX, NZ, POINTS, LANES)
     send = call(last_sum_kernel, ((NA, 8, LANES), BF))(got)
     got = exchange(send, ("v", "w", "c"))
-    scratch = [(own, BF), (own, BF), ((POINTS * NI, LANES), F32)]
+    scratch = [(own, BF), (own, BF), ((POINTS * NI + 8, LANES), F32)]
     run = call(last_kernel, [(own, BF), (own, BF)], scratch, copies=2, far_outs=2)
     focus_plus, focus_minus = run(got, tail, inv, kept, focus_start)
     return (focus_plus, focus_minus)

time: 156 us -> 156 us (level)
  no operation moved by 1% of the time
where the time goes in v7:
time: 156 us
  blocking collectives  129 us (83%)
  Pallas kernels  11.1 us (7%)
  starting transfers between devices  10.2 us (7%)
  waiting for transfers between devices  4.86 us (3%)
    all_to_all x10, blocking collectives, exchange(): return lax.all_to_all(values, axes, 0, 0, tiled=True)  129 us
    pallas_call x13, Pallas kernels, run(): pl.pallas_call(kernel, out_shape=shapes, in_specs=[pl.BlockSpec(memory_sp...  11.1 us
    all_to_all x1, starting transfers between devices, exchange(): return lax.all_to_all(values, axes, 0, 0, tiled=True)  10.2 us
    all_to_all x1, waiting for transfers between devices, exchange(): return lax.all_to_all(values, axes, 0, 0, tiled=True)  4.86 us
  transfers between devices with their start and end apart: 1, of which 1 were waited for; matrix products, arithmetic and copies ran while one was open for 0% of the time, Pallas kernels for 2%

profile of v7, /device:TPU:1, one launch (start us, length us, event | category | flops | bytes accessed | tf_op | source)
XLA Modules:
  0.0 155.6 jit_solution(29944419344566369)
XLA Ops:
  0.6 2.1 %shard_map.96 = bf16[16,8,128]{2,1,0:T(8,128)(2,1)} custom-call(s32[1,64]{1,0:T(1,128)} %bitcast.26, s32[4,16]{1,0:T(4,128)} %bitcast.24, bf16[16,4,1024]{2,1,0:T(4,128)(2,1)} %focus.1, bf16[64,2048]{1,0:T(8,128)(2,1)} %constant.29.clone.base_in), custom_call_target="tpu_custom_call" | custom-call | tf_op jit(solution)/shard_map/pallas_call | solution.py:424
  2.7 10.2 %all-to-all-start = ((bf16[16,8,128]{2,1,0:T(8,128)(2,1)}), bf16[16,8,128]{2,1,0:T(8,128)(2,1)S(1)}, u32[]{:S(2)}, u32[]{:S(2)}) async-start(bf16[16,8,128]{2,1,0:T(8,128)(2,1)} %shard_map.96), calls=%async_computation | async-start | bytes 65536 | tf_op jit(solution)/shard_map/all_to_all | solution.py:439
  12.9 0.1 pad_add_fusion.where
  13.0 2.5 %shard_map.95 = (s32[8,128]{1,0:T(8,128)S(1)}, bf16[800,128]{1,0:T(8,128)(2,1)S(1)}, bf16[576,32]{1,0:T(8,128)(2,1)S(1)}, bf16[16,512]{1,0:T(8,128)(2,1)S(1)}, b...) custom-call(s32[4]{0:T(128)S(1)} %pad_add_fusion.where, ...), custom_call_target="tpu_custom_call" | custom-call | tf_op jit(solution)/shard_map/pallas_call | solution.py:424
  15.5 4.9 %all-to-all-done.got = bf16[16,8,128]{2,1,0:T(8,128)(2,1)S(1)} async-done(((bf16[16,8,128]{2,1,0:T(8,128)(2,1)}), bf16[16,8,128]{2,1,0:T(8,128)(2,1)S(1)}, u32[]{:S(2)}, u32[]{:S(2)}) %all-to-all-start) | async-done | bytes 32800 | tf_op jit(solution)/shard_map/all_to_all | solution.py:439
  20.4 0.3 shard_map.97
  20.7 20.4 %all_to_all.55.got = bf16[32,24,128]{2,1,0:T(8,128)(2,1)S(1)} all-to-all(bf16[32,24,128]{2,1,0:T(8,128)(2,1)S(1)} %bitcast.15), channel_id=1, replica_groups=mesh['x'=4,'v'=4,'w'=2,'c'=2,'z'=8] {'x','z'}, dimensions={0} | all-to-all | bytes 393216 | tf_op jit(solution)/shard_map/all_to_all | solution.py:439
  41.2 0.7 shard_map.98
  41.9 13.2 %all_to_all.56.got = bf16[16,16,128]{2,1,0:T(8,128)(2,1)S(1)} all-to-all(bf16[16,16,128]{2,1,0:T(8,128)(2,1)S(1)} %bitcast.21), channel_id=1, replica_groups=mesh['x'=4,'v'=4,'w'=2,'c'=2,'z'=8] {'v','w','c'}, dimensions={0} | all-to-all | bytes 131072 | tf_op jit(solution)/shard_map/all_to_all | solution.py:439
  55.1 0.7 shard_map.99
  55.8 8.9 %all_to_all.57.got = bf16[16,16,128]{2,1,0:T(8,128)(2,1)S(1)} all-to-all(bf16[16,16,128]{2,1,0:T(8,128)(2,1)S(1)} %shard_map.99), channel_id=1, replica_groups=mesh['x'=4,'v'=4,'w'=2,'c'=2,'z'=8] {'x','c','w'}, dimensions={0} | all-to-all | bytes 131072 | tf_op jit(solution)/shard_map/all_to_all | solution.py:439
  64.6 0.5 shard_map.100
  65.1 12.4 %all_to_all.58.got = bf16[32,16,128]{2,1,0:T(8,128)(2,1)S(1)} all-to-all(bf16[32,16,128]{2,1,0:T(8,128)(2,1)S(1)} %shard_map.100), channel_id=1, replica_groups=mesh['x'=4,'v'=4,'w'=2,'c'=2,'z'=8] {'x','z'}, dimensions={0} | all-to-all | bytes 262144 | tf_op jit(solution)/shard_map/all_to_all | solution.py:439
  77.6 14.3 %all_to_all.59.got = bf16[16,32,128]{2,1,0:T(8,128)(2,1)S(1)} all-to-all(bf16[16,32,128]{2,1,0:T(8,128)(2,1)S(1)} %bitcast.18), channel_id=1, replica_groups=mesh['x'=4,'v'=4,'w'=2,'c'=2,'z'=8] {'v','w','c'}, dimensions={0} | all-to-all | bytes 262144 | tf_op jit(solution)/shard_map/all_to_all | solution.py:439
  91.9 0.6 shard_map.102
  92.5 13.8 %all_to_all.60.got = bf16[64,8,128]{2,1,0:T(8,128)(2,1)S(1)} all-to-all(bf16[64,8,128]{2,1,0:T(8,128)(2,1)S(1)} %bitcast.19), channel_id=1, replica_groups=mesh['x'=4,'v'=4,'w'=2,'c'=2,'z'=8] {'x','c','z'}, dimensions={0} | all-to-all | bytes 262144 | tf_op jit(solution)/shard_map/all_to_all | solution.py:439
  106.3 0.8 shard_map.103
  107.1 11.8 %all_to_all.61.got = bf16[16,16,128]{2,1,0:T(8,128)(2,1)S(1)} all-to-all(bf16[16,16,128]{2,1,0:T(8,128)(2,1)S(1)} %bitcast.20), channel_id=1, replica_groups=mesh['x'=4,'v'=4,'w'=2,'c'=2,'z'=8] {'v','w','c'}, dimensions={0} | all-to-all | bytes 131072 | tf_op jit(solution)/shard_map/all_to_all | solution.py:439
  118.8 0.7 shard_map.104
  119.6 9.2 %all_to_all.62.got.tail = bf16[16,24,128]{2,1,0:T(8,128)(2,1)S(1)} all-to-all(bf16[16,24,128]{2,1,0:T(8,128)(2,1)S(1)} %shard_map.104), channel_id=1, replica_groups=mesh['x'=4,'v'=4,'w'=2,'c'=2,'z'=8] {'x','c','w'}, dimensions={0} | all-to-all | bytes 196608 | tf_op jit(solution)/shard_map/all_to_all | solution.py:439
  128.8 0.5 shard_map.105
  129.3 12.1 %all_to_all.63 = bf16[32,16,128]{2,1,0:T(8,128)(2,1)S(1)} all-to-all(bf16[32,16,128]{2,1,0:T(8,128)(2,1)S(1)} %bitcast.16), channel_id=1, replica_groups=mesh['x'=4,'v'=4,'w'=2,'c'=2,'z'=8] {'x','z'}, dimensions={0} | all-to-all | bytes 262144 | tf_op jit(solution)/shard_map/all_to_all | solution.py:439
  141.4 0.0 copy-start
  141.4 0.3 shard_map.106
  141.8 12.5 %all_to_all.64.got = bf16[16,8,128]{2,1,0:T(8,128)(2,1)S(1)} all-to-all(bf16[16,8,128]{2,1,0:T(8,128)(2,1)S(1)} %shard_map.106), channel_id=1, replica_groups=mesh['x'=4,'v'=4,'w'=2,'c'=2,'z'=8] {'v','w','c'}, dimensions={0} | all-to-all | bytes 65536 | tf_op jit(solution)/shard_map/all_to_all | solution.py:439
  154.3 0.0 copy-done
  154.3 1.3 shard_map.107
  (1 shorter events, 0.0 us)
Async XLA Ops:
  2.7 17.7 %all-to-all-start = ((bf16[16,8,128]{2,1,0:T(8,128)(2,1)}), bf16[16,8,128]{2,1,0:T(8,128)(2,1)S(1)}, u32[]{:S(2)}, u32[]{:S(2)}) async-start(bf16[16,8,128]{2,1,0:T(8,128)(2,1)} %shard_map.96), calls=%async_computation | async-start | bytes 65536 | tf_op jit(solution)/shard_map/all_to_all | solution.py:439
  141.4 12.9 %copy-start = (bf16[16,4,1024]{2,1,0:T(4,128)(2,1)S(1)}, bf16[16,4,1024]{2,1,0:T(4,128)(2,1)}, u32[]{:S(2)}) copy-start(bf16[16,4,1024]{2,1,0:T(4,128)(2,1)} %focus.1) | copy-start | bytes 393220

commit v8 on v7

--- a/solution.py
+++ b/solution.py
@@ -368,7 +368,7 @@
 
 
 def keep_own(spectra, inv, marks):
-    t = iota((spectra.shape[0], LANES), 1)
+    t = iota((POINTS * NI, LANES), 1)
     trace = [nt(spectra, inv[a:b]) for a, b in ((0, CUT), (TIMES, TIMES + KEPT - CUT))]
     trace = jnp.concatenate(trace, axis=1)
     pieces = [trace[:, LANES * n : LANES * (n + 1)] for n in range(KEPT // LANES)]
@@ -379,6 +379,17 @@
 
 
 def last_kernel(got, tail, inv, marks, focus, plus_out, minus_out, plus, minus, spectra, sems):
+    rows = got[...].astype(F32).reshape(8 * NA, LANES).T.astype(BF)
+    m, k = grid(8 * NA, LANES)
+    own = jnp.zeros((POINTS * NI, LANES), F32)
+    for part in range(2):
+        place = hot(((m & 7) < NX) & (k == ((m & 7) << 5) + 16 * part + (m >> 3)))
+        own = own + nn(rows[NF * part : NF * (part + 1)], place)
+    trace = keep_own(own.astype(BF), inv[...], marks[...])
+    for p in range(POINTS):
+        plus[p] = (focus[p].astype(F32) + trace[NI * p : NI * (p + 1)]).astype(BF)
+    first = pltpu.make_async_copy(plus, plus_out, sems.at[0])
+    first.start()
     own = []
     for x in range(NX):
         both = [sum(tail[4 * x + 2 * c + w].astype(F32)[16:] for w in range(NW)) for c in range(NC)]
@@ -389,25 +400,13 @@
     own = [nn(own, hot(same & (((n >> 5) & 3) == p))) for p in range(4)]
     for p in range(POINTS):
         spectra[NI * p : NI * (p + 1), :] = own[p & 3][NI * (p >> 2) : NI * ((p >> 2) + 1)]
-    rows = got[...].astype(F32).reshape(8 * NA, LANES).T.astype(BF)
-    m, k = grid(8 * NA, LANES)
-    own = jnp.zeros((POINTS * NI, LANES), F32)
-    for part in range(2):
-        place = hot(((m & 7) < NX) & (k == ((m & 7) << 5) + 16 * part + (m >> 3)))
-        own = own + nn(rows[NF * part : NF * (part + 1)], place)
-    own = jnp.concatenate([own, spectra[: POINTS * NI, :]], axis=0).astype(BF)
-    trace = keep_own(own, inv[...], jnp.concatenate([marks[...], marks[...]], axis=0))
+    trace = keep_own(spectra[: POINTS * NI, :].astype(BF), inv[...], marks[...])
     for p in range(POINTS):
-        plus[p] = (focus[p].astype(F32) + trace[NI * p : NI * (p + 1)]).astype(BF)
-    copies = [pltpu.make_async_copy(plus, plus_out, sems.at[0])]
-    copies[0].start()
-    for p in range(POINTS):
-        at = NI * (POINTS + p)
-        minus[p] = trace[at : at + NI].astype(BF)
-    copies.append(pltpu.make_async_copy(minus, minus_out, sems.at[1]))
-    copies[1].start()
-    for copy in copies:
-        copy.wait()
+        minus[p] = trace[NI * p : NI * (p + 1)].astype(BF)
+    second = pltpu.make_async_copy(minus, minus_out, sems.at[1])
+    second.start()
+    first.wait()
+    second.wait()
 
 
 def call(kernel, outs, scratch=(), scalars=0, far=0, copies=0, far_outs=0):

time: 156 us -> 156 us (level)
  no operation moved by 1% of the time
where the time goes in v8:
time: 156 us
  blocking collectives  129 us (83%)
  Pallas kernels  11.2 us (7%)
  starting transfers between devices  10.2 us (7%)
  waiting for transfers between devices  4.86 us (3%)
    all_to_all x10, blocking collectives, exchange(): return lax.all_to_all(values, axes, 0, 0, tiled=True)  129 us
    pallas_call x13, Pallas kernels, run(): pl.pallas_call(kernel, out_shape=shapes, in_specs=[pl.BlockSpec(memory_sp...  11.2 us
    all_to_all x1, starting transfers between devices, exchange(): return lax.all_to_all(values, axes, 0, 0, tiled=True)  10.2 us
    all_to_all x1, waiting for transfers between devices, exchange(): return lax.all_to_all(values, axes, 0, 0, tiled=True)  4.86 us
  transfers between devices with their start and end apart: 1, of which 1 were waited for; matrix products, arithmetic and copies ran while one was open for 0% of the time, Pallas kernels for 2%

profile of v8, /device:TPU:1, one launch (start us, length us, event | category | flops | bytes accessed | tf_op | source)
XLA Modules:
  0.0 155.7 jit_solution(1609222396377279082)
XLA Ops:
  0.6 2.1 %shard_map.96 = bf16[16,8,128]{2,1,0:T(8,128)(2,1)} custom-call(s32[1,64]{1,0:T(1,128)} %bitcast.26, s32[4,16]{1,0:T(4,128)} %bitcast.24, bf16[16,4,1024]{2,1,0:T(4,128)(2,1)} %focus.1, bf16[64,2048]{1,0:T(8,128)(2,1)} %constant.29.clone.base_in), custom_call_target="tpu_custom_call" | custom-call | tf_op jit(solution)/shard_map/pallas_call | solution.py:423
  2.7 10.2 %all-to-all-start = ((bf16[16,8,128]{2,1,0:T(8,128)(2,1)}), bf16[16,8,128]{2,1,0:T(8,128)(2,1)S(1)}, u32[]{:S(2)}, u32[]{:S(2)}) async-start(bf16[16,8,128]{2,1,0:T(8,128)(2,1)} %shard_map.96), calls=%async_computation | async-start | bytes 65536 | tf_op jit(solution)/shard_map/all_to_all | solution.py:438
  12.9 0.1 pad_add_fusion.where
  13.0 2.5 %shard_map.95 = (s32[8,128]{1,0:T(8,128)S(1)}, bf16[800,128]{1,0:T(8,128)(2,1)S(1)}, bf16[576,32]{1,0:T(8,128)(2,1)S(1)}, bf16[16,512]{1,0:T(8,128)(2,1)S(1)}, b...) custom-call(s32[4]{0:T(128)S(1)} %pad_add_fusion.where, ...), custom_call_target="tpu_custom_call" | custom-call | tf_op jit(solution)/shard_map/pallas_call | solution.py:423
  15.5 4.9 %all-to-all-done.got = bf16[16,8,128]{2,1,0:T(8,128)(2,1)S(1)} async-done(((bf16[16,8,128]{2,1,0:T(8,128)(2,1)}), bf16[16,8,128]{2,1,0:T(8,128)(2,1)S(1)}, u32[]{:S(2)}, u32[]{:S(2)}) %all-to-all-start) | async-done | bytes 32800 | tf_op jit(solution)/shard_map/all_to_all | solution.py:438
  20.4 0.3 shard_map.97
  20.7 20.4 %all_to_all.55.got = bf16[32,24,128]{2,1,0:T(8,128)(2,1)S(1)} all-to-all(bf16[32,24,128]{2,1,0:T(8,128)(2,1)S(1)} %bitcast.15), channel_id=1, replica_groups=mesh['x'=4,'v'=4,'w'=2,'c'=2,'z'=8] {'x','z'}, dimensions={0} | all-to-all | bytes 393216 | tf_op jit(solution)/shard_map/all_to_all | solution.py:438
  41.2 0.7 shard_map.98
  41.9 13.2 %all_to_all.56.got = bf16[16,16,128]{2,1,0:T(8,128)(2,1)S(1)} all-to-all(bf16[16,16,128]{2,1,0:T(8,128)(2,1)S(1)} %bitcast.21), channel_id=1, replica_groups=mesh['x'=4,'v'=4,'w'=2,'c'=2,'z'=8] {'v','w','c'}, dimensions={0} | all-to-all | bytes 131072 | tf_op jit(solution)/shard_map/all_to_all | solution.py:438
  55.1 0.7 shard_map.99
  55.8 8.9 %all_to_all.57.got = bf16[16,16,128]{2,1,0:T(8,128)(2,1)S(1)} all-to-all(bf16[16,16,128]{2,1,0:T(8,128)(2,1)S(1)} %shard_map.99), channel_id=1, replica_groups=mesh['x'=4,'v'=4,'w'=2,'c'=2,'z'=8] {'x','c','w'}, dimensions={0} | all-to-all | bytes 131072 | tf_op jit(solution)/shard_map/all_to_all | solution.py:438
  64.6 0.5 shard_map.100
  65.1 12.4 %all_to_all.58.got = bf16[32,16,128]{2,1,0:T(8,128)(2,1)S(1)} all-to-all(bf16[32,16,128]{2,1,0:T(8,128)(2,1)S(1)} %shard_map.100), channel_id=1, replica_groups=mesh['x'=4,'v'=4,'w'=2,'c'=2,'z'=8] {'x','z'}, dimensions={0} | all-to-all | bytes 262144 | tf_op jit(solution)/shard_map/all_to_all | solution.py:438
  77.6 14.3 %all_to_all.59.got = bf16[16,32,128]{2,1,0:T(8,128)(2,1)S(1)} all-to-all(bf16[16,32,128]{2,1,0:T(8,128)(2,1)S(1)} %bitcast.18), channel_id=1, replica_groups=mesh['x'=4,'v'=4,'w'=2,'c'=2,'z'=8] {'v','w','c'}, dimensions={0} | all-to-all | bytes 262144 | tf_op jit(solution)/shard_map/all_to_all | solution.py:438
  91.9 0.6 shard_map.102
  92.5 13.8 %all_to_all.60.got = bf16[64,8,128]{2,1,0:T(8,128)(2,1)S(1)} all-to-all(bf16[64,8,128]{2,1,0:T(8,128)(2,1)S(1)} %bitcast.19), channel_id=1, replica_groups=mesh['x'=4,'v'=4,'w'=2,'c'=2,'z'=8] {'x','c','z'}, dimensions={0} | all-to-all | bytes 262144 | tf_op jit(solution)/shard_map/all_to_all | solution.py:438
  106.3 0.8 shard_map.103
  107.1 11.8 %all_to_all.61.got = bf16[16,16,128]{2,1,0:T(8,128)(2,1)S(1)} all-to-all(bf16[16,16,128]{2,1,0:T(8,128)(2,1)S(1)} %bitcast.20), channel_id=1, replica_groups=mesh['x'=4,'v'=4,'w'=2,'c'=2,'z'=8] {'v','w','c'}, dimensions={0} | all-to-all | bytes 131072 | tf_op jit(solution)/shard_map/all_to_all | solution.py:438
  118.8 0.7 shard_map.104
  119.6 9.2 %all_to_all.62.got.tail = bf16[16,24,128]{2,1,0:T(8,128)(2,1)S(1)} all-to-all(bf16[16,24,128]{2,1,0:T(8,128)(2,1)S(1)} %shard_map.104), channel_id=1, replica_groups=mesh['x'=4,'v'=4,'w'=2,'c'=2,'z'=8] {'x','c','w'}, dimensions={0} | all-to-all | bytes 196608 | tf_op jit(solution)/shard_map/all_to_all | solution.py:438
  128.8 0.5 shard_map.105
  129.3 12.1 %all_to_all.63 = bf16[32,16,128]{2,1,0:T(8,128)(2,1)S(1)} all-to-all(bf16[32,16,128]{2,1,0:T(8,128)(2,1)S(1)} %bitcast.16), channel_id=1, replica_groups=mesh['x'=4,'v'=4,'w'=2,'c'=2,'z'=8] {'x','z'}, dimensions={0} | all-to-all | bytes 262144 | tf_op jit(solution)/shard_map/all_to_all | solution.py:438
  141.4 0.0 copy-start
  141.4 0.3 shard_map.106
  141.8 12.5 %all_to_all.64.got = bf16[16,8,128]{2,1,0:T(8,128)(2,1)S(1)} all-to-all(bf16[16,8,128]{2,1,0:T(8,128)(2,1)S(1)} %shard_map.106), channel_id=1, replica_groups=mesh['x'=4,'v'=4,'w'=2,'c'=2,'z'=8] {'v','w','c'}, dimensions={0} | all-to-all | bytes 65536 | tf_op jit(solution)/shard_map/all_to_all | solution.py:438
  154.3 0.0 copy-done
  154.3 1.3 shard_map.107
  (1 shorter events, 0.0 us)
Async XLA Ops:
  2.7 17.7 %all-to-all-start = ((bf16[16,8,128]{2,1,0:T(8,128)(2,1)}), bf16[16,8,128]{2,1,0:T(8,128)(2,1)S(1)}, u32[]{:S(2)}, u32[]{:S(2)}) async-start(bf16[16,8,128]{2,1,0:T(8,128)(2,1)} %shard_map.96), calls=%async_computation | async-start | bytes 65536 | tf_op jit(solution)/shard_map/all_to_all | solution.py:438
  141.4 12.9 %copy-start = (bf16[16,4,1024]{2,1,0:T(4,128)(2,1)S(1)}, bf16[16,4,1024]{2,1,0:T(4,128)(2,1)}, u32[]{:S(2)}) copy-start(bf16[16,4,1024]{2,1,0:T(4,128)(2,1)} %focus.1) | copy-start | bytes 393220

commit v9 on v8

--- a/solution.py
+++ b/solution.py
@@ -363,8 +363,10 @@
     turned = nn(hot(((m >> 2) & 15) == p), total)
     m, n = grid(LANES, NX * LANES)
     turned = jnp.where(((n & 3) == (m & 3)) & (((n >> 6) & 1) == (m >> 6)), turned, 0.0).astype(BF)
-    sent = nt(hot(((m & 7) == (n >> 7)) & ((m >> 3) == ((n >> 2) & 15))), turned)
-    out[...] = sent.reshape(NA, 8, LANES).astype(BF)
+    m, n = grid(NX * NA, NX * LANES)
+    sent = nt(hot(((m & 3) == (n >> 7)) & ((m >> 2) == ((n >> 2) & 15))), turned)
+    for a in range(NA):
+        out[a] = sent[NX * a : NX * (a + 1)].astype(BF)
 
 
 def keep_own(spectra, inv, marks):
@@ -378,12 +380,14 @@
     return jnp.concatenate([pieces[4], *front, none, none, *back, pieces[5]], axis=1)
 
 
-def last_kernel(got, tail, inv, marks, focus, plus_out, minus_out, plus, minus, spectra, sems):
-    rows = got[...].astype(F32).reshape(8 * NA, LANES).T.astype(BF)
-    m, k = grid(8 * NA, LANES)
+def last_kernel(got, tail, inv, marks, focus, plus_out, minus_out, plus, minus, spectra, arrived, sems):
+    for a in range(NA):
+        arrived[NX * a : NX * (a + 1), :] = got[a].astype(F32)
+    rows = arrived[: NX * NA, :].T.astype(BF)
+    m, k = grid(NX * NA, LANES)
     own = jnp.zeros((POINTS * NI, LANES), F32)
     for part in range(2):
-        place = hot(((m & 7) < NX) & (k == ((m & 7) << 5) + 16 * part + (m >> 3)))
+        place = hot(k == ((m & 3) << 5) + 16 * part + (m >> 2))
         own = own + nn(rows[NF * part : NF * (part + 1)], place)
     trace = keep_own(own.astype(BF), inv[...], marks[...])
     for p in range(POINTS):
@@ -482,9 +486,9 @@
     tail = got
     send = call(last_corr_kernel, ((NX, NZ, POINTS, LANES), BF))(got, *mats)
     got = exchange(send.reshape(NX * NZ, POINTS, LANES), ("x", "z")).reshape(NX, NZ, POINTS, LANES)
-    send = call(last_sum_kernel, ((NA, 8, LANES), BF))(got)
+    send = call(last_sum_kernel, ((NA, NX, LANES), BF))(got)
     got = exchange(send, ("v", "w", "c"))
-    scratch = [(own, BF), (own, BF), ((POINTS * NI + 8, LANES), F32)]
+    scratch = [(own, BF), (own, BF), ((POINTS * NI + 8, LANES), F32), ((NX * NA + 8, LANES), F32)]
     run = call(last_kernel, [(own, BF), (own, BF)], scratch, copies=2, far_outs=2)
     focus_plus, focus_minus = run(got, tail, inv, kept, focus_start)
     return (focus_plus, focus_minus)

time: 156 us -> 156 us (level)
  no operation moved by 1% of the time
where the time goes in v9:
time: 156 us
  blocking collectives  129 us (83%)
  Pallas kernels  11.2 us (7%)
  starting transfers between devices  10.2 us (7%)
  waiting for transfers between devices  4.86 us (3%)
    all_to_all x10, blocking collectives, exchange(): return lax.all_to_all(values, axes, 0, 0, tiled=True)  129 us
    pallas_call x13, Pallas kernels, run(): pl.pallas_call(kernel, out_shape=shapes, in_specs=[pl.BlockSpec(memory_sp...  11.2 us
    all_to_all x1, starting transfers between devices, exchange(): return lax.all_to_all(values, axes, 0, 0, tiled=True)  10.2 us
    all_to_all x1, waiting for transfers between devices, exchange(): return lax.all_to_all(values, axes, 0, 0, tiled=True)  4.86 us
  transfers between devices with their start and end apart: 1, of which 1 were waited for; matrix products, arithmetic and copies ran while one was open for 0% of the time, Pallas kernels for 2%

profile of v9, /device:TPU:1, one launch (start us, length us, event | category | flops | bytes accessed | tf_op | source)
XLA Modules:
  0.0 155.6 jit_solution(6561688737891111793)
XLA Ops:
  0.6 2.1 %shard_map.96 = bf16[16,8,128]{2,1,0:T(8,128)(2,1)} custom-call(s32[1,64]{1,0:T(1,128)} %bitcast.26, s32[4,16]{1,0:T(4,128)} %bitcast.24, bf16[16,4,1024]{2,1,0:T(4,128)(2,1)} %focus.1, bf16[64,2048]{1,0:T(8,128)(2,1)} %constant.29.clone.base_in), custom_call_target="tpu_custom_call" | custom-call | tf_op jit(solution)/shard_map/pallas_call | solution.py:427
  2.7 10.2 %all-to-all-start = ((bf16[16,8,128]{2,1,0:T(8,128)(2,1)}), bf16[16,8,128]{2,1,0:T(8,128)(2,1)S(1)}, u32[]{:S(2)}, u32[]{:S(2)}) async-start(bf16[16,8,128]{2,1,0:T(8,128)(2,1)} %shard_map.96), calls=%async_computation | async-start | bytes 65536 | tf_op jit(solution)/shard_map/all_to_all | solution.py:442
  12.9 0.1 pad_add_fusion.where
  13.0 2.5 %shard_map.95 = (s32[8,128]{1,0:T(8,128)S(1)}, bf16[800,128]{1,0:T(8,128)(2,1)S(1)}, bf16[576,32]{1,0:T(8,128)(2,1)S(1)}, bf16[16,512]{1,0:T(8,128)(2,1)S(1)}, b...) custom-call(s32[4]{0:T(128)S(1)} %pad_add_fusion.where, ...), custom_call_target="tpu_custom_call" | custom-call | tf_op jit(solution)/shard_map/pallas_call | solution.py:427
  15.5 4.9 %all-to-all-done.got = bf16[16,8,128]{2,1,0:T(8,128)(2,1)S(1)} async-done(((bf16[16,8,128]{2,1,0:T(8,128)(2,1)}), bf16[16,8,128]{2,1,0:T(8,128)(2,1)S(1)}, u32[]{:S(2)}, u32[]{:S(2)}) %all-to-all-start) | async-done | bytes 32800 | tf_op jit(solution)/shard_map/all_to_all | solution.py:442
  20.4 0.3 shard_map.97
  20.7 20.4 %all_to_all.55.got = bf16[32,24,128]{2,1,0:T(8,128)(2,1)S(1)} all-to-all(bf16[32,24,128]{2,1,0:T(8,128)(2,1)S(1)} %bitcast.15), channel_id=1, replica_groups=mesh['x'=4,'v'=4,'w'=2,'c'=2,'z'=8] {'x','z'}, dimensions={0} | all-to-all | bytes 393216 | tf_op jit(solution)/shard_map/all_to_all | solution.py:442
  41.2 0.7 shard_map.98
  41.9 13.2 %all_to_all.56.got = bf16[16,16,128]{2,1,0:T(8,128)(2,1)S(1)} all-to-all(bf16[16,16,128]{2,1,0:T(8,128)(2,1)S(1)} %bitcast.21), channel_id=1, replica_groups=mesh['x'=4,'v'=4,'w'=2,'c'=2,'z'=8] {'v','w','c'}, dimensions={0} | all-to-all | bytes 131072 | tf_op jit(solution)/shard_map/all_to_all | solution.py:442
  55.1 0.7 shard_map.99
  55.8 8.9 %all_to_all.57.got = bf16[16,16,128]{2,1,0:T(8,128)(2,1)S(1)} all-to-all(bf16[16,16,128]{2,1,0:T(8,128)(2,1)S(1)} %shard_map.99), channel_id=1, replica_groups=mesh['x'=4,'v'=4,'w'=2,'c'=2,'z'=8] {'x','c','w'}, dimensions={0} | all-to-all | bytes 131072 | tf_op jit(solution)/shard_map/all_to_all | solution.py:442
  64.6 0.5 shard_map.100
  65.1 12.4 %all_to_all.58.got = bf16[32,16,128]{2,1,0:T(8,128)(2,1)S(1)} all-to-all(bf16[32,16,128]{2,1,0:T(8,128)(2,1)S(1)} %shard_map.100), channel_id=1, replica_groups=mesh['x'=4,'v'=4,'w'=2,'c'=2,'z'=8] {'x','z'}, dimensions={0} | all-to-all | bytes 262144 | tf_op jit(solution)/shard_map/all_to_all | solution.py:442
  77.6 14.3 %all_to_all.59.got = bf16[16,32,128]{2,1,0:T(8,128)(2,1)S(1)} all-to-all(bf16[16,32,128]{2,1,0:T(8,128)(2,1)S(1)} %bitcast.17), channel_id=1, replica_groups=mesh['x'=4,'v'=4,'w'=2,'c'=2,'z'=8] {'v','w','c'}, dimensions={0} | all-to-all | bytes 262144 | tf_op jit(solution)/shard_map/all_to_all | solution.py:442
  91.9 0.6 shard_map.102
  92.5 13.8 %all_to_all.60.got = bf16[64,8,128]{2,1,0:T(8,128)(2,1)S(1)} all-to-all(bf16[64,8,128]{2,1,0:T(8,128)(2,1)S(1)} %bitcast.19), channel_id=1, replica_groups=mesh['x'=4,'v'=4,'w'=2,'c'=2,'z'=8] {'x','c','z'}, dimensions={0} | all-to-all | bytes 262144 | tf_op jit(solution)/shard_map/all_to_all | solution.py:442
  106.3 0.8 shard_map.103
  107.1 11.8 %all_to_all.61.got = bf16[16,16,128]{2,1,0:T(8,128)(2,1)S(1)} all-to-all(bf16[16,16,128]{2,1,0:T(8,128)(2,1)S(1)} %bitcast.20), channel_id=1, replica_groups=mesh['x'=4,'v'=4,'w'=2,'c'=2,'z'=8] {'v','w','c'}, dimensions={0} | all-to-all | bytes 131072 | tf_op jit(solution)/shard_map/all_to_all | solution.py:442
  118.8 0.7 shard_map.104
  119.6 9.2 %all_to_all.62.got.tail = bf16[16,24,128]{2,1,0:T(8,128)(2,1)S(1)} all-to-all(bf16[16,24,128]{2,1,0:T(8,128)(2,1)S(1)} %shard_map.104), channel_id=1, replica_groups=mesh['x'=4,'v'=4,'w'=2,'c'=2,'z'=8] {'x','c','w'}, dimensions={0} | all-to-all | bytes 196608 | tf_op jit(solution)/shard_map/all_to_all | solution.py:442
  128.8 0.5 shard_map.105
  129.3 12.1 %all_to_all.63 = bf16[32,16,128]{2,1,0:T(8,128)(2,1)S(1)} all-to-all(bf16[32,16,128]{2,1,0:T(8,128)(2,1)S(1)} %bitcast.16), channel_id=1, replica_groups=mesh['x'=4,'v'=4,'w'=2,'c'=2,'z'=8] {'x','z'}, dimensions={0} | all-to-all | bytes 262144 | tf_op jit(solution)/shard_map/all_to_all | solution.py:442
  141.4 0.0 copy-start
  141.4 0.3 shard_map.106
  141.8 12.5 %all_to_all.64.got = bf16[16,4,128]{2,1,0:T(4,128)(2,1)S(1)} all-to-all(bf16[16,4,128]{2,1,0:T(4,128)(2,1)S(1)} %shard_map.106), channel_id=1, replica_groups=mesh['x'=4,'v'=4,'w'=2,'c'=2,'z'=8] {'v','w','c'}, dimensions={0} | all-to-all | bytes 32768 | tf_op jit(solution)/shard_map/all_to_all | solution.py:442
  154.2 0.0 copy-done
  154.2 1.3 shard_map.107
  (1 shorter events, 0.0 us)
Async XLA Ops:
  2.7 17.7 %all-to-all-start = ((bf16[16,8,128]{2,1,0:T(8,128)(2,1)}), bf16[16,8,128]{2,1,0:T(8,128)(2,1)S(1)}, u32[]{:S(2)}, u32[]{:S(2)}) async-start(bf16[16,8,128]{2,1,0:T(8,128)(2,1)} %shard_map.96), calls=%async_computation | async-start | bytes 65536 | tf_op jit(solution)/shard_map/all_to_all | solution.py:442
  141.4 12.8 %copy-start = (bf16[16,4,1024]{2,1,0:T(4,128)(2,1)S(1)}, bf16[16,4,1024]{2,1,0:T(4,128)(2,1)}, u32[]{:S(2)}) copy-start(bf16[16,4,1024]{2,1,0:T(4,128)(2,1)} %focus.1) | copy-start | bytes 393220

commit v10 on v9

--- a/solution.py
+++ b/solution.py
@@ -35,8 +35,7 @@
     forward = (rows * np.float32(1.0 / math.sqrt(NT))).astype(BF)
     inverse = (rows * np.float32(math.sqrt(2.0 / NF))).astype(BF)
     inverse = np.concatenate([inverse[:, a:b] for a, b in SPANS], axis=1)
-    wide = np.concatenate([forward[:NF], forward[NF:]], axis=1)
-    return forward, wide, np.ascontiguousarray(inverse.T)
+    return forward, np.ascontiguousarray(inverse.T)
 
 
 def iota(shape, dim):
@@ -77,25 +76,24 @@
 
 
 def start_kernel(bins_in, onset_in, focus_in, base_in, out, bins, onset, focus, base, flat, sems):
-    copies = fetch([(bins_in, bins), (onset_in, onset), (focus_in, focus), (base_in, base)], sems)
-    copies[0].wait()
+    copies = fetch([(focus_in, focus), (base_in, base), (bins_in, bins), (onset_in, onset)], sems)
+    copies[2].wait()
     m, j = grid(8 * NA, NF)
     place = hot(((m & 7) < NX) & (j == ((m & 7) << 4) + (m >> 3)))
     order = nt(place, slab_of_bin(bins[...])).astype(BF)
-    copies[1].wait()
+    copies[3].wait()
     p, lane = grid(POINTS, LANES)
     spread = hot((((lane >> 2) & 15) == p) & ((lane >> 6) == (p >> 3)))
     marks = nn((onset[...] - ONSET_MID).astype(F32).astype(BF), spread)
     i, lane = grid(NI, LANES)
     marks = jnp.where((lane & 3) == i, marks, 0.0).sum(axis=0, keepdims=True)
-    copies[2].wait()
+    copies[0].wait()
     for p in range(POINTS):
         flat[NI * p : NI * (p + 1), :] = focus[p].astype(F32)
     rows = flat[: POINTS * NI, :].astype(BF)
-    none = jnp.zeros_like(rows)
-    copies[3].wait()
-    spec = nt(base[:, :NT], jnp.concatenate([rows, none], axis=0))
-    spec = spec + nt(base[:, NT:], jnp.concatenate([none, rows], axis=0))
+    copies[1].wait()
+    spec = nt(base[...], rows)
+    spec = jnp.concatenate([spec[:NF], spec[NF:]], axis=1)
     sent = nn(order, spec.astype(BF))
     sent = jnp.where((iota((8 * NA, LANES), 0) & 7) == NX, marks, sent)
     out[...] = sent.reshape(NA, 8, LANES).astype(BF)
@@ -447,12 +445,12 @@
     where = jnp.stack([lax.axis_index(axis) for axis in ("x", ("v", "w"), "c", "z")]).astype(I32)
     bins = bins.reshape(1, NF)
     onset = onset.T
-    forward, wide, inverse = base_tables()
+    forward, inverse = base_tables()
     own = (POINTS, NI, NT)
 
-    scratch = [((1, NF), I32), ((NI, POINTS), I32), (own, BF), ((NF, 2 * NT), BF), ((POINTS * NI + 8, NT), F32)]
+    scratch = [((1, NF), I32), ((NI, POINTS), I32), (own, BF), ((2 * NF, NT), BF), ((POINTS * NI + 8, NT), F32)]
     run = call(start_kernel, ((NA, 8, LANES), BF), scratch, far=4, copies=4)
-    got = exchange(run(bins, onset, focus_start, wide), ("v", "w", "c"))
+    got = exchange(run(bins, onset, focus_start, forward), ("v", "w", "c"))
     outs = [((8, LANES), I32), ((TIMES + KEPT - CUT, LANES), BF), ((OWN_TIMES, 2 * NA), BF), ((2 * NG, CUT), BF), ((2 * NU, CUT), BF)]
     outs += [((POINTS * NI, LANES), I32), ((BLOCK, COLS), BF), ((BLOCK, COLS), BF)]
     scratch = [((1, NF), I32), ((NI, POINTS), I32), ((2 * NF, NT), BF), ((KEPT, LANES), BF)]

time: 156 us -> 156 us (level)
  no operation moved by 1% of the time
where the time goes in v10:
time: 156 us
  blocking collectives  129 us (83%)
  Pallas kernels  11.3 us (7%)
  starting transfers between devices  10.2 us (7%)
  waiting for transfers between devices  4.86 us (3%)
    all_to_all x10, blocking collectives, exchange(): return lax.all_to_all(values, axes, 0, 0, tiled=True)  129 us
    pallas_call x13, Pallas kernels, run(): pl.pallas_call(kernel, out_shape=shapes, in_specs=[pl.BlockSpec(memory_sp...  11.3 us
    all_to_all x1, starting transfers between devices, exchange(): return lax.all_to_all(values, axes, 0, 0, tiled=True)  10.2 us
    all_to_all x1, waiting for transfers between devices, exchange(): return lax.all_to_all(values, axes, 0, 0, tiled=True)  4.86 us
  transfers between devices with their start and end apart: 1, of which 1 were waited for; matrix products, arithmetic and copies ran while one was open for 0% of the time, Pallas kernels for 2%

profile of v10, /device:TPU:1, one launch (start us, length us, event | category | flops | bytes accessed | tf_op | source)
XLA Modules:
  0.0 155.7 jit_solution(16466255845803522832)
XLA Ops:
  0.6 2.2 %shard_map.87 = bf16[16,8,128]{2,1,0:T(8,128)(2,1)} custom-call(s32[1,64]{1,0:T(1,128)} %bitcast.26, s32[4,16]{1,0:T(4,128)} %bitcast.24, bf16[16,4,1024]{2,1,0:T(4,128)(2,1)} %focus.1, bf16[128,1024]{1,0:T(8,128)(2,1)} %constant.27.clone.forward_in.base_in), custom_call_target="tpu_custom_call" | custom-call | tf_op jit(solution)/shard_map/pallas_call | solution.py:425
  2.8 10.2 %all-to-all-start = ((bf16[16,8,128]{2,1,0:T(8,128)(2,1)}), bf16[16,8,128]{2,1,0:T(8,128)(2,1)S(1)}, u32[]{:S(2)}, u32[]{:S(2)}) async-start(bf16[16,8,128]{2,1,0:T(8,128)(2,1)} %shard_map.87), calls=%async_computation | async-start | bytes 65536 | tf_op jit(solution)/shard_map/all_to_all | solution.py:440
  13.0 0.1 pad_add_fusion.where
  13.1 2.5 %shard_map.86 = (s32[8,128]{1,0:T(8,128)S(1)}, bf16[800,128]{1,0:T(8,128)(2,1)S(1)}, bf16[576,32]{1,0:T(8,128)(2,1)S(1)}, bf16[16,512]{1,0:T(8,128)(2,1)S(1)}, b...) custom-call(s32[4]{0:T(128)S(1)} %pad_add_fusion.where, ...), custom_call_target="tpu_custom_call" | custom-call | tf_op jit(solution)/shard_map/pallas_call | solution.py:425
  15.6 4.9 %all-to-all-done.got = bf16[16,8,128]{2,1,0:T(8,128)(2,1)S(1)} async-done(((bf16[16,8,128]{2,1,0:T(8,128)(2,1)}), bf16[16,8,128]{2,1,0:T(8,128)(2,1)S(1)}, u32[]{:S(2)}, u32[]{:S(2)}) %all-to-all-start) | async-done | bytes 32800 | tf_op jit(solution)/shard_map/all_to_all | solution.py:440
  20.5 0.3 shard_map.88
  20.8 20.4 %all_to_all.55.got = bf16[32,24,128]{2,1,0:T(8,128)(2,1)S(1)} all-to-all(bf16[32,24,128]{2,1,0:T(8,128)(2,1)S(1)} %bitcast.15), channel_id=1, replica_groups=mesh['x'=4,'v'=4,'w'=2,'c'=2,'z'=8] {'x','z'}, dimensions={0} | all-to-all | bytes 393216 | tf_op jit(solution)/shard_map/all_to_all | solution.py:440
  41.3 0.7 shard_map.89
  42.0 13.2 %all_to_all.56.got = bf16[16,16,128]{2,1,0:T(8,128)(2,1)S(1)} all-to-all(bf16[16,16,128]{2,1,0:T(8,128)(2,1)S(1)} %bitcast.21), channel_id=1, replica_groups=mesh['x'=4,'v'=4,'w'=2,'c'=2,'z'=8] {'v','w','c'}, dimensions={0} | all-to-all | bytes 131072 | tf_op jit(solution)/shard_map/all_to_all | solution.py:440
  55.2 0.7 shard_map.90
  55.9 8.9 %all_to_all.57.got = bf16[16,16,128]{2,1,0:T(8,128)(2,1)S(1)} all-to-all(bf16[16,16,128]{2,1,0:T(8,128)(2,1)S(1)} %shard_map.90), channel_id=1, replica_groups=mesh['x'=4,'v'=4,'w'=2,'c'=2,'z'=8] {'x','c','w'}, dimensions={0} | all-to-all | bytes 131072 | tf_op jit(solution)/shard_map/all_to_all | solution.py:440
  64.8 0.5 shard_map.91
  65.2 12.4 %all_to_all.58.got = bf16[32,16,128]{2,1,0:T(8,128)(2,1)S(1)} all-to-all(bf16[32,16,128]{2,1,0:T(8,128)(2,1)S(1)} %shard_map.91), channel_id=1, replica_groups=mesh['x'=4,'v'=4,'w'=2,'c'=2,'z'=8] {'x','z'}, dimensions={0} | all-to-all | bytes 262144 | tf_op jit(solution)/shard_map/all_to_all | solution.py:440
  77.7 14.3 %all_to_all.59.got = bf16[16,32,128]{2,1,0:T(8,128)(2,1)S(1)} all-to-all(bf16[16,32,128]{2,1,0:T(8,128)(2,1)S(1)} %bitcast.17), channel_id=1, replica_groups=mesh['x'=4,'v'=4,'w'=2,'c'=2,'z'=8] {'v','w','c'}, dimensions={0} | all-to-all | bytes 262144 | tf_op jit(solution)/shard_map/all_to_all | solution.py:440
  92.0 0.6 shard_map.93
  92.6 13.8 %all_to_all.60.got = bf16[64,8,128]{2,1,0:T(8,128)(2,1)S(1)} all-to-all(bf16[64,8,128]{2,1,0:T(8,128)(2,1)S(1)} %bitcast.19), channel_id=1, replica_groups=mesh['x'=4,'v'=4,'w'=2,'c'=2,'z'=8] {'x','c','z'}, dimensions={0} | all-to-all | bytes 262144 | tf_op jit(solution)/shard_map/all_to_all | solution.py:440
  106.4 0.8 shard_map.94
  107.2 11.8 %all_to_all.61.got = bf16[16,16,128]{2,1,0:T(8,128)(2,1)S(1)} all-to-all(bf16[16,16,128]{2,1,0:T(8,128)(2,1)S(1)} %bitcast.20), channel_id=1, replica_groups=mesh['x'=4,'v'=4,'w'=2,'c'=2,'z'=8] {'v','w','c'}, dimensions={0} | all-to-all | bytes 131072 | tf_op jit(solution)/shard_map/all_to_all | solution.py:440
  119.0 0.7 shard_map.95
  119.7 9.2 %all_to_all.62.got.tail = bf16[16,24,128]{2,1,0:T(8,128)(2,1)S(1)} all-to-all(bf16[16,24,128]{2,1,0:T(8,128)(2,1)S(1)} %shard_map.95), channel_id=1, replica_groups=mesh['x'=4,'v'=4,'w'=2,'c'=2,'z'=8] {'x','c','w'}, dimensions={0} | all-to-all | bytes 196608 | tf_op jit(solution)/shard_map/all_to_all | solution.py:440
  128.9 0.5 shard_map.96
  129.4 12.1 %all_to_all.63 = bf16[32,16,128]{2,1,0:T(8,128)(2,1)S(1)} all-to-all(bf16[32,16,128]{2,1,0:T(8,128)(2,1)S(1)} %bitcast.16), channel_id=1, replica_groups=mesh['x'=4,'v'=4,'w'=2,'c'=2,'z'=8] {'x','z'}, dimensions={0} | all-to-all | bytes 262144 | tf_op jit(solution)/shard_map/all_to_all | solution.py:440
  141.6 0.0 copy-start
  141.6 0.3 shard_map.97
  141.9 12.5 %all_to_all.64.got = bf16[16,4,128]{2,1,0:T(4,128)(2,1)S(1)} all-to-all(bf16[16,4,128]{2,1,0:T(4,128)(2,1)S(1)} %shard_map.97), channel_id=1, replica_groups=mesh['x'=4,'v'=4,'w'=2,'c'=2,'z'=8] {'v','w','c'}, dimensions={0} | all-to-all | bytes 32768 | tf_op jit(solution)/shard_map/all_to_all | solution.py:440
  154.4 0.0 copy-done
  154.4 1.3 shard_map.98
  (1 shorter events, 0.0 us)
Async XLA Ops:
  2.8 17.7 %all-to-all-start = ((bf16[16,8,128]{2,1,0:T(8,128)(2,1)}), bf16[16,8,128]{2,1,0:T(8,128)(2,1)S(1)}, u32[]{:S(2)}, u32[]{:S(2)}) async-start(bf16[16,8,128]{2,1,0:T(8,128)(2,1)} %shard_map.87), calls=%async_computation | async-start | bytes 65536 | tf_op jit(solution)/shard_map/all_to_all | solution.py:440
  141.6 12.8 %copy-start = (bf16[16,4,1024]{2,1,0:T(4,128)(2,1)S(1)}, bf16[16,4,1024]{2,1,0:T(4,128)(2,1)}, u32[]{:S(2)}) copy-start(bf16[16,4,1024]{2,1,0:T(4,128)(2,1)} %focus.1) | copy-start | bytes 393220
